TPU v7x, 32 devices: a whole 2x2x4 slice. The times are simulated.
32 devices in a mesh: wide: 16 (over z, y, x), narrow: 2 (over core).
Axes of the slice: x: 2, y: 2, z: 4, core: 2. Of those that a mesh axis runs over, the one named last changes fastest.
Arguments:
- orbitals: float32 [112, 14, 7, 512], P('wide', 'narrow'), may hold values from -6 to 6
- cell_matrix: bfloat16 [16, 2, 1, 512, 512], P('wide', 'narrow'), as said below
- cell_order: int32 [16, 2, 1, 512], P('wide', 'narrow'), may hold values from 0 to 511, as said below
Outputs:
- filtered_basis: float32 [112, 14, 7, 512], P('wide', 'narrow')
Inputs may be any that keep to these rules, and one draw needn't show every extreme that they name: Each row of cell_order lists the 512 cell node numbers of one cell in the order given by one of the 48 rotations and reflections of the cube. `cell_matrix`: each cell's matrix is symmetric.
All inputs are finite; a program needn't handle non-finite values.
Results may differ from a plain program's by a relative error of at most 0.00045.
The roundings to bfloat16 on the way count: a program that leaves them out, or rounds other values in their place, can miss the bound.
Values sent between devices are 32-bit elements; how exact they have to be, the bound alone decides.
No kernel may reach another device: no remote copies, remote signals or barrier semaphores. Data moves between devices by JAX's collectives and lax.ppermute only.
A program may use at most 64 MiB of HBM per device.

v0:
```python
import jax
import jax.numpy as jnp
from jax import lax
from jax.sharding import PartitionSpec as P

DEG = 4


band_low = 4.0
band_high = 34.0
anchor = 0.0


def extended_2(cells, sides, width):
    for axis, dim in sides:
        count = lax.axis_size(axis)
        head = lax.slice_in_dim(cells, 0, width, axis=dim)
        tail = lax.slice_in_dim(cells, cells.shape[dim] - width, cells.shape[dim], axis=dim)
        cells = jnp.concatenate(
            [
                lax.ppermute(tail, axis, [(i, (i + 1) % count) for i in range(count)]),
                cells,
                lax.ppermute(head, axis, [((i + 1) % count, i) for i in range(count)]),
            ],
            axis=dim,
        )
    return cells


def shifted_2(block, axis, distance):
    devices = range(lax.axis_size(axis))
    route = [((i - distance) % len(devices), i) for i in devices]
    return lax.ppermute(block, axis, route)


def fold_faces(padded, axis_pos):
    inner = lax.slice_in_dim(padded, 1, padded.shape[axis_pos] - 1, axis=axis_pos)
    count = inner.shape[axis_pos]
    first_plane = lax.slice_in_dim(inner, 0, 1, axis=axis_pos) + lax.slice_in_dim(
        padded, 0, 1, axis=axis_pos
    )
    middle = lax.slice_in_dim(inner, 1, count - 1, axis=axis_pos)
    last_plane = lax.slice_in_dim(inner, count - 1, count, axis=axis_pos) + lax.slice_in_dim(
        padded, count + 1, count + 2, axis=axis_pos
    )
    return jnp.concatenate([first_plane, middle, last_plane], axis=axis_pos)


def face_sum(partial_value):
    padded = extended_2(partial_value, (("wide", 0),), 1)
    folded = fold_faces(padded, 0)
    padded = extended_2(folded, (("narrow", 1),), 1)
    return fold_faces(padded, 1)


def final_sum(partial_value, order_now):
    return face_sum(partial_value)[:order_now, :order_now]


def apply_cells(fields, permuted, order_now, cells_here):
    edge = order_now + 1
    z_nodes = fields.shape[2]
    width = fields.shape[3]
    wrapped = jnp.concatenate([fields, fields[:, :, :1]], axis=2)
    inner_part = wrapped[:, :, :z_nodes].reshape(edge, edge, cells_here, order_now, width)
    tail_plane = wrapped[:, :, order_now::order_now][:, :, :, None]
    cell_boxes = jnp.concatenate([inner_part, tail_plane], axis=3).astype(jnp.bfloat16)
    products = jnp.einsum(
        "ckxyz,xyczn->ckn", permuted, cell_boxes, preferred_element_type=jnp.float32
    )
    products = products.reshape(cells_here, edge, edge, edge, width)
    body_part = products[:, :, :, :order_now]
    shifted = jnp.roll(products[:, :, :, order_now], 1, axis=0)
    combined = jnp.concatenate(
        [body_part[:, :, :, :1] + shifted[:, :, :, None], body_part[:, :, :, 1:]], axis=3
    )
    assembled = jnp.transpose(combined, (1, 2, 0, 3, 4))
    return assembled.reshape(edge, edge, z_nodes, width)


def on_device(orbitals, cell_matrix, cell_order):
    order_now = orbitals.shape[0]
    edge = order_now + 1
    width = orbitals.shape[3]
    matrices = cell_matrix[0, 0]
    ordering = cell_order[0, 0]
    cells_here = matrices.shape[0]
    inverse_order = jnp.argsort(ordering, axis=-1)
    permuted = jnp.take_along_axis(matrices, inverse_order[:, :, None], axis=1)
    permuted = jnp.take_along_axis(permuted, inverse_order[:, None, :], axis=2)
    permuted = permuted.reshape(cells_here, edge**3, edge, edge, edge)
    row_next = shifted_2(orbitals[:1], "wide", -1)
    extended = jnp.concatenate([orbitals, row_next], axis=0)
    column_next = shifted_2(extended[:, :1], "narrow", -1)
    current = jnp.concatenate([extended, column_next], axis=1)
    center = (band_low + band_high) / 2.0
    half_width = (band_high - band_low) / 2.0
    sigma_now = half_width / (anchor - center)
    tau_value = 2.0 / sigma_now
    previous = current
    for degree_step in range(DEG):
        final_apply = degree_step == DEG - 1
        image = apply_cells(current, permuted, order_now, cells_here)
        if final_apply:
            image = final_sum(image, order_now)
            current_part = current[:order_now, :order_now]
            previous_part = previous[:order_now, :order_now]
        else:
            image = face_sum(image)
            current_part = current
            previous_part = previous
        if degree_step == 0:
            updated = (image - center * current_part) * (sigma_now / half_width)
        else:
            sigma_new = 1.0 / (tau_value - sigma_now)
            updated = (image - center * current_part) * (
                2.0 * sigma_new / half_width
            ) - sigma_now * sigma_new * previous_part
            sigma_now = sigma_new
        previous, current = (current, updated)
    flattened = current.reshape(-1, width)
    node_total = flattened.shape[0] * lax.axis_size("wide") * lax.axis_size("narrow")
    local_correlation = jnp.einsum(
        "kn,km->nm", flattened, flattened, precision=lax.Precision.HIGHEST
    )
    correlation = lax.psum(local_correlation, ("wide", "narrow")) / node_total
    lower_factor = jnp.linalg.cholesky(correlation)
    identity_matrix = jnp.eye(width, dtype=jnp.float32)
    r_inverse = lax.linalg.triangular_solve(
        lower_factor, identity_matrix, left_side=True, lower=True
    ).T
    result = jnp.dot(flattened, r_inverse, precision=lax.Precision.HIGHEST)
    return result.reshape(current.shape)


def solution(mesh):
    return jax.shard_map(
        on_device,
        mesh=mesh,
        in_specs=(
            P("wide", "narrow", None, None),
            P("wide", "narrow", None, None, None),
            P("wide", "narrow", None, None),
        ),
        out_specs=P("wide", "narrow", None, None),
        check_vma=False,
    )
```

profile of v0, /device:TPU:0, one launch (start us, length us, event | category | flops | bytes accessed | tf_op | source)
XLA Modules:
  0.0 444.6 jit_solution(11412141752535920425)
XLA Ops:
  7.5 6.9 %collective-permute-start = (f32[1,7,7,512]{3,2,1,0:T(8,128)S(1)}, f32[1,7,7,512]{3,2,1,0:T(8,128)S(1)}, u32[]{:S(2)}, u32[]{:S(2)}) collective-permute-start(f32[1,7,7,512]{3,2,1,0:T(8,128)S(1)} %slice.305), channel_id=1, source_target_pairs={{2,0},{4,2},{6,4},{8,6},{10,8},{12,10},{14,12},{16,14},{18,16},{20... | collective-permute-start | bytes 301064 | tf_op jit(solution)/shard_map/ppermute | solution.py:33
  24.4 10.8 %gather.14 = bf16[8,8,8,8,8,8]{2,1,0,5,4,3:T(8,128)(2,1)} reshape(bf16[512,512]{0,1:T(8,128)(2,1)S(1)} %bitcast.148) | data formatting | bytes 1048576 | tf_op jit(solution)/shard_map/jit(take_along_axis)/gather | solution.py:90
  35.2 14.7 %copy.9 = bf16[8,8,8,8,8,8]{5,2,4,3,1,0:T(8,128)(2,1)} copy(bf16[8,8,8,8,8,8]{2,1,0,5,4,3:T(8,128)(2,1)} %gather.14) | data formatting | bytes 1048576 | tf_op jit(solution)/shard_map/jit(take_along_axis)/gather | solution.py:90
  52.8 6.2 %fusion.8 = f32[1,8,8,8,512]{4,3,2,1,0:T(8,128)S(1)} fusion(bf16[8,8,8,8,8,8]{5,2,4,3,1,0:T(8,128)(2,1)} %copy.9, pred[8,8,8]{2,1,0:T(8,128)(4,1)S(1)} %compare_and_fusion, bf16[8,8,1,512]{3,2,1,0:T(2,128)(2,1)S(1)} %slice.378, bf16[8,8,7,512]{3,2,1,0:T(8,128)(2,1)S(1)} %fusion.48), kind=kOutput, calls=%fused_computation.15 | convolution fusion | flops 269746176 | bytes 2097664 | tf_op jit(solution)/shard_map/ckxyz,xyczn->ckn/dot_general | solution.py:68
  59.5 9.2 %collective-permute-done.2 = f32[1,8,7,512]{3,2,1,0:T(8,128)S(1)} collective-permute-done((f32[1,8,7,512]{3,2,1,0:T(8,128)S(1)}, f32[1,8,7,512]{3,2,1,0:T(8,128)S(1)}, u32[]{:S(2)}, u32[]{:S(2)}) %collective-permute-start.2) | collective-permute-done | bytes 114720 | tf_op jit(solution)/shard_map/ppermute | solution.py:21
  69.0 4.8 %collective-permute-done.3 = f32[1,8,7,512]{3,2,1,0:T(8,128)S(1)} collective-permute-done((f32[1,8,7,512]{3,2,1,0:T(8,128)S(1)}, f32[1,8,7,512]{3,2,1,0:T(8,128)S(1)}, u32[]{:S(2)}, u32[]{:S(2)}) %collective-permute-start.3) | collective-permute-done | bytes 114720 | tf_op jit(solution)/shard_map/ppermute | solution.py:23
  80.3 9.2 %collective-permute-done.6 = f32[1,8,7,512]{3,2,1,0:T(8,128)S(1)} collective-permute-done((f32[1,8,7,512]{3,2,1,0:T(8,128)S(1)}, f32[1,8,7,512]{3,2,1,0:T(8,128)S(1)}, u32[]{:S(2)}, u32[]{:S(2)}) %collective-permute-start.6) | collective-permute-done | bytes 114720 | tf_op jit(solution)/shard_map/ppermute | solution.py:21
  90.3 4.8 %collective-permute-done.7 = f32[1,8,7,512]{3,2,1,0:T(8,128)S(1)} collective-permute-done((f32[1,8,7,512]{3,2,1,0:T(8,128)S(1)}, f32[1,8,7,512]{3,2,1,0:T(8,128)S(1)}, u32[]{:S(2)}, u32[]{:S(2)}) %collective-permute-start.7) | collective-permute-done | bytes 114720 | tf_op jit(solution)/shard_map/ppermute | solution.py:23
  101.7 9.2 %collective-permute-done.10 = f32[1,8,7,512]{3,2,1,0:T(8,128)S(1)} collective-permute-done((f32[1,8,7,512]{3,2,1,0:T(8,128)S(1)}, f32[1,8,7,512]{3,2,1,0:T(8,128)S(1)}, u32[]{:S(2)}, u32[]{:S(2)}) %collective-permute-start.10) | collective-permute-done | bytes 114720 | tf_op jit(solution)/shard_map/ppermute | solution.py:21
  111.2 4.8 %collective-permute-done.11 = f32[1,8,7,512]{3,2,1,0:T(8,128)S(1)} collective-permute-done((f32[1,8,7,512]{3,2,1,0:T(8,128)S(1)}, f32[1,8,7,512]{3,2,1,0:T(8,128)S(1)}, u32[]{:S(2)}, u32[]{:S(2)}) %collective-permute-start.11) | collective-permute-done | bytes 114720 | tf_op jit(solution)/shard_map/ppermute | solution.py:23
  122.5 9.2 %collective-permute-done.14 = f32[1,8,7,512]{3,2,1,0:T(8,128)S(1)} collective-permute-done((f32[1,8,7,512]{3,2,1,0:T(8,128)S(1)}, f32[1,8,7,512]{3,2,1,0:T(8,128)S(1)}, u32[]{:S(2)}, u32[]{:S(2)}) %collective-permute-start.14) | collective-permute-done | bytes 114720 | tf_op jit(solution)/shard_map/ppermute | solution.py:21
  132.2 4.8 %collective-permute-done.15 = f32[1,8,7,512]{3,2,1,0:T(8,128)S(1)} collective-permute-done((f32[1,8,7,512]{3,2,1,0:T(8,128)S(1)}, f32[1,8,7,512]{3,2,1,0:T(8,128)S(1)}, u32[]{:S(2)}, u32[]{:S(2)}) %collective-permute-start.15) | collective-permute-done | bytes 114720 | tf_op jit(solution)/shard_map/ppermute | solution.py:23
  138.8 2.9 convolution_bitcast_fusion
  144.2 126.9 %all-reduce.3.cloned.1.call-done = f32[512,512]{0,1:T(8,128)} async-done(((f32[512,512]{0,1:T(8,128)}), f32[512,512]{0,1:T(8,128)}) %all-reduce.3.cloned.1.call-update) | async-done | bytes 1048592 | tf_op jit(solution)/shard_map/psum | solution.py:126
  275.4 11.7 %cholesky.104 = f32[128,128]{1,0:T(8,128)S(1)} custom-call(f32[128,128]{1,0:T(8,128)S(1)} %cholesky.266), custom_call_target="Cholesky" | custom-call | tf_op jit(solution)/shard_map/jit(cholesky)/cholesky | solution.py:127
  287.8 9.8 %custom-call.30 = f32[1,128,128]{1,2,0:T(8,128)S(1)} custom-call(f32[1,128,128]{2,1,0:T(8,128)S(1)} %get-tuple-element.54), custom_call_target="InvertDiagBlocksLowerTriangular" | custom-call | tf_op jit(solution)/shard_map/jit(cholesky)/cholesky | solution.py:127
  300.8 11.9 %cholesky.217 = f32[128,128]{1,0:T(8,128)S(1)} custom-call(f32[128,128]{1,0:T(8,128)S(1)} %cholesky.270), custom_call_target="Cholesky" | custom-call | tf_op jit(solution)/shard_map/jit(cholesky)/cholesky | solution.py:127
  313.3 9.8 %custom-call.31 = f32[1,128,128]{1,2,0:T(8,128)S(1)} custom-call(f32[1,128,128]{2,1,0:T(8,128)S(1)} %get-tuple-element.51), custom_call_target="InvertDiagBlocksLowerTriangular" | custom-call | tf_op jit(solution)/shard_map/jit(cholesky)/cholesky | solution.py:127
  326.2 13.2 %cholesky.238 = f32[128,128]{1,0:T(8,128)} custom-call(f32[128,128]{1,0:T(8,128)} %cholesky.275), custom_call_target="Cholesky" | custom-call | tf_op jit(solution)/shard_map/jit(cholesky)/cholesky | solution.py:127
  341.5 11.3 %custom-call.32 = f32[1,128,128]{1,2,0:T(8,128)} custom-call(f32[1,128,128]{2,1,0:T(8,128)} %get-tuple-element.48), custom_call_target="InvertDiagBlocksLowerTriangular" | custom-call | tf_op jit(solution)/shard_map/jit(cholesky)/cholesky | solution.py:127
  355.1 12.0 %cholesky.255 = f32[128,128]{1,0:T(8,128)S(1)} custom-call(f32[128,128]{1,0:T(8,128)S(1)} %convolution_subtract_fusion.5), custom_call_target="Cholesky" | custom-call | tf_op jit(solution)/shard_map/jit(cholesky)/cholesky | solution.py:127
  373.4 14.1 %while.1 = (s32[]{:T(128)}, f32[512,512]{1,0:T(8,128)}, s32[4,2]{0,1:T(2,128)S(1)}, f32[4,128,128]{2,1,0:T(8,128)}, s32[]{:T(128)}) while((s32[]{:T(128)}, f32[512,512]{1,0:T(8,128)}, s32[4,2]{0,1:T(2,128)S(1)}, f32[4,128,128]{2,1,0:T(8,128)}, s32[]{:T(128)}) %tuple.37), condition=%wide.while_cond, body=%wide.while_body.sunk | while | flops 2 | bytes 132705 | solution.py:129
  387.5 40.1 %custom-call.33 = f32[4,128,128]{1,2,0:T(8,128)S(1)} custom-call(f32[4,128,128]{2,1,0:T(8,128)} %get-tuple-element.14), custom_call_target="InvertDiagBlocksLowerTriangular" | custom-call | tf_op jit(solution)/shard_map/triangular_solve | solution.py:129
  434.1 3.3 fusion.25
  (153 shorter events, 80.0 us)
Async XLA Ops:
  6.5 13.5 %copy-start = (bf16[1,1,1,512,512]{4,3,2,1,0:T(8,128)(2,1)S(1)}, bf16[1,1,1,512,512]{4,3,2,1,0:T(8,128)(2,1)}, u32[]{:S(2)}) copy-start(bf16[1,1,1,512,512]{4,3,2,1,0:T(8,128)(2,1)} %param.4) | copy-start | bytes 1572868
  6.5 12.2 %sort.19.cloned.1.call-start = ((), (), s32[]{:S(2)}) async-start(), calls=%async_computation.1 | async-start | bytes 12320 | tf_op jit(solution)/shard_map/jit(argsort)/sort | solution.py:88
  7.5 43.6 %collective-permute-start = (f32[1,7,7,512]{3,2,1,0:T(8,128)S(1)}, f32[1,7,7,512]{3,2,1,0:T(8,128)S(1)}, u32[]{:S(2)}, u32[]{:S(2)}) collective-permute-start(f32[1,7,7,512]{3,2,1,0:T(8,128)S(1)} %slice.305), channel_id=1, source_target_pairs={{2,0},{4,2},{6,4},{8,6},{10,8},{12,10},{14,12},{16,14},{18,16},{20... | collective-permute-start | bytes 301064 | tf_op jit(solution)/shard_map/ppermute | solution.py:33
  15.0 256.1 %all-reduce.3.cloned.1.call-start = ((), (), s32[]{:S(2)}) async-start(), calls=%async_computation | async-start | bytes 2097152 | tf_op jit(solution)/shard_map/psum | solution.py:126
  35.2 15.2 %copy-start.4 = (s32[1,512]{1,0:T(1,128)S(1)}, s32[1,512]{1,0:T(1,128)}, u32[]{:S(2)}) copy-start(s32[1,512]{1,0:T(1,128)} %get-tuple-element.6) | copy-start | bytes 6148
  51.2 1.4 collective-permute-start.1
  52.7 24.4 %slice-start = ((s8[8388608]{0:T(1024)(128)(4,1)}), s8[4194304]{0:T(1024)(128)(4,1)S(1)}, s32[]{:S(2)}) async-start(s8[8388608]{0:T(1024)(128)(4,1)} %bitcast.146), calls=%async_computation.3 | async-start | bytes 8388608
  52.8 24.3 %slice-start.1 = ((s8[8388608]{0:T(1024)(128)(4,1)}), s8[4194304]{0:T(1024)(128)(4,1)S(1)}, s32[]{:S(2)}) async-start(s8[8388608]{0:T(1024)(128)(4,1)} %bitcast.146), calls=%async_computation.4 | async-start | bytes 8388608
  59.4 9.3 %collective-permute-start.2 = (f32[1,8,7,512]{3,2,1,0:T(8,128)S(1)}, f32[1,8,7,512]{3,2,1,0:T(8,128)S(1)}, u32[]{:S(2)}, u32[]{:S(2)}) collective-permute-start(f32[1,8,7,512]{3,2,1,0:T(8,128)S(1)} %maximum_bitcast_fusion.16), channel_id=1, source_target_pairs={{0,2},{2,4},{4,6},{6,8},{8,10},{10,12},{12,14},{14,16},{16,18},{18... | collective-permute-start | bytes 344072 | tf_op jit(solution)/shard_map/ppermute | solution.py:21
  68.8 5.0 %collective-permute-start.3 = (f32[1,8,7,512]{3,2,1,0:T(8,128)S(1)}, f32[1,8,7,512]{3,2,1,0:T(8,128)S(1)}, u32[]{:S(2)}, u32[]{:S(2)}) collective-permute-start(f32[1,8,7,512]{3,2,1,0:T(8,128)S(1)} %get-tuple-element.42), channel_id=1, source_target_pairs={{2,0},{4,2},{6,4},{8,6},{10,8},{12,10},{14,12},{16,14},{18,16},{20... | collective-permute-start | bytes 344072 | tf_op jit(solution)/shard_map/ppermute | solution.py:23
  73.8 1.4 collective-permute-start.4
  75.3 1.4 collective-permute-start.5
  80.2 9.3 %collective-permute-start.6 = (f32[1,8,7,512]{3,2,1,0:T(8,128)S(1)}, f32[1,8,7,512]{3,2,1,0:T(8,128)S(1)}, u32[]{:S(2)}, u32[]{:S(2)}) collective-permute-start(f32[1,8,7,512]{3,2,1,0:T(8,128)S(1)} %maximum_bitcast_fusion.14), channel_id=1, source_target_pairs={{0,2},{2,4},{4,6},{6,8},{8,10},{10,12},{12,14},{14,16},{16,18},{18... | collective-permute-start | bytes 344072 | tf_op jit(solution)/shard_map/ppermute | solution.py:21
  89.6 5.5 %collective-permute-start.7 = (f32[1,8,7,512]{3,2,1,0:T(8,128)S(1)}, f32[1,8,7,512]{3,2,1,0:T(8,128)S(1)}, u32[]{:S(2)}, u32[]{:S(2)}) collective-permute-start(f32[1,8,7,512]{3,2,1,0:T(8,128)S(1)} %get-tuple-element.36), channel_id=1, source_target_pairs={{2,0},{4,2},{6,4},{8,6},{10,8},{12,10},{14,12},{16,14},{18,16},{20... | collective-permute-start | bytes 344072 | tf_op jit(solution)/shard_map/ppermute | solution.py:23
  95.1 1.4 collective-permute-start.8
  96.6 1.4 collective-permute-start.9
  101.6 9.3 %collective-permute-start.10 = (f32[1,8,7,512]{3,2,1,0:T(8,128)S(1)}, f32[1,8,7,512]{3,2,1,0:T(8,128)S(1)}, u32[]{:S(2)}, u32[]{:S(2)}) collective-permute-start(f32[1,8,7,512]{3,2,1,0:T(8,128)S(1)} %maximum_bitcast_fusion.12), channel_id=1, source_target_pairs={{0,2},{2,4},{4,6},{6,8},{8,10},{10,12},{12,14},{14,16},{16,18},{18... | collective-permute-start | bytes 344072 | tf_op jit(solution)/shard_map/ppermute | solution.py:21
  110.9 5.0 %collective-permute-start.11 = (f32[1,8,7,512]{3,2,1,0:T(8,128)S(1)}, f32[1,8,7,512]{3,2,1,0:T(8,128)S(1)}, u32[]{:S(2)}, u32[]{:S(2)}) collective-permute-start(f32[1,8,7,512]{3,2,1,0:T(8,128)S(1)} %get-tuple-element.30), channel_id=1, source_target_pairs={{2,0},{4,2},{6,4},{8,6},{10,8},{12,10},{14,12},{16,14},{18,16},{20... | collective-permute-start | bytes 344072 | tf_op jit(solution)/shard_map/ppermute | solution.py:23
  116.0 1.4 collective-permute-start.12
  117.5 1.4 collective-permute-start.13
  122.5 9.3 %collective-permute-start.14 = (f32[1,8,7,512]{3,2,1,0:T(8,128)S(1)}, f32[1,8,7,512]{3,2,1,0:T(8,128)S(1)}, u32[]{:S(2)}, u32[]{:S(2)}) collective-permute-start(f32[1,8,7,512]{3,2,1,0:T(8,128)S(1)} %maximum_bitcast_fusion.10), channel_id=1, source_target_pairs={{0,2},{2,4},{4,6},{6,8},{8,10},{10,12},{12,14},{14,16},{16,18},{18... | collective-permute-start | bytes 344072 | tf_op jit(solution)/shard_map/ppermute | solution.py:21
  131.8 5.2 %collective-permute-start.15 = (f32[1,8,7,512]{3,2,1,0:T(8,128)S(1)}, f32[1,8,7,512]{3,2,1,0:T(8,128)S(1)}, u32[]{:S(2)}, u32[]{:S(2)}) collective-permute-start(f32[1,8,7,512]{3,2,1,0:T(8,128)S(1)} %get-tuple-element.24), channel_id=1, source_target_pairs={{2,0},{4,2},{6,4},{8,6},{10,8},{12,10},{14,12},{16,14},{18,16},{20... | collective-permute-start | bytes 344072 | tf_op jit(solution)/shard_map/ppermute | solution.py:23
  137.0 1.4 collective-permute-start.16
  272.8 155.9 %copy-start.1 = (f32[512,512]{1,0:T(8,128)S(1)}, f32[512,512]{1,0:T(8,128)}, u32[]{:S(2)}) copy-start(f32[512,512]{1,0:T(8,128)} %fusion.61) | copy-start | bytes 3145732
  (2 other events, 1.7 us)
Sparse Core Ops, SparseCore 0:
  15.2 3.2 sort.21.cloned.1.call-done
  141.9 129.2 all-reduce.2
  (1 shorter events, 0.0 us)
where the time goes:
time: 453 us; the launch traced here: 445 us
  waiting for transfers between devices  193 us (43%)
  other arithmetic  137 us (30%)
  local copies, waits for them, and re-layouts  53.8 us (12%)
  matrix products  34.3 us (8%)
  between operations  17.1 us (4%)
  starting transfers between devices  9.08 us (2%)
    psum x1, waiting for transfers between devices, on_device(): correlation = lax.psum(local_correlation, ('wide', 'narrow')) / node_total  127 us
    another operation x14, other arithmetic, on_device(): lower_factor = jnp.linalg.cholesky(correlation)  85 us
    ppermute x8, waiting for transfers between devices, extended_2(): lax.ppermute(tail, axis, [(i, (i + 1) % count) for i in range(count)])  42.3 us
    another operation x3, other arithmetic, on_device(): lax.linalg.triangular_solve(lower_factor, identity_matrix, left_side=True...  41.8 us
    gather x3, local copies, waits for them, and re-layouts, on_device(): permuted = jnp.take_along_axis(permuted, inverse_order[:, None, :], axis=2)  27.5 us
    ppermute x7, waiting for transfers between devices, extended_2(): lax.ppermute(head, axis, [((i + 1) % count, i) for i in range(count)])  22.7 us
    dot_general x4, matrix products, apply_cells(): jnp.einsum('ckxyz,xyczn->ckn', permuted, cell_boxes, preferred_element_ty...  14.5 us
    another operation x12, local copies, waits for them, and re-layouts  14.1 us
  transfers between devices with their start and end apart: 18, of which 17 were waited for; matrix products, arithmetic and copies ran while one was open for 8% of the time, Pallas kernels for 0%

commit v1 on v0

v1 whole, which is shorter than its diff:
```python
import functools

import jax
import jax.numpy as jnp
from jax import lax
from jax.experimental import pallas as pl
from jax.experimental.pallas import tpu as pltpu
from jax.sharding import PartitionSpec as P

DEG = 4
SUB = 8
LANES = 128


band_low = 4.0
band_high = 34.0
anchor = 0.0


def vmem_call(body, out_shapes, scratch=(), flops=0):
    def call(*operands):
        return pl.pallas_call(
            body,
            out_shape=out_shapes,
            in_specs=[pl.BlockSpec(memory_space=pltpu.VMEM)] * len(operands),
            out_specs=jax.tree.map(
                lambda _: pl.BlockSpec(memory_space=pltpu.VMEM), out_shapes
            ),
            scratch_shapes=list(scratch),
            compiler_params=pltpu.CompilerParams(vmem_limit_bytes=32 << 20),
            cost_estimate=pl.CostEstimate(
                flops=flops, bytes_accessed=1 << 20, transcendentals=0
            ),
        )(*operands)

    return call


def f32(*shape):
    return jax.ShapeDtypeStruct(shape, jnp.float32)


def exact_dot(a, b, dims=((1,), (0,))):
    return lax.dot_general(
        a,
        b,
        (dims, ((), ())),
        precision=lax.Precision.HIGHEST,
        preferred_element_type=jnp.float32,
    )


def permute_body(matrix, order, out):
    count = matrix.shape[0]
    pick = (
        lax.broadcasted_iota(jnp.int32, (count, count), 1) == order[...]
    ).astype(jnp.bfloat16)
    half = lax.dot_general(
        matrix[...],
        pick,
        (((1,), (0,)), ((), ())),
        preferred_element_type=jnp.float32,
    ).astype(jnp.bfloat16)
    out[...] = lax.dot_general(
        half, pick, (((0,), (0,)), ((), ())), preferred_element_type=jnp.float32
    ).astype(jnp.bfloat16)


def cell_product(values, matrix, image, faces):
    edge = values.shape[0]
    width = values.shape[3]
    rows = values.reshape(edge**3, width).astype(jnp.bfloat16)
    products = jnp.dot(matrix[...], rows, preferred_element_type=jnp.float32)
    products = products.reshape(edge, edge, edge, width)
    wrap = products[:, :, :1] + products[:, :, edge - 1 :]
    where = lax.broadcasted_iota(jnp.int32, products.shape, 2)
    products = jnp.where((where == 0) | (where == edge - 1), wrap, products)
    image[...] = products
    faces[0] = products[:, 0]
    faces[1] = products[:, edge - 1]


def first_body(own, x_next, y_next, matrix, values, image, faces):
    order_now = own.shape[0]
    values[:order_now, :order_now, :order_now] = own[...]
    values[order_now:, :order_now, :order_now] = x_next[...]
    values[:, order_now:, :order_now] = y_next[...]
    values[:, :, order_now:] = values[:, :, :1]
    cell_product(values[...], matrix, image, faces)


def updated(image, y_faces, x_low, x_high, current, previous, alpha, beta):
    center = (band_low + band_high) / 2.0
    edge = image.shape[0]
    image[:, 0] = image[:, 0] + y_faces[0]
    if y_faces.shape[0] > 1:
        image[:, edge - 1] = image[:, edge - 1] + y_faces[1]
    image[0] = image[0] + x_low[...]
    if x_high is not None:
        image[edge - 1] = image[edge - 1] + x_high[...]
    got = (image[...] - center * current[...]) * alpha
    if previous is not None:
        got = got - beta * previous[...]
    return got


def middle_body(*refs, alpha, beta):
    if beta is None:
        image_in, y_faces, x_low, x_high, current, matrix, values, image, faces, work = refs
        previous = None
    else:
        image_in, y_faces, x_low, x_high, current, previous, matrix, values, image, faces, work = refs
    work[...] = image_in[...]
    got = updated(work, y_faces, x_low, x_high, current, previous, alpha, beta)
    values[...] = got
    cell_product(got, matrix, image, faces)


def last_body(image_in, y_face, x_low, current, previous, own, corr, work, *, alpha, beta):
    edge = image_in.shape[0]
    width = image_in.shape[3]
    work[...] = image_in[...]
    got = updated(work, y_face, x_low, None, current, previous, alpha, beta)
    got = got[: edge - 1, : edge - 1]
    where = lax.broadcasted_iota(jnp.int32, got.shape, 2)
    got = jnp.where(where == edge - 1, 0.0, got)
    flat = got.reshape((edge - 1) ** 2 * edge, width)
    own[...] = flat
    at = 0
    for j in range(0, width, LANES):
        block = exact_dot(flat[:, j:], flat[:, j : j + LANES], ((0,), (0,)))
        corr[at : at + width - j] = block
        at += width - j


def swap(block, axis, distance):
    count = lax.axis_size(axis)
    return lax.ppermute(block, axis, [(i, i ^ distance) for i in range(count)])


def stages_of(axis, size):
    stages, stride = [], 1
    while stride < size:
        radix = 4 if size // stride >= 4 else 2
        stages.append((axis, stride, radix))
        stride *= radix
    return stages


def summed(block):
    rows, lanes = block.shape
    stages = stages_of("narrow", lax.axis_size("narrow")) + stages_of(
        "wide", lax.axis_size("wide")
    )
    cut = 1
    for _, _, radix in stages[:-1]:
        cut *= radix
    padded = -(-rows // (cut * SUB)) * cut * SUB
    if padded != rows:
        block = jnp.pad(block, ((0, padded - rows), (0, 0)))
    for axis, stride, radix in stages[:-1]:
        mine = lax.axis_index(axis) // stride % radix
        parts = block.reshape(radix, -1, lanes)
        total = lax.dynamic_index_in_dim(parts, mine, 0, False)
        for d in range(1, radix):
            sent = lax.dynamic_index_in_dim(parts, mine ^ d, 0, False)
            total = total + swap(sent, axis, d * stride)
        block = total
    axis, stride, radix = stages[-1]
    got = [block] + [swap(block, axis, d * stride) for d in range(1, radix)]
    while len(got) > 1:
        got = [a + b for a, b in zip(got[::2], got[1::2])]
    block = got[0]
    for axis, stride, radix in reversed(stages[:-1]):
        mine = lax.axis_index(axis) // stride % radix
        parts = jnp.zeros((radix,) + block.shape, block.dtype)
        parts = lax.dynamic_update_index_in_dim(parts, block, mine, 0)
        for d in range(1, radix):
            parts = lax.dynamic_update_index_in_dim(
                parts, swap(block, axis, d * stride), mine ^ d, 0
            )
        block = parts.reshape(-1, lanes)
    return block[:rows]


def lane_spread(tile, column):
    return jnp.broadcast_to(tile[:, column : column + 1], tile.shape)


def row_spread(tile, row):
    return jnp.broadcast_to(tile[row : row + 1, :], tile.shape)


def inverse_factor(block):
    size = block.shape[0]
    steps = size // SUB
    left = [block[SUB * t : SUB * (t + 1)] for t in range(steps)]
    rows = lax.broadcasted_iota(jnp.int32, (SUB, size), 0)
    cols = lax.broadcasted_iota(jnp.int32, (SUB, size), 1)
    right = [
        jnp.where(cols == rows + SUB * t, 1.0, 0.0).astype(jnp.float32)
        for t in range(steps)
    ]
    done = []
    for s in range(steps):
        base = SUB * s
        spread = [lane_spread(left[s], base + d) for d in range(SUB)]
        a = {
            (c, d): row_spread(spread[d], c)
            for d in range(SUB)
            for c in range(d, SUB)
        }
        scale, low = [], {}
        for k in range(SUB):
            scale.append(lax.rsqrt(a[k, k]))
            for c in range(k + 1, SUB):
                low[c, k] = a[c, k] * scale[k]
            for d in range(k + 1, SUB):
                for c in range(d, SUB):
                    a[c, d] = a[c, d] - low[c, k] * low[d, k]

        def forward(tile):
            got = []
            for k in range(SUB):
                row = row_spread(tile, k)
                for m in range(k):
                    row = row - low[k, m] * got[m]
                got.append(row * scale[k])
            return got

        def backward(got):
            back = [None] * SUB
            for k in reversed(range(SUB)):
                row = got[k]
                for m in range(k + 1, SUB):
                    row = row - low[m, k] * back[m]
                back[k] = row * scale[k]
            return back

        inverse = forward(right[s])
        packed = inverse[0]
        for k in range(1, SUB):
            packed = jnp.where(rows == k, inverse[k], packed)
        done.append(packed)
        if s + 1 == steps:
            break
        upper = forward(left[s])
        t = s + 1
        factors = []
        for k in range(SUB):
            column = lane_spread(left[t], base + k)
            for m in range(k):
                column = column - factors[m] * low[k, m]
            factors.append(column * scale[k])
        for k in range(SUB):
            left[t] = left[t] - factors[k] * upper[k]
            right[t] = right[t] - factors[k] * inverse[k]
        if s + 2 < steps:
            upper, inverse = backward(upper), backward(inverse)
        for t in range(s + 2, steps):
            raw = [lane_spread(left[t], base + k) for k in range(SUB)]
            for k in range(SUB):
                left[t] = left[t] - raw[k] * upper[k]
                right[t] = right[t] - raw[k] * inverse[k]
    return jnp.concatenate(done, axis=0)


def ortho_body(corr, own, out, lower, rest, *, scale):
    width = own.shape[1]
    count = width // LANES
    at = 0
    for j in range(0, width, LANES):
        lower[j:, j : j + LANES] = corr[at : at + width - j] * scale
        at += width - j
    rest[...] = own[...]
    for k in range(count):
        begin, end = LANES * k, LANES * (k + 1)
        inverse = inverse_factor(lower[begin:end, begin:end])
        block = exact_dot(rest[:, begin:end], inverse, ((1,), (1,)))
        out[:, :, begin:end] = block.reshape(out.shape[0], SUB, LANES)[:, : SUB - 1]
        if k + 1 < count:
            under = exact_dot(lower[end:, begin:end], inverse, ((1,), (1,)))
            lower[end:, end:] = lower[end:, end:] - exact_dot(
                under, under, ((1,), (1,))
            )
            rest[:, end:] = rest[:, end:] - exact_dot(block, under, ((1,), (1,)))


def to_next(block, axis, distance):
    count = lax.axis_size(axis)
    return lax.ppermute(block, axis, [(i, (i + distance) % count) for i in range(count)])


def y_exchange(faces):
    if lax.axis_size("narrow") == 2:
        return to_next(faces[::-1], "narrow", 1)
    return jnp.stack([to_next(faces[1], "narrow", 1), to_next(faces[0], "narrow", -1)])


def with_faces(plane, y_faces, x_at):
    low = plane[:1] + y_faces[0, x_at][None]
    high = plane[-1:] + y_faces[1, x_at][None]
    return jnp.concatenate([low, plane[1:-1], high], axis=0)


def on_device(orbitals, cell_matrix, cell_order):
    order_now = orbitals.shape[0]
    edge = order_now + 1
    width = orbitals.shape[3]
    box = f32(edge, edge, edge, width)
    faces_shape = f32(2, edge, edge, width)
    cell_nodes = edge**3
    matrix = vmem_call(
        permute_body,
        jax.ShapeDtypeStruct((cell_nodes, cell_nodes), jnp.bfloat16),
        flops=4 * cell_nodes**3,
    )(
        cell_matrix.reshape(cell_nodes, cell_nodes),
        cell_order.reshape(cell_nodes, 1),
    )

    x_next = to_next(orbitals[:1], "wide", -1)
    first_rows = jnp.concatenate([orbitals[:, :1], x_next[:, :1]], axis=0)
    y_next = to_next(first_rows, "narrow", -1)
    product_flops = 2 * cell_nodes**2 * width
    current, image, faces = vmem_call(
        first_body, (box, box, faces_shape), flops=product_flops
    )(orbitals, x_next, y_next, matrix)

    half_width = (band_high - band_low) / 2.0
    sigma_now = half_width / (anchor - (band_low + band_high) / 2.0)
    tau_value = 2.0 / sigma_now
    alpha, beta, previous = sigma_now / half_width, None, None
    for degree_step in range(1, DEG):
        y_faces = y_exchange(faces)
        x_low = to_next(with_faces(image[edge - 1], y_faces, edge - 1), "wide", 1)
        x_high = to_next(with_faces(image[0], y_faces, 0), "wide", -1)
        operands = [image, y_faces, x_low, x_high, current]
        if previous is not None:
            operands.append(previous)
        next_values, image, faces = vmem_call(
            functools.partial(middle_body, alpha=alpha, beta=beta),
            (box, box, faces_shape),
            scratch=[pltpu.VMEM(box.shape, jnp.float32)],
            flops=product_flops,
        )(*operands, matrix)
        previous, current = current, next_values
        sigma_new = 1.0 / (tau_value - sigma_now)
        alpha, beta = 2.0 * sigma_new / half_width, sigma_now * sigma_new
        sigma_now = sigma_new

    y_low = to_next(faces[1:], "narrow", 1)
    last_plane = image[edge - 1]
    last_plane = jnp.concatenate(
        [last_plane[:1] + y_low[0, edge - 1][None], last_plane[1:]], axis=0
    )
    x_low = to_next(last_plane, "wide", 1)
    blocks = width // LANES
    own, corr = vmem_call(
        functools.partial(last_body, alpha=alpha, beta=beta),
        (
            f32(order_now**2 * edge, width),
            f32(blocks * (blocks + 1) // 2 * LANES, LANES),
        ),
        scratch=[pltpu.VMEM(box.shape, jnp.float32)],
        flops=2 * cell_nodes * width**2,
    )(image, y_low, x_low, current, previous)

    nodes = order_now**3 * lax.axis_size("wide") * lax.axis_size("narrow")
    corr = summed(corr)
    out = vmem_call(
        functools.partial(ortho_body, scale=1.0 / nodes),
        f32(order_now**2, order_now, width),
        scratch=[
            pltpu.VMEM((width, width), jnp.float32),
            pltpu.VMEM(own.shape, jnp.float32),
        ],
        flops=width**3,
    )(corr, own)
    return out.reshape(orbitals.shape)


def solution(mesh):
    return jax.shard_map(
        on_device,
        mesh=mesh,
        in_specs=(
            P("wide", "narrow", None, None),
            P("wide", "narrow", None, None, None),
            P("wide", "narrow", None, None),
        ),
        out_specs=P("wide", "narrow", None, None),
        check_vma=False,
    )
```

time: 453 us -> 127 us (0.28); the launches traced: 445 us -> 126 us
  waiting for transfers between devices: 193 us -> 52.6 us
  other arithmetic: 137 us -> 1.74 us
  local copies, waits for them, and re-layouts: 53.8 us -> 13.3 us
  matrix products: 34.3 us -> 0 us
  Pallas kernels: 0 us -> 27.7 us
  starting transfers between devices: 9.08 us -> 30.6 us
  between operations: 17.1 us -> 0.45 us
    another operation x21 -> x0, other arithmetic: 128 us -> none  [the longest x14 85 us: on_device(): lower_factor = jnp.linalg.cholesky(correlation)]
    psum x1 -> x0, waiting for transfers between devices: 127 us -> none  [on_device(): correlation = lax.psum(local_correlation, ('wide', 'narrow')) / node_total]
    gather x4 -> x0, local copies, waits for them, and re-layouts: 29.4 us -> none  [the longest x3 27.5 us: on_device(): permuted = jnp.take_along_axis(permuted, inverse_order[:, None, :], axis=2)]
    pallas_call x0 -> x7, Pallas kernels: none -> 27.7 us  [call(): pl.pallas_call(body, out_shape=out_shapes, in_specs=[pl.BlockSpec(memory_...]
    ppermute x17 -> x24, starting transfers between devices: 9.04 us -> 30.6 us  [the longest x13 18.5 us: to_next(): lax.ppermute(block, axis, [(i, (i + distance) % count) for i in range(cou...]
    dot_general x6 -> x0, matrix products: 20.7 us -> none  [the longest x4 14.5 us: apply_cells(): jnp.einsum('ckxyz,xyczn->ckn', permuted, cell_boxes, preferred_element_ty...]
    another operation x17 -> x0, local copies, waits for them, and re-layouts: 15.5 us -> none
    ppermute x17 -> x24, waiting for transfers between devices: 66.3 us -> 52.6 us  [the longest x13 38.5 us: to_next(): lax.ppermute(block, axis, [(i, (i + distance) % count) for i in range(cou...]
  transfers between devices with their start and end apart: 18 -> 24, of which waited for: 17 -> 22; matrix products, arithmetic and copies ran while one was open for 8% -> 2% of each run, Pallas kernels for 0% -> 1%
where the time goes in v1:
time: 127 us; the launch traced here: 126 us
  waiting for transfers between devices  52.6 us (41%)
  starting transfers between devices  30.6 us (24%)
  Pallas kernels  27.7 us (22%)
  local copies, waits for them, and re-layouts  13.3 us (10%)
  other arithmetic  1.74 us (1%)
    ppermute x13, waiting for transfers between devices, to_next(): lax.ppermute(block, axis, [(i, (i + distance) % count) for i in range(cou...  38.5 us
    pallas_call x7, Pallas kernels, call(): pl.pallas_call(body, out_shape=out_shapes, in_specs=[pl.BlockSpec(memory_...  27.7 us
    ppermute x13, starting transfers between devices, to_next(): lax.ppermute(block, axis, [(i, (i + distance) % count) for i in range(cou...  18.5 us
    ppermute x11, waiting for transfers between devices, swap(): return lax.ppermute(block, axis, [(i, i ^ distance) for i in range(count)])  14.1 us
    ppermute x11, starting transfers between devices, swap(): return lax.ppermute(block, axis, [(i, i ^ distance) for i in range(count)])  12.1 us
    unnamed x28, local copies, waits for them, and re-layouts  9.86 us
  transfers between devices with their start and end apart: 24, of which 22 were waited for; matrix products, arithmetic and copies ran while one was open for 2% of the time, Pallas kernels for 1%

profile of v1, /device:TPU:0, one launch (start us, length us, event | category | flops | bytes accessed | tf_op | source)
XLA Modules:
  0.0 126.5 jit_solution(6064215827601578821)
XLA Ops:
  0.9 7.0 %collective-permute-start = (f32[1,7,7,512]{3,2,1,0:T(8,128)S(1)}, f32[1,7,7,512]{3,2,1,0:T(8,128)S(1)}, u32[]{:S(2)}, u32[]{:S(2)}) collective-permute-start(f32[1,7,7,512]{3,2,1,0:T(8,128)S(1)} %slice.172), channel_id=1, source_target_pairs={{0,30},{2,0},{4,2},{6,4},{8,6},{10,8},{12,10},{14,12},{16,14},{18,... | collective-permute-start | bytes 301064 | tf_op jit(solution)/shard_map/ppermute | solution.py:291
  7.9 2.4 %collective-permute-done.x_next = f32[1,7,7,512]{3,2,1,0:T(8,128)S(1)} collective-permute-done((f32[1,7,7,512]{3,2,1,0:T(8,128)S(1)}, f32[1,7,7,512]{3,2,1,0:T(8,128)S(1)}, u32[]{:S(2)}, u32[]{:S(2)}) %collective-permute-start) | collective-permute-done | bytes 100384 | tf_op jit(solution)/shard_map/ppermute | solution.py:291
  14.1 6.1 %collective-permute-start.4 = (f32[8,8,512]{2,1,0:T(8,128)S(1)}, f32[8,8,512]{2,1,0:T(8,128)S(1)}, u32[]{:S(2)}, u32[]{:S(2)}) collective-permute-start(f32[8,8,512]{2,1,0:T(8,128)S(1)} %pad_maximum_fusion.2), channel_id=1, source_target_pairs={{0,30},{2,0},{4,2},{6,4},{8,6},{10,8},{12,10},{14,12},{16,14},{18,... | collective-permute-start | bytes 393224 | tf_op jit(solution)/shard_map/ppermute | solution.py:291
  20.3 3.2 %collective-permute-done.4.refs_3_ = f32[8,8,512]{2,1,0:T(8,128)S(1)} collective-permute-done((f32[8,8,512]{2,1,0:T(8,128)S(1)}, f32[8,8,512]{2,1,0:T(8,128)S(1)}, u32[]{:S(2)}, u32[]{:S(2)}) %collective-permute-start.4) | collective-permute-done | bytes 131104 | tf_op jit(solution)/shard_map/ppermute | solution.py:291
  23.5 5.9 %collective-permute-done.3.refs_2_ = f32[8,8,512]{2,1,0:T(8,128)S(1)} collective-permute-done((f32[8,8,512]{2,1,0:T(8,128)S(1)}, f32[8,8,512]{2,1,0:T(8,128)S(1)}, u32[]{:S(2)}, u32[]{:S(2)}) %collective-permute-start.3) | collective-permute-done | bytes 131104 | tf_op jit(solution)/shard_map/ppermute | solution.py:291
  34.6 1.9 %collective-permute-start.6 = (f32[8,8,512]{2,1,0:T(8,128)S(1)}, f32[8,8,512]{2,1,0:T(8,128)S(1)}, u32[]{:S(2)}, u32[]{:S(2)}) collective-permute-start(f32[8,8,512]{2,1,0:T(8,128)S(1)} %pad_maximum_fusion.3), channel_id=1, source_target_pairs={{0,2},{2,4},{4,6},{6,8},{8,10},{10,12},{12,14},{14,16},{16,18},{18... | collective-permute-start | bytes 393224 | tf_op jit(solution)/shard_map/ppermute | solution.py:291
  36.4 4.2 %collective-permute-done.7.refs_3_ = f32[8,8,512]{2,1,0:T(8,128)S(1)} collective-permute-done((f32[8,8,512]{2,1,0:T(8,128)S(1)}, f32[8,8,512]{2,1,0:T(8,128)S(1)}, u32[]{:S(2)}, u32[]{:S(2)}) %collective-permute-start.7) | collective-permute-done | bytes 131104 | tf_op jit(solution)/shard_map/ppermute | solution.py:291
  40.7 2.9 %collective-permute-done.6.refs_2_ = f32[8,8,512]{2,1,0:T(8,128)S(1)} collective-permute-done((f32[8,8,512]{2,1,0:T(8,128)S(1)}, f32[8,8,512]{2,1,0:T(8,128)S(1)}, u32[]{:S(2)}, u32[]{:S(2)}) %collective-permute-start.6) | collective-permute-done | bytes 131104 | tf_op jit(solution)/shard_map/ppermute | solution.py:291
  49.0 1.9 %collective-permute-start.9 = (f32[8,8,512]{2,1,0:T(8,128)S(1)}, f32[8,8,512]{2,1,0:T(8,128)S(1)}, u32[]{:S(2)}, u32[]{:S(2)}) collective-permute-start(f32[8,8,512]{2,1,0:T(8,128)S(1)} %pad_maximum_fusion.5), channel_id=1, source_target_pairs={{0,2},{2,4},{4,6},{6,8},{8,10},{10,12},{12,14},{14,16},{16,18},{18... | collective-permute-start | bytes 393224 | tf_op jit(solution)/shard_map/ppermute | solution.py:291
  50.9 4.2 %collective-permute-done.10.refs_3_ = f32[8,8,512]{2,1,0:T(8,128)S(1)} collective-permute-done((f32[8,8,512]{2,1,0:T(8,128)S(1)}, f32[8,8,512]{2,1,0:T(8,128)S(1)}, u32[]{:S(2)}, u32[]{:S(2)}) %collective-permute-start.10) | collective-permute-done | bytes 131104 | tf_op jit(solution)/shard_map/ppermute | solution.py:291
  55.1 2.9 %collective-permute-done.9.refs_2_ = f32[8,8,512]{2,1,0:T(8,128)S(1)} collective-permute-done((f32[8,8,512]{2,1,0:T(8,128)S(1)}, f32[8,8,512]{2,1,0:T(8,128)S(1)}, u32[]{:S(2)}, u32[]{:S(2)}) %collective-permute-start.9) | collective-permute-done | bytes 131104 | tf_op jit(solution)/shard_map/ppermute | solution.py:291
  63.5 9.1 %collective-permute-done.12.x_low = f32[8,8,512]{2,1,0:T(8,128)S(1)} collective-permute-done((f32[8,8,512]{2,1,0:T(8,128)S(1)}, f32[8,8,512]{2,1,0:T(8,128)S(1)}, u32[]{:S(2)}, u32[]{:S(2)}) %collective-permute-start.12) | collective-permute-done | bytes 131104 | tf_op jit(solution)/shard_map/ppermute | solution.py:291
  75.1 2.4 %shard_map.42 = (f32[392,512]{1,0:T(8,128)S(1)}, f32[1280,128]{1,0:T(8,128)S(1)}) custom-call(f32[8,8,8,512]{3,2,1,0:T(8,128)S(1)} %copy-done.9, f32[1,8,8,512]{3,2,1,0:T(8,128)S(1)} %collective-permute-done.11.y_face, f32[8,8,512]{2,1,0:T(8,128)S(1)} %collective-permute-done.12.x_low, f32[8,8,8,512]{3,2,1,0:T(8,128)S(1)} %copy-done.11, ...), custom_call_target="tpu_custom_call" | custom-call | flops 268435456 | bytes 1048576 | tf_op jit(solution)/shard_map/pallas_call | solution.py:22
  77.6 1.6 %collective-permute-done.13 = f32[640,128]{1,0:T(8,128)S(1)} collective-permute-done((f32[640,128]{1,0:T(8,128)S(1)}, f32[640,128]{1,0:T(8,128)S(1)}, u32[]{:S(2)}, u32[]{:S(2)}) %collective-permute-start.13) | collective-permute-done | bytes 327712 | tf_op jit(solution)/shard_map/ppermute | solution.py:138
  79.4 3.4 %collective-permute-start.16 = (f32[160,128]{1,0:T(8,128)S(1)}, f32[160,128]{1,0:T(8,128)S(1)}, u32[]{:S(2)}, u32[]{:S(2)}) collective-permute-start(f32[160,128]{1,0:T(8,128)S(1)} %get-tuple-element.54), channel_id=1, source_target_pairs={{0,6},{2,4},{4,2},{6,0},{8,14},{10,12},{12,10},{14,8},{16,22},{18,... | collective-permute-start | bytes 245768 | tf_op jit(solution)/shard_map/ppermute | solution.py:138
  82.8 1.6 %collective-permute-done.14 = f32[160,128]{1,0:T(8,128)S(1)} collective-permute-done((f32[160,128]{1,0:T(8,128)S(1)}, f32[160,128]{1,0:T(8,128)S(1)}, u32[]{:S(2)}, u32[]{:S(2)}) %collective-permute-start.14) | collective-permute-done | bytes 81952 | tf_op jit(solution)/shard_map/ppermute | solution.py:138
  86.0 4.1 %collective-permute-start.19 = (f32[160,128]{1,0:T(8,128)S(1)}, f32[160,128]{1,0:T(8,128)S(1)}, u32[]{:S(2)}, u32[]{:S(2)}) collective-permute-start(f32[160,128]{1,0:T(8,128)S(1)} %fusion.1), channel_id=1, source_target_pairs={{0,24},{2,26},{4,28},{6,30},{8,16},{10,18},{12,20},{14,22},{16,8},... | collective-permute-start | bytes 245768 | tf_op jit(solution)/shard_map/ppermute | solution.py:138
  91.3 2.5 %collective-permute-done.18 = f32[160,128]{1,0:T(8,128)S(1)} collective-permute-done((f32[160,128]{1,0:T(8,128)S(1)}, f32[160,128]{1,0:T(8,128)S(1)}, u32[]{:S(2)}, u32[]{:S(2)}) %collective-permute-start.18) | collective-permute-done | bytes 81952 | tf_op jit(solution)/shard_map/ppermute | solution.py:138
  93.9 1.5 %collective-permute-start.20 = (f32[160,128]{1,0:T(8,128)S(1)}, f32[160,128]{1,0:T(8,128)S(1)}, u32[]{:S(2)}, u32[]{:S(2)}) collective-permute-start(f32[160,128]{1,0:T(8,128)S(1)} %get-tuple-element.34), channel_id=1, source_target_pairs={{0,2},{2,0},{4,6},{6,4},{8,10},{10,8},{12,14},{14,12},{16,18},{18,... | collective-permute-start | bytes 245768 | tf_op jit(solution)/shard_map/ppermute | solution.py:138
  95.4 1.7 %collective-permute-start.21 = (f32[160,128]{1,0:T(8,128)S(1)}, f32[160,128]{1,0:T(8,128)S(1)}, u32[]{:S(2)}, u32[]{:S(2)}) collective-permute-start(f32[160,128]{1,0:T(8,128)S(1)} %get-tuple-element.34), channel_id=1, source_target_pairs={{0,4},{2,6},{4,0},{6,2},{8,12},{10,14},{12,8},{14,10},{16,20},{18,... | collective-permute-start | bytes 245768 | tf_op jit(solution)/shard_map/ppermute | solution.py:138
  98.4 1.4 %collective-permute-done.21 = f32[160,128]{1,0:T(8,128)S(1)} collective-permute-done((f32[160,128]{1,0:T(8,128)S(1)}, f32[160,128]{1,0:T(8,128)S(1)}, u32[]{:S(2)}, u32[]{:S(2)}) %collective-permute-start.21) | collective-permute-done | bytes 81952 | tf_op jit(solution)/shard_map/ppermute | solution.py:138
  99.8 2.6 %collective-permute-done.22 = f32[160,128]{1,0:T(8,128)S(1)} collective-permute-done((f32[160,128]{1,0:T(8,128)S(1)}, f32[160,128]{1,0:T(8,128)S(1)}, u32[]{:S(2)}, u32[]{:S(2)}) %collective-permute-start.22) | collective-permute-done | bytes 81952 | tf_op jit(solution)/shard_map/ppermute | solution.py:138
  102.6 1.5 %collective-permute-done.23 = f32[640,128]{1,0:T(8,128)S(1)} collective-permute-done((f32[640,128]{1,0:T(8,128)S(1)}, f32[640,128]{1,0:T(8,128)S(1)}, u32[]{:S(2)}, u32[]{:S(2)}) %collective-permute-start.23) | collective-permute-done | bytes 327712 | tf_op jit(solution)/shard_map/ppermute | solution.py:138
  104.1 22.3 %shard_map.43 = f32[49,7,512]{2,1,0:T(8,128)} custom-call(f32[1280,128]{1,0:T(8,128)S(1)} %bitcast.76, f32[392,512]{1,0:T(8,128)S(1)} %get-tuple-element.32.own), custom_call_target="tpu_custom_call" | custom-call | flops 134217728 | bytes 1048576 | tf_op jit(solution)/shard_map/pallas_call | solution.py:22
  (96 shorter events, 27.8 us)
Async XLA Ops:
  0.9 9.4 %collective-permute-start = (f32[1,7,7,512]{3,2,1,0:T(8,128)S(1)}, f32[1,7,7,512]{3,2,1,0:T(8,128)S(1)}, u32[]{:S(2)}, u32[]{:S(2)}) collective-permute-start(f32[1,7,7,512]{3,2,1,0:T(8,128)S(1)} %slice.172), channel_id=1, source_target_pairs={{0,30},{2,0},{4,2},{6,4},{8,6},{10,8},{12,10},{14,12},{16,14},{18,... | collective-permute-start | bytes 301064 | tf_op jit(solution)/shard_map/ppermute | solution.py:291
  10.4 1.4 %collective-permute-start.1 = (f32[8,1,7,512]{3,2,1,0:T(8,128)S(1)}, f32[8,1,7,512]{3,2,1,0:T(8,128)S(1)}, u32[]{:S(2)}, u32[]{:S(2)}) collective-permute-start(f32[8,1,7,512]{3,2,1,0:T(8,128)S(1)} %pad_maximum_fusion), channel_id=1, source_target_pairs={{0,1},{1,0},{2,3},{3,2},{4,5},{5,4},{6,7},{7,6},{8,9},{9,8},{10,11... | collective-permute-start | bytes 344072 | tf_op jit(solution)/shard_map/ppermute | solution.py:291
  12.4 1.7 %collective-permute-start.2 = (f32[2,8,8,512]{3,2,1,0:T(8,128)S(1)}, f32[2,8,8,512]{3,2,1,0:T(8,128)S(1)}, u32[]{:S(2)}, u32[]{:S(2)}) collective-permute-start(f32[2,8,8,512]{3,2,1,0:T(8,128)S(1)} %rev.9), channel_id=1, source_target_pairs={{0,1},{1,0},{2,3},{3,2},{4,5},{5,4},{6,7},{7,6},{8,9},{9,8},{10,11... | collective-permute-start | bytes 786440 | tf_op jit(solution)/shard_map/ppermute | solution.py:291
  14.1 9.4 %collective-permute-start.4 = (f32[8,8,512]{2,1,0:T(8,128)S(1)}, f32[8,8,512]{2,1,0:T(8,128)S(1)}, u32[]{:S(2)}, u32[]{:S(2)}) collective-permute-start(f32[8,8,512]{2,1,0:T(8,128)S(1)} %pad_maximum_fusion.2), channel_id=1, source_target_pairs={{0,30},{2,0},{4,2},{6,4},{8,6},{10,8},{12,10},{14,12},{16,14},{18,... | collective-permute-start | bytes 393224 | tf_op jit(solution)/shard_map/ppermute | solution.py:291
  20.2 9.1 %collective-permute-start.3 = (f32[8,8,512]{2,1,0:T(8,128)S(1)}, f32[8,8,512]{2,1,0:T(8,128)S(1)}, u32[]{:S(2)}, u32[]{:S(2)}) collective-permute-start(f32[8,8,512]{2,1,0:T(8,128)S(1)} %pad_maximum_fusion.1), channel_id=1, source_target_pairs={{0,2},{2,4},{4,6},{6,8},{8,10},{10,12},{12,14},{14,16},{16,18},{18... | collective-permute-start | bytes 393224 | tf_op jit(solution)/shard_map/ppermute | solution.py:291
  31.9 1.6 %collective-permute-start.5 = (f32[2,8,8,512]{3,2,1,0:T(8,128)S(1)}, f32[2,8,8,512]{3,2,1,0:T(8,128)S(1)}, u32[]{:S(2)}, u32[]{:S(2)}) collective-permute-start(f32[2,8,8,512]{3,2,1,0:T(8,128)S(1)} %rev.10), channel_id=1, source_target_pairs={{0,1},{1,0},{2,3},{3,2},{4,5},{5,4},{6,7},{7,6},{8,9},{9,8},{10,11... | collective-permute-start | bytes 786440 | tf_op jit(solution)/shard_map/ppermute | solution.py:291
  34.3 6.4 %collective-permute-start.7 = (f32[8,8,512]{2,1,0:T(8,128)S(1)}, f32[8,8,512]{2,1,0:T(8,128)S(1)}, u32[]{:S(2)}, u32[]{:S(2)}) collective-permute-start(f32[8,8,512]{2,1,0:T(8,128)S(1)} %pad_maximum_fusion.4), channel_id=1, source_target_pairs={{0,30},{2,0},{4,2},{6,4},{8,6},{10,8},{12,10},{14,12},{16,14},{18,... | collective-permute-start | bytes 393224 | tf_op jit(solution)/shard_map/ppermute | solution.py:291
  34.6 9.0 %collective-permute-start.6 = (f32[8,8,512]{2,1,0:T(8,128)S(1)}, f32[8,8,512]{2,1,0:T(8,128)S(1)}, u32[]{:S(2)}, u32[]{:S(2)}) collective-permute-start(f32[8,8,512]{2,1,0:T(8,128)S(1)} %pad_maximum_fusion.3), channel_id=1, source_target_pairs={{0,2},{2,4},{4,6},{6,8},{8,10},{10,12},{12,14},{14,16},{16,18},{18... | collective-permute-start | bytes 393224 | tf_op jit(solution)/shard_map/ppermute | solution.py:291
  46.3 1.6 %collective-permute-start.8 = (f32[2,8,8,512]{3,2,1,0:T(8,128)S(1)}, f32[2,8,8,512]{3,2,1,0:T(8,128)S(1)}, u32[]{:S(2)}, u32[]{:S(2)}) collective-permute-start(f32[2,8,8,512]{3,2,1,0:T(8,128)S(1)} %rev.11), channel_id=1, source_target_pairs={{0,1},{1,0},{2,3},{3,2},{4,5},{5,4},{6,7},{7,6},{8,9},{9,8},{10,11... | collective-permute-start | bytes 786440 | tf_op jit(solution)/shard_map/ppermute | solution.py:291
  48.8 6.4 %collective-permute-start.10 = (f32[8,8,512]{2,1,0:T(8,128)S(1)}, f32[8,8,512]{2,1,0:T(8,128)S(1)}, u32[]{:S(2)}, u32[]{:S(2)}) collective-permute-start(f32[8,8,512]{2,1,0:T(8,128)S(1)} %pad_maximum_fusion.6), channel_id=1, source_target_pairs={{0,30},{2,0},{4,2},{6,4},{8,6},{10,8},{12,10},{14,12},{16,14},{18,... | collective-permute-start | bytes 393224 | tf_op jit(solution)/shard_map/ppermute | solution.py:291
  49.0 9.0 %collective-permute-start.9 = (f32[8,8,512]{2,1,0:T(8,128)S(1)}, f32[8,8,512]{2,1,0:T(8,128)S(1)}, u32[]{:S(2)}, u32[]{:S(2)}) collective-permute-start(f32[8,8,512]{2,1,0:T(8,128)S(1)} %pad_maximum_fusion.5), channel_id=1, source_target_pairs={{0,2},{2,4},{4,6},{6,8},{8,10},{10,12},{12,14},{14,16},{16,18},{18... | collective-permute-start | bytes 393224 | tf_op jit(solution)/shard_map/ppermute | solution.py:291
  60.8 1.4 %collective-permute-start.11 = (f32[1,8,8,512]{3,2,1,0:T(8,128)S(1)}, f32[1,8,8,512]{3,2,1,0:T(8,128)S(1)}, u32[]{:S(2)}, u32[]{:S(2)}) collective-permute-start(f32[1,8,8,512]{3,2,1,0:T(8,128)S(1)} %slice.211), channel_id=1, source_target_pairs={{0,1},{1,0},{2,3},{3,2},{4,5},{5,4},{6,7},{7,6},{8,9},{9,8},{10,11... | collective-permute-start | bytes 393224 | tf_op jit(solution)/shard_map/ppermute | solution.py:291
  63.2 9.4 %collective-permute-start.12 = (f32[8,8,512]{2,1,0:T(8,128)S(1)}, f32[8,8,512]{2,1,0:T(8,128)S(1)}, u32[]{:S(2)}, u32[]{:S(2)}) collective-permute-start(f32[8,8,512]{2,1,0:T(8,128)S(1)} %pad_maximum_fusion.7), channel_id=1, source_target_pairs={{0,2},{2,4},{4,6},{6,8},{8,10},{10,12},{12,14},{14,16},{16,18},{18... | collective-permute-start | bytes 393224 | tf_op jit(solution)/shard_map/ppermute | solution.py:291
  77.5 1.7 %collective-permute-start.13 = (f32[640,128]{1,0:T(8,128)S(1)}, f32[640,128]{1,0:T(8,128)S(1)}, u32[]{:S(2)}, u32[]{:S(2)}) collective-permute-start(f32[640,128]{1,0:T(8,128)S(1)} %dynamic-slice_bitcast_fusion), channel_id=1, source_target_pairs={{0,1},{1,0},{2,3},{3,2},{4,5},{5,4},{6,7},{7,6},{8,9},{9,8},{10,11... | collective-permute-start | bytes 983048 | tf_op jit(solution)/shard_map/ppermute | solution.py:138
  79.2 5.1 %collective-permute-start.14 = (f32[160,128]{1,0:T(8,128)S(1)}, f32[160,128]{1,0:T(8,128)S(1)}, u32[]{:S(2)}, u32[]{:S(2)}) collective-permute-start(f32[160,128]{1,0:T(8,128)S(1)} %get-tuple-element.53), channel_id=1, source_target_pairs={{0,2},{2,0},{4,6},{6,4},{8,10},{10,8},{12,14},{14,12},{16,18},{18,... | collective-permute-start | bytes 245768 | tf_op jit(solution)/shard_map/ppermute | solution.py:138
  79.3 6.3 %collective-permute-start.15 = (f32[160,128]{1,0:T(8,128)S(1)}, f32[160,128]{1,0:T(8,128)S(1)}, u32[]{:S(2)}, u32[]{:S(2)}) collective-permute-start(f32[160,128]{1,0:T(8,128)S(1)} %get-tuple-element.55), channel_id=1, source_target_pairs={{0,4},{2,6},{4,0},{6,2},{8,12},{10,14},{12,8},{14,10},{16,20},{18,... | collective-permute-start | bytes 245768 | tf_op jit(solution)/shard_map/ppermute | solution.py:138
  79.4 6.2 %collective-permute-start.16 = (f32[160,128]{1,0:T(8,128)S(1)}, f32[160,128]{1,0:T(8,128)S(1)}, u32[]{:S(2)}, u32[]{:S(2)}) collective-permute-start(f32[160,128]{1,0:T(8,128)S(1)} %get-tuple-element.54), channel_id=1, source_target_pairs={{0,6},{2,4},{4,2},{6,0},{8,14},{10,12},{12,10},{14,8},{16,22},{18,... | collective-permute-start | bytes 245768 | tf_op jit(solution)/shard_map/ppermute | solution.py:138
  85.6 5.7 %collective-permute-start.17 = (f32[160,128]{1,0:T(8,128)S(1)}, f32[160,128]{1,0:T(8,128)S(1)}, u32[]{:S(2)}, u32[]{:S(2)}) collective-permute-start(f32[160,128]{1,0:T(8,128)S(1)} %fusion.1), channel_id=1, source_target_pairs={{0,8},{2,10},{4,12},{6,14},{8,0},{10,2},{12,4},{14,6},{16,24},{18,... | collective-permute-start | bytes 245768 | tf_op jit(solution)/shard_map/ppermute | solution.py:138
  85.7 8.1 %collective-permute-start.18 = (f32[160,128]{1,0:T(8,128)S(1)}, f32[160,128]{1,0:T(8,128)S(1)}, u32[]{:S(2)}, u32[]{:S(2)}) collective-permute-start(f32[160,128]{1,0:T(8,128)S(1)} %fusion.1), channel_id=1, source_target_pairs={{0,16},{2,18},{4,20},{6,22},{8,24},{10,26},{12,28},{14,30},{16,0},... | collective-permute-start | bytes 245768 | tf_op jit(solution)/shard_map/ppermute | solution.py:138
  86.0 7.9 %collective-permute-start.19 = (f32[160,128]{1,0:T(8,128)S(1)}, f32[160,128]{1,0:T(8,128)S(1)}, u32[]{:S(2)}, u32[]{:S(2)}) collective-permute-start(f32[160,128]{1,0:T(8,128)S(1)} %fusion.1), channel_id=1, source_target_pairs={{0,24},{2,26},{4,28},{6,30},{8,16},{10,18},{12,20},{14,22},{16,8},... | collective-permute-start | bytes 245768 | tf_op jit(solution)/shard_map/ppermute | solution.py:138
  93.9 4.5 %collective-permute-start.20 = (f32[160,128]{1,0:T(8,128)S(1)}, f32[160,128]{1,0:T(8,128)S(1)}, u32[]{:S(2)}, u32[]{:S(2)}) collective-permute-start(f32[160,128]{1,0:T(8,128)S(1)} %get-tuple-element.34), channel_id=1, source_target_pairs={{0,2},{2,0},{4,6},{6,4},{8,10},{10,8},{12,14},{14,12},{16,18},{18,... | collective-permute-start | bytes 245768 | tf_op jit(solution)/shard_map/ppermute | solution.py:138
  95.4 4.4 %collective-permute-start.21 = (f32[160,128]{1,0:T(8,128)S(1)}, f32[160,128]{1,0:T(8,128)S(1)}, u32[]{:S(2)}, u32[]{:S(2)}) collective-permute-start(f32[160,128]{1,0:T(8,128)S(1)} %get-tuple-element.34), channel_id=1, source_target_pairs={{0,4},{2,6},{4,0},{6,2},{8,12},{10,14},{12,8},{14,10},{16,20},{18,... | collective-permute-start | bytes 245768 | tf_op jit(solution)/shard_map/ppermute | solution.py:138
  97.0 5.3 %collective-permute-start.22 = (f32[160,128]{1,0:T(8,128)S(1)}, f32[160,128]{1,0:T(8,128)S(1)}, u32[]{:S(2)}, u32[]{:S(2)}) collective-permute-start(f32[160,128]{1,0:T(8,128)S(1)} %get-tuple-element.34), channel_id=1, source_target_pairs={{0,6},{2,4},{4,2},{6,0},{8,14},{10,12},{12,10},{14,8},{16,22},{18,... | collective-permute-start | bytes 245768 | tf_op jit(solution)/shard_map/ppermute | solution.py:138
  102.4 1.7 %collective-permute-start.23 = (f32[640,128]{1,0:T(8,128)S(1)}, f32[640,128]{1,0:T(8,128)S(1)}, u32[]{:S(2)}, u32[]{:S(2)}) collective-permute-start(f32[640,128]{1,0:T(8,128)S(1)} %bitcast.82), channel_id=1, source_target_pairs={{0,1},{1,0},{2,3},{3,2},{4,5},{5,4},{6,7},{7,6},{8,9},{9,8},{10,11... | collective-permute-start | bytes 983048 | tf_op jit(solution)/shard_map/ppermute | solution.py:138
  (15 other events, 63.9 us)

commit v2 on v1

--- a/solution.py
+++ b/solution.py
@@ -10,6 +10,7 @@
 DEG = 4
 SUB = 8
 LANES = 128
+VMEM_LIMIT = 8 << 20
 
 
 band_low = 4.0
@@ -27,7 +28,7 @@
                 lambda _: pl.BlockSpec(memory_space=pltpu.VMEM), out_shapes
             ),
             scratch_shapes=list(scratch),
-            compiler_params=pltpu.CompilerParams(vmem_limit_bytes=32 << 20),
+            compiler_params=pltpu.CompilerParams(vmem_limit_bytes=VMEM_LIMIT),
             cost_estimate=pl.CostEstimate(
                 flops=flops, bytes_accessed=1 << 20, transcendentals=0
             ),
@@ -66,7 +67,7 @@
     ).astype(jnp.bfloat16)
 
 
-def cell_product(values, matrix, image, faces):
+def cell_product(values, matrix, image, x_first, x_last, y_sent):
     edge = values.shape[0]
     width = values.shape[3]
     rows = values.reshape(edge**3, width).astype(jnp.bfloat16)
@@ -76,17 +77,31 @@
     where = lax.broadcasted_iota(jnp.int32, products.shape, 2)
     products = jnp.where((where == 0) | (where == edge - 1), wrap, products)
     image[...] = products
-    faces[0] = products[:, 0]
-    faces[1] = products[:, edge - 1]
-
-
-def first_body(own, x_next, y_next, matrix, values, image, faces):
+    x_first[...] = products[0]
+    x_last[...] = products[edge - 1]
+    y_sent[0] = products[:, edge - 1]
+    y_sent[1] = products[:, 0]
+
+
+def first_body(own, x_next, y_next, corner, matrix, values, *sums):
     order_now = own.shape[0]
     values[:order_now, :order_now, :order_now] = own[...]
     values[order_now:, :order_now, :order_now] = x_next[...]
-    values[:, order_now:, :order_now] = y_next[...]
+    values[:order_now, order_now:, :order_now] = y_next[...]
+    values[order_now:, order_now:, :order_now] = corner[...]
     values[:, :, order_now:] = values[:, :, :1]
-    cell_product(values[...], matrix, image, faces)
+    cell_product(values[...], matrix, *sums)
+
+
+def edge_body(*refs):
+    *planes, y_faces = refs[: len(refs) // 2 + 1]
+    outs = refs[len(refs) // 2 + 1 :]
+    edge = planes[0].shape[0]
+    for plane, out, at in zip(planes, outs, (edge - 1, 0)):
+        out[...] = plane[...]
+        out[0] = out[0] + y_faces[0, at]
+        if y_faces.shape[0] > 1:
+            out[edge - 1] = out[edge - 1] + y_faces[1, at]
 
 
 def updated(image, y_faces, x_low, x_high, current, previous, alpha, beta):
@@ -106,14 +121,14 @@
 
 def middle_body(*refs, alpha, beta):
     if beta is None:
-        image_in, y_faces, x_low, x_high, current, matrix, values, image, faces, work = refs
+        image_in, y_faces, x_low, x_high, current, matrix, values, *sums, work = refs
         previous = None
     else:
-        image_in, y_faces, x_low, x_high, current, previous, matrix, values, image, faces, work = refs
+        image_in, y_faces, x_low, x_high, current, previous, matrix, values, *sums, work = refs
     work[...] = image_in[...]
     got = updated(work, y_faces, x_low, x_high, current, previous, alpha, beta)
     values[...] = got
-    cell_product(got, matrix, image, faces)
+    cell_product(got, matrix, *sums)
 
 
 def last_body(image_in, y_face, x_low, current, previous, own, corr, work, *, alpha, beta):
@@ -291,16 +306,22 @@
     return lax.ppermute(block, axis, [(i, (i + distance) % count) for i in range(count)])
 
 
-def y_exchange(faces):
+def from_next_both(block):
+    rows, columns = lax.axis_size("wide"), lax.axis_size("narrow")
+    route = [
+        ((i + 1) % rows * columns + (j + 1) % columns, i * columns + j)
+        for i in range(rows)
+        for j in range(columns)
+    ]
+    return lax.ppermute(block, ("wide", "narrow"), route)
+
+
+def y_exchange(sent):
     if lax.axis_size("narrow") == 2:
-        return to_next(faces[::-1], "narrow", 1)
-    return jnp.stack([to_next(faces[1], "narrow", 1), to_next(faces[0], "narrow", -1)])
-
-
-def with_faces(plane, y_faces, x_at):
-    low = plane[:1] + y_faces[0, x_at][None]
-    high = plane[-1:] + y_faces[1, x_at][None]
-    return jnp.concatenate([low, plane[1:-1], high], axis=0)
+        return to_next(sent, "narrow", 1)
+    return jnp.concatenate(
+        [to_next(sent[:1], "narrow", 1), to_next(sent[1:], "narrow", -1)]
+    )
 
 
 def on_device(orbitals, cell_matrix, cell_order):
@@ -308,7 +329,8 @@
     edge = order_now + 1
     width = orbitals.shape[3]
     box = f32(edge, edge, edge, width)
-    faces_shape = f32(2, edge, edge, width)
+    plane = f32(edge, edge, width)
+    sums = (box, plane, plane, f32(2, edge, edge, width))
     cell_nodes = edge**3
     matrix = vmem_call(
         permute_body,
@@ -320,27 +342,30 @@
     )
 
     x_next = to_next(orbitals[:1], "wide", -1)
-    first_rows = jnp.concatenate([orbitals[:, :1], x_next[:, :1]], axis=0)
-    y_next = to_next(first_rows, "narrow", -1)
+    corner = from_next_both(orbitals[:1, :1])
+    y_next = to_next(orbitals[:, :1], "narrow", -1)
     product_flops = 2 * cell_nodes**2 * width
-    current, image, faces = vmem_call(
-        first_body, (box, box, faces_shape), flops=product_flops
-    )(orbitals, x_next, y_next, matrix)
+    current, image, x_first, x_last, y_sent = vmem_call(
+        first_body, (box, *sums), flops=product_flops
+    )(orbitals, x_next, y_next, corner, matrix)
 
     half_width = (band_high - band_low) / 2.0
     sigma_now = half_width / (anchor - (band_low + band_high) / 2.0)
     tau_value = 2.0 / sigma_now
     alpha, beta, previous = sigma_now / half_width, None, None
     for degree_step in range(1, DEG):
-        y_faces = y_exchange(faces)
-        x_low = to_next(with_faces(image[edge - 1], y_faces, edge - 1), "wide", 1)
-        x_high = to_next(with_faces(image[0], y_faces, 0), "wide", -1)
+        y_faces = y_exchange(y_sent)
+        x_last, x_first = vmem_call(edge_body, (plane, plane))(
+            x_last, x_first, y_faces
+        )
+        x_low = to_next(x_last, "wide", 1)
+        x_high = to_next(x_first, "wide", -1)
         operands = [image, y_faces, x_low, x_high, current]
         if previous is not None:
             operands.append(previous)
-        next_values, image, faces = vmem_call(
+        next_values, image, x_first, x_last, y_sent = vmem_call(
             functools.partial(middle_body, alpha=alpha, beta=beta),
-            (box, box, faces_shape),
+            (box, *sums),
             scratch=[pltpu.VMEM(box.shape, jnp.float32)],
             flops=product_flops,
         )(*operands, matrix)
@@ -349,12 +374,9 @@
         alpha, beta = 2.0 * sigma_new / half_width, sigma_now * sigma_new
         sigma_now = sigma_new
 
-    y_low = to_next(faces[1:], "narrow", 1)
-    last_plane = image[edge - 1]
-    last_plane = jnp.concatenate(
-        [last_plane[:1] + y_low[0, edge - 1][None], last_plane[1:]], axis=0
-    )
-    x_low = to_next(last_plane, "wide", 1)
+    y_low = to_next(y_sent[:1], "narrow", 1)
+    (x_last,) = vmem_call(edge_body, (plane,))(x_last, y_low)
+    x_low = to_next(x_last, "wide", 1)
     blocks = width // LANES
     own, corr = vmem_call(
         functools.partial(last_body, alpha=alpha, beta=beta),

time: 127 us -> 114 us (0.90)
  waiting for transfers between devices: 52.6 us -> 40.9 us
  local copies, waits for them, and re-layouts: 13.3 us -> 5.37 us
  starting transfers between devices: 30.6 us -> 37.3 us
    ppermute x13, waiting for transfers between devices: 38.5 us -> 25.6 us  [to_next(): lax.ppermute(block, axis, [(i, (i + distance) % count) for i in range(cou...]
    unnamed x28 -> x10, local copies, waits for them, and re-layouts: 9.86 us -> 1.75 us
    ppermute x13, starting transfers between devices: 18.5 us -> 25 us  [to_next(): lax.ppermute(block, axis, [(i, (i + distance) % count) for i in range(cou...]
    add x4 -> x0, other arithmetic: 1.57 us -> none  [the longest x3 1.57 us: with_faces(): low = plane[:1] + y_faces[0, x_at][None]]
    pallas_call x7 -> x11, Pallas kernels: 27.7 us -> 28.4 us  [call(): pl.pallas_call(body, out_shape=out_shapes, in_specs=[pl.BlockSpec(memory_...]
  transfers between devices with their start and end apart: 24 -> 25, of which waited for: 22 -> 19; matrix products, arithmetic and copies ran while one was open for 2% -> 2% of each run, Pallas kernels for 1% -> 1%
where the time goes in v2:
time: 114 us; the launch traced here: 113 us
  waiting for transfers between devices  40.9 us (36%)
  starting transfers between devices  37.3 us (33%)
  Pallas kernels  28.4 us (25%)
  local copies, waits for them, and re-layouts  5.37 us (5%)
    pallas_call x11, Pallas kernels, call(): pl.pallas_call(body, out_shape=out_shapes, in_specs=[pl.BlockSpec(memory_...  28.4 us
    ppermute x13, waiting for transfers between devices, to_next(): lax.ppermute(block, axis, [(i, (i + distance) % count) for i in range(cou...  25.6 us
    ppermute x13, starting transfers between devices, to_next(): lax.ppermute(block, axis, [(i, (i + distance) % count) for i in range(cou...  25 us
    ppermute x11, waiting for transfers between devices, swap(): return lax.ppermute(block, axis, [(i, i ^ distance) for i in range(count)])  14.6 us
    ppermute x11, starting transfers between devices, swap(): return lax.ppermute(block, axis, [(i, i ^ distance) for i in range(count)])  11.7 us
  transfers between devices with their start and end apart: 25, of which 19 were waited for; matrix products, arithmetic and copies ran while one was open for 2% of the time, Pallas kernels for 1%

profile of v2, /device:TPU:0, one launch (start us, length us, event | category | flops | bytes accessed | tf_op | source)
XLA Modules:
  0.0 113.3 jit_solution(7599810026640740180)
XLA Ops:
  1.0 6.9 %collective-permute-start = (f32[1,7,7,512]{3,2,1,0:T(8,128)S(1)}, f32[1,7,7,512]{3,2,1,0:T(8,128)S(1)}, u32[]{:S(2)}, u32[]{:S(2)}) collective-permute-start(f32[1,7,7,512]{3,2,1,0:T(8,128)S(1)} %slice.12), channel_id=1, source_target_pairs={{0,30},{2,0},{4,2},{6,4},{8,6},{10,8},{12,10},{14,12},{16,14},{18,... | collective-permute-start | bytes 301064 | tf_op jit(solution)/shard_map/ppermute | solution.py:306
  15.9 4.8 %collective-permute-start.5 = (f32[8,8,512]{2,1,0:T(8,128)S(1)}, f32[8,8,512]{2,1,0:T(8,128)S(1)}, u32[]{:S(2)}, u32[]{:S(2)}) collective-permute-start(f32[8,8,512]{2,1,0:T(8,128)S(1)} %get-tuple-element.37), channel_id=1, source_target_pairs={{0,30},{2,0},{4,2},{6,4},{8,6},{10,8},{12,10},{14,12},{16,14},{18,... | collective-permute-start | bytes 393224 | tf_op jit(solution)/shard_map/ppermute | solution.py:306
  20.7 3.7 %collective-permute-done.4.refs_2_ = f32[8,8,512]{2,1,0:T(8,128)S(1)} collective-permute-done((f32[8,8,512]{2,1,0:T(8,128)S(1)}, f32[8,8,512]{2,1,0:T(8,128)S(1)}, u32[]{:S(2)}, u32[]{:S(2)}) %collective-permute-start.4) | collective-permute-done | bytes 131104 | tf_op jit(solution)/shard_map/ppermute | solution.py:306
  25.0 1.5 %collective-permute-done.6.refs_2_.refs_1_ = f32[2,8,8,512]{3,2,1,0:T(8,128)S(1)} collective-permute-done((f32[2,8,8,512]{3,2,1,0:T(8,128)S(1)}, f32[2,8,8,512]{3,2,1,0:T(8,128)S(1)}, u32[]{:S(2)}, u32[]{:S(2)}) %collective-permute-start.6) | collective-permute-done | bytes 262176 | tf_op jit(solution)/shard_map/ppermute | solution.py:306
  26.7 5.6 %collective-permute-start.8 = (f32[8,8,512]{2,1,0:T(8,128)S(1)}, f32[8,8,512]{2,1,0:T(8,128)S(1)}, u32[]{:S(2)}, u32[]{:S(2)}) collective-permute-start(f32[8,8,512]{2,1,0:T(8,128)S(1)} %get-tuple-element.44), channel_id=1, source_target_pairs={{0,30},{2,0},{4,2},{6,4},{8,6},{10,8},{12,10},{14,12},{16,14},{18,... | collective-permute-start | bytes 393224 | tf_op jit(solution)/shard_map/ppermute | solution.py:306
  32.3 3.5 %collective-permute-done.7.refs_2_ = f32[8,8,512]{2,1,0:T(8,128)S(1)} collective-permute-done((f32[8,8,512]{2,1,0:T(8,128)S(1)}, f32[8,8,512]{2,1,0:T(8,128)S(1)}, u32[]{:S(2)}, u32[]{:S(2)}) %collective-permute-start.7) | collective-permute-done | bytes 131104 | tf_op jit(solution)/shard_map/ppermute | solution.py:306
  36.4 1.5 %collective-permute-done.9.refs_2_.refs_1_ = f32[2,8,8,512]{3,2,1,0:T(8,128)S(1)} collective-permute-done((f32[2,8,8,512]{3,2,1,0:T(8,128)S(1)}, f32[2,8,8,512]{3,2,1,0:T(8,128)S(1)}, u32[]{:S(2)}, u32[]{:S(2)}) %collective-permute-start.9) | collective-permute-done | bytes 262176 | tf_op jit(solution)/shard_map/ppermute | solution.py:306
  38.0 5.6 %collective-permute-start.11 = (f32[8,8,512]{2,1,0:T(8,128)S(1)}, f32[8,8,512]{2,1,0:T(8,128)S(1)}, u32[]{:S(2)}, u32[]{:S(2)}) collective-permute-start(f32[8,8,512]{2,1,0:T(8,128)S(1)} %get-tuple-element.51), channel_id=1, source_target_pairs={{0,30},{2,0},{4,2},{6,4},{8,6},{10,8},{12,10},{14,12},{16,14},{18,... | collective-permute-start | bytes 393224 | tf_op jit(solution)/shard_map/ppermute | solution.py:306
  43.6 3.6 %collective-permute-done.10.refs_2_ = f32[8,8,512]{2,1,0:T(8,128)S(1)} collective-permute-done((f32[8,8,512]{2,1,0:T(8,128)S(1)}, f32[8,8,512]{2,1,0:T(8,128)S(1)}, u32[]{:S(2)}, u32[]{:S(2)}) %collective-permute-start.10) | collective-permute-done | bytes 131104 | tf_op jit(solution)/shard_map/ppermute | solution.py:306
  48.4 1.3 %collective-permute-done.12.refs_1_.y_face = f32[1,8,8,512]{3,2,1,0:T(8,128)S(1)} collective-permute-done((f32[1,8,8,512]{3,2,1,0:T(8,128)S(1)}, f32[1,8,8,512]{3,2,1,0:T(8,128)S(1)}, u32[]{:S(2)}, u32[]{:S(2)}) %collective-permute-start.12) | collective-permute-done | bytes 131104 | tf_op jit(solution)/shard_map/ppermute | solution.py:306
  50.0 9.2 %collective-permute-done.13.x_low = f32[8,8,512]{2,1,0:T(8,128)S(1)} collective-permute-done((f32[8,8,512]{2,1,0:T(8,128)S(1)}, f32[8,8,512]{2,1,0:T(8,128)S(1)}, u32[]{:S(2)}, u32[]{:S(2)}) %collective-permute-start.13) | collective-permute-done | bytes 131104 | tf_op jit(solution)/shard_map/ppermute | solution.py:306
  59.2 2.4 %shard_map.46 = (f32[392,512]{1,0:T(8,128)S(1)}, f32[1280,128]{1,0:T(8,128)S(1)}) custom-call(f32[8,8,8,512]{3,2,1,0:T(8,128)S(1)} %get-tuple-element.53.image_in, f32[1,8,8,512]{3,2,1,0:T(8,128)S(1)} %collective-permute-done.12.refs_1_.y_face, f32[8,8,512]{2,1,0:T(8,128)S(1)} %collective-permute-done.13.x_low, ...), custom_call_target="tpu_custom_call" | custom-call | flops 268435456 | bytes 1048576 | tf_op jit(solution)/shard_map/pallas_call | solution.py:23
  63.4 1.6 %collective-permute-done.14 = f32[640,128]{1,0:T(8,128)S(1)} collective-permute-done((f32[640,128]{1,0:T(8,128)S(1)}, f32[640,128]{1,0:T(8,128)S(1)}, u32[]{:S(2)}, u32[]{:S(2)}) %collective-permute-start.14) | collective-permute-done | bytes 327712 | tf_op jit(solution)/shard_map/ppermute | solution.py:153
  66.2 3.4 %collective-permute-start.17 = (f32[160,128]{1,0:T(8,128)S(1)}, f32[160,128]{1,0:T(8,128)S(1)}, u32[]{:S(2)}, u32[]{:S(2)}) collective-permute-start(f32[160,128]{1,0:T(8,128)S(1)} %get-tuple-element.62), channel_id=1, source_target_pairs={{0,6},{2,4},{4,2},{6,0},{8,14},{10,12},{12,10},{14,8},{16,22},{18,... | collective-permute-start | bytes 245768 | tf_op jit(solution)/shard_map/ppermute | solution.py:153
  69.6 1.6 %collective-permute-done.15 = f32[160,128]{1,0:T(8,128)S(1)} collective-permute-done((f32[160,128]{1,0:T(8,128)S(1)}, f32[160,128]{1,0:T(8,128)S(1)}, u32[]{:S(2)}, u32[]{:S(2)}) %collective-permute-start.15) | collective-permute-done | bytes 81952 | tf_op jit(solution)/shard_map/ppermute | solution.py:153
  71.2 1.3 %collective-permute-done.16 = f32[160,128]{1,0:T(8,128)S(1)} collective-permute-done((f32[160,128]{1,0:T(8,128)S(1)}, f32[160,128]{1,0:T(8,128)S(1)}, u32[]{:S(2)}, u32[]{:S(2)}) %collective-permute-start.16) | collective-permute-done | bytes 81952 | tf_op jit(solution)/shard_map/ppermute | solution.py:153
  72.5 2.4 %collective-permute-start.19 = (f32[160,128]{1,0:T(8,128)S(1)}, f32[160,128]{1,0:T(8,128)S(1)}, u32[]{:S(2)}, u32[]{:S(2)}) collective-permute-start(f32[160,128]{1,0:T(8,128)S(1)} %fusion.1), channel_id=1, source_target_pairs={{0,16},{2,18},{4,20},{6,22},{8,24},{10,26},{12,28},{14,30},{16,0},... | collective-permute-start | bytes 245768 | tf_op jit(solution)/shard_map/ppermute | solution.py:153
  75.0 1.9 %collective-permute-start.20 = (f32[160,128]{1,0:T(8,128)S(1)}, f32[160,128]{1,0:T(8,128)S(1)}, u32[]{:S(2)}, u32[]{:S(2)}) collective-permute-start(f32[160,128]{1,0:T(8,128)S(1)} %fusion.1), channel_id=1, source_target_pairs={{0,24},{2,26},{4,28},{6,30},{8,16},{10,18},{12,20},{14,22},{16,8},... | collective-permute-start | bytes 245768 | tf_op jit(solution)/shard_map/ppermute | solution.py:153
  77.0 2.8 %collective-permute-done.19 = f32[160,128]{1,0:T(8,128)S(1)} collective-permute-done((f32[160,128]{1,0:T(8,128)S(1)}, f32[160,128]{1,0:T(8,128)S(1)}, u32[]{:S(2)}, u32[]{:S(2)}) %collective-permute-start.19) | collective-permute-done | bytes 81952 | tf_op jit(solution)/shard_map/ppermute | solution.py:153
  79.8 1.6 %collective-permute-done.20 = f32[160,128]{1,0:T(8,128)S(1)} collective-permute-done((f32[160,128]{1,0:T(8,128)S(1)}, f32[160,128]{1,0:T(8,128)S(1)}, u32[]{:S(2)}, u32[]{:S(2)}) %collective-permute-start.20) | collective-permute-done | bytes 81952 | tf_op jit(solution)/shard_map/ppermute | solution.py:153
  82.2 1.7 %collective-permute-start.22 = (f32[160,128]{1,0:T(8,128)S(1)}, f32[160,128]{1,0:T(8,128)S(1)}, u32[]{:S(2)}, u32[]{:S(2)}) collective-permute-start(f32[160,128]{1,0:T(8,128)S(1)} %get-tuple-element.60), channel_id=1, source_target_pairs={{0,4},{2,6},{4,0},{6,2},{8,12},{10,14},{12,8},{14,10},{16,20},{18,... | collective-permute-start | bytes 245768 | tf_op jit(solution)/shard_map/ppermute | solution.py:153
  86.7 2.6 %collective-permute-done.23 = f32[160,128]{1,0:T(8,128)S(1)} collective-permute-done((f32[160,128]{1,0:T(8,128)S(1)}, f32[160,128]{1,0:T(8,128)S(1)}, u32[]{:S(2)}, u32[]{:S(2)}) %collective-permute-start.23) | collective-permute-done | bytes 81952 | tf_op jit(solution)/shard_map/ppermute | solution.py:153
  89.4 1.5 %collective-permute-done.24 = f32[640,128]{1,0:T(8,128)S(1)} collective-permute-done((f32[640,128]{1,0:T(8,128)S(1)}, f32[640,128]{1,0:T(8,128)S(1)}, u32[]{:S(2)}, u32[]{:S(2)}) %collective-permute-start.24) | collective-permute-done | bytes 327712 | tf_op jit(solution)/shard_map/ppermute | solution.py:153
  91.0 22.4 %shard_map.47 = f32[49,7,512]{2,1,0:T(8,128)} custom-call(f32[1280,128]{1,0:T(8,128)S(1)} %bitcast.36, f32[392,512]{1,0:T(8,128)S(1)} %copy-done.2), custom_call_target="tpu_custom_call" | custom-call | flops 134217728 | bytes 1048576 | tf_op jit(solution)/shard_map/pallas_call | solution.py:23
  (64 shorter events, 18.6 us)
Async XLA Ops:
  1.0 11.7 %collective-permute-start = (f32[1,7,7,512]{3,2,1,0:T(8,128)S(1)}, f32[1,7,7,512]{3,2,1,0:T(8,128)S(1)}, u32[]{:S(2)}, u32[]{:S(2)}) collective-permute-start(f32[1,7,7,512]{3,2,1,0:T(8,128)S(1)} %slice.12), channel_id=1, source_target_pairs={{0,30},{2,0},{4,2},{6,4},{8,6},{10,8},{12,10},{14,12},{16,14},{18,... | collective-permute-start | bytes 301064 | tf_op jit(solution)/shard_map/ppermute | solution.py:306
  8.8 3.9 %collective-permute-start.1 = (f32[7,1,7,512]{3,2,1,0:T(8,128)S(1)}, f32[7,1,7,512]{3,2,1,0:T(8,128)S(1)}, u32[]{:S(2)}, u32[]{:S(2)}) collective-permute-start(f32[7,1,7,512]{3,2,1,0:T(8,128)S(1)} %slice.13), channel_id=1, source_target_pairs={{0,1},{1,0},{2,3},{3,2},{4,5},{5,4},{6,7},{7,6},{8,9},{9,8},{10,11... | collective-permute-start | bytes 301064 | tf_op jit(solution)/shard_map/ppermute | solution.py:306
  9.5 3.2 %collective-permute-start.2 = (f32[1,1,7,512]{3,2,1,0:T(8,128)S(1)}, f32[1,1,7,512]{3,2,1,0:T(8,128)S(1)}, u32[]{:S(2)}, u32[]{:S(2)}) collective-permute-start(f32[1,1,7,512]{3,2,1,0:T(8,128)S(1)} %slice.14), channel_id=1, source_target_pairs={{3,0},{2,1},{5,2},{4,3},{7,4},{6,5},{9,6},{8,7},{11,8},{10,9},{13,... | collective-permute-start | bytes 43016 | tf_op jit(solution)/shard_map/ppermute | solution.py:316
  13.3 1.7 %collective-permute-start.3 = (f32[2,8,8,512]{3,2,1,0:T(8,128)S(1)}, f32[2,8,8,512]{3,2,1,0:T(8,128)S(1)}, u32[]{:S(2)}, u32[]{:S(2)}) collective-permute-start(f32[2,8,8,512]{3,2,1,0:T(8,128)S(1)} %get-tuple-element.33), channel_id=1, source_target_pairs={{0,1},{1,0},{2,3},{3,2},{4,5},{5,4},{6,7},{7,6},{8,9},{9,8},{10,11... | collective-permute-start | bytes 786440 | tf_op jit(solution)/shard_map/ppermute | solution.py:306
  15.0 9.4 %collective-permute-start.4 = (f32[8,8,512]{2,1,0:T(8,128)S(1)}, f32[8,8,512]{2,1,0:T(8,128)S(1)}, u32[]{:S(2)}, u32[]{:S(2)}) collective-permute-start(f32[8,8,512]{2,1,0:T(8,128)S(1)} %get-tuple-element.36), channel_id=1, source_target_pairs={{0,2},{2,4},{4,6},{6,8},{8,10},{10,12},{12,14},{14,16},{16,18},{18... | collective-permute-start | bytes 393224 | tf_op jit(solution)/shard_map/ppermute | solution.py:306
  15.9 8.6 %collective-permute-start.5 = (f32[8,8,512]{2,1,0:T(8,128)S(1)}, f32[8,8,512]{2,1,0:T(8,128)S(1)}, u32[]{:S(2)}, u32[]{:S(2)}) collective-permute-start(f32[8,8,512]{2,1,0:T(8,128)S(1)} %get-tuple-element.37), channel_id=1, source_target_pairs={{0,30},{2,0},{4,2},{6,4},{8,6},{10,8},{12,10},{14,12},{16,14},{18,... | collective-permute-start | bytes 393224 | tf_op jit(solution)/shard_map/ppermute | solution.py:306
  25.0 1.6 %collective-permute-start.6 = (f32[2,8,8,512]{3,2,1,0:T(8,128)S(1)}, f32[2,8,8,512]{3,2,1,0:T(8,128)S(1)}, u32[]{:S(2)}, u32[]{:S(2)}) collective-permute-start(f32[2,8,8,512]{3,2,1,0:T(8,128)S(1)} %get-tuple-element.40), channel_id=1, source_target_pairs={{0,1},{1,0},{2,3},{3,2},{4,5},{5,4},{6,7},{7,6},{8,9},{9,8},{10,11... | collective-permute-start | bytes 786440 | tf_op jit(solution)/shard_map/ppermute | solution.py:306
  26.6 9.2 %collective-permute-start.7 = (f32[8,8,512]{2,1,0:T(8,128)S(1)}, f32[8,8,512]{2,1,0:T(8,128)S(1)}, u32[]{:S(2)}, u32[]{:S(2)}) collective-permute-start(f32[8,8,512]{2,1,0:T(8,128)S(1)} %get-tuple-element.43), channel_id=1, source_target_pairs={{0,2},{2,4},{4,6},{6,8},{8,10},{10,12},{12,14},{14,16},{16,18},{18... | collective-permute-start | bytes 393224 | tf_op jit(solution)/shard_map/ppermute | solution.py:306
  26.7 9.1 %collective-permute-start.8 = (f32[8,8,512]{2,1,0:T(8,128)S(1)}, f32[8,8,512]{2,1,0:T(8,128)S(1)}, u32[]{:S(2)}, u32[]{:S(2)}) collective-permute-start(f32[8,8,512]{2,1,0:T(8,128)S(1)} %get-tuple-element.44), channel_id=1, source_target_pairs={{0,30},{2,0},{4,2},{6,4},{8,6},{10,8},{12,10},{14,12},{16,14},{18,... | collective-permute-start | bytes 393224 | tf_op jit(solution)/shard_map/ppermute | solution.py:306
  36.3 1.6 %collective-permute-start.9 = (f32[2,8,8,512]{3,2,1,0:T(8,128)S(1)}, f32[2,8,8,512]{3,2,1,0:T(8,128)S(1)}, u32[]{:S(2)}, u32[]{:S(2)}) collective-permute-start(f32[2,8,8,512]{3,2,1,0:T(8,128)S(1)} %get-tuple-element.47), channel_id=1, source_target_pairs={{0,1},{1,0},{2,3},{3,2},{4,5},{5,4},{6,7},{7,6},{8,9},{9,8},{10,11... | collective-permute-start | bytes 786440 | tf_op jit(solution)/shard_map/ppermute | solution.py:306
  38.0 9.2 %collective-permute-start.10 = (f32[8,8,512]{2,1,0:T(8,128)S(1)}, f32[8,8,512]{2,1,0:T(8,128)S(1)}, u32[]{:S(2)}, u32[]{:S(2)}) collective-permute-start(f32[8,8,512]{2,1,0:T(8,128)S(1)} %get-tuple-element.50), channel_id=1, source_target_pairs={{0,2},{2,4},{4,6},{6,8},{8,10},{10,12},{12,14},{14,16},{16,18},{18... | collective-permute-start | bytes 393224 | tf_op jit(solution)/shard_map/ppermute | solution.py:306
  38.0 9.2 %collective-permute-start.11 = (f32[8,8,512]{2,1,0:T(8,128)S(1)}, f32[8,8,512]{2,1,0:T(8,128)S(1)}, u32[]{:S(2)}, u32[]{:S(2)}) collective-permute-start(f32[8,8,512]{2,1,0:T(8,128)S(1)} %get-tuple-element.51), channel_id=1, source_target_pairs={{0,30},{2,0},{4,2},{6,4},{8,6},{10,8},{12,10},{14,12},{16,14},{18,... | collective-permute-start | bytes 393224 | tf_op jit(solution)/shard_map/ppermute | solution.py:306
  49.7 9.4 %collective-permute-start.13 = (f32[8,8,512]{2,1,0:T(8,128)S(1)}, f32[8,8,512]{2,1,0:T(8,128)S(1)}, u32[]{:S(2)}, u32[]{:S(2)}) collective-permute-start(f32[8,8,512]{2,1,0:T(8,128)S(1)} %shard_map.45), channel_id=1, source_target_pairs={{0,2},{2,4},{4,6},{6,8},{8,10},{10,12},{12,14},{14,16},{16,18},{18... | collective-permute-start | bytes 393224 | tf_op jit(solution)/shard_map/ppermute | solution.py:306
  63.3 1.7 %collective-permute-start.14 = (f32[640,128]{1,0:T(8,128)S(1)}, f32[640,128]{1,0:T(8,128)S(1)}, u32[]{:S(2)}, u32[]{:S(2)}) collective-permute-start(f32[640,128]{1,0:T(8,128)S(1)} %dynamic-slice_bitcast_fusion), channel_id=1, source_target_pairs={{0,1},{1,0},{2,3},{3,2},{4,5},{5,4},{6,7},{7,6},{8,9},{9,8},{10,11... | collective-permute-start | bytes 983048 | tf_op jit(solution)/shard_map/ppermute | solution.py:153
  66.1 5.1 %collective-permute-start.15 = (f32[160,128]{1,0:T(8,128)S(1)}, f32[160,128]{1,0:T(8,128)S(1)}, u32[]{:S(2)}, u32[]{:S(2)}) collective-permute-start(f32[160,128]{1,0:T(8,128)S(1)} %get-tuple-element.61), channel_id=1, source_target_pairs={{0,2},{2,0},{4,6},{6,4},{8,10},{10,8},{12,14},{14,12},{16,18},{18,... | collective-permute-start | bytes 245768 | tf_op jit(solution)/shard_map/ppermute | solution.py:153
  66.1 6.3 %collective-permute-start.16 = (f32[160,128]{1,0:T(8,128)S(1)}, f32[160,128]{1,0:T(8,128)S(1)}, u32[]{:S(2)}, u32[]{:S(2)}) collective-permute-start(f32[160,128]{1,0:T(8,128)S(1)} %get-tuple-element.63), channel_id=1, source_target_pairs={{0,4},{2,6},{4,0},{6,2},{8,12},{10,14},{12,8},{14,10},{16,20},{18,... | collective-permute-start | bytes 245768 | tf_op jit(solution)/shard_map/ppermute | solution.py:153
  66.2 6.2 %collective-permute-start.17 = (f32[160,128]{1,0:T(8,128)S(1)}, f32[160,128]{1,0:T(8,128)S(1)}, u32[]{:S(2)}, u32[]{:S(2)}) collective-permute-start(f32[160,128]{1,0:T(8,128)S(1)} %get-tuple-element.62), channel_id=1, source_target_pairs={{0,6},{2,4},{4,2},{6,0},{8,14},{10,12},{12,10},{14,8},{16,22},{18,... | collective-permute-start | bytes 245768 | tf_op jit(solution)/shard_map/ppermute | solution.py:153
  72.5 4.5 %collective-permute-start.18 = (f32[160,128]{1,0:T(8,128)S(1)}, f32[160,128]{1,0:T(8,128)S(1)}, u32[]{:S(2)}, u32[]{:S(2)}) collective-permute-start(f32[160,128]{1,0:T(8,128)S(1)} %fusion.1), channel_id=1, source_target_pairs={{0,8},{2,10},{4,12},{6,14},{8,0},{10,2},{12,4},{14,6},{16,24},{18,... | collective-permute-start | bytes 245768 | tf_op jit(solution)/shard_map/ppermute | solution.py:153
  72.5 7.2 %collective-permute-start.19 = (f32[160,128]{1,0:T(8,128)S(1)}, f32[160,128]{1,0:T(8,128)S(1)}, u32[]{:S(2)}, u32[]{:S(2)}) collective-permute-start(f32[160,128]{1,0:T(8,128)S(1)} %fusion.1), channel_id=1, source_target_pairs={{0,16},{2,18},{4,20},{6,22},{8,24},{10,26},{12,28},{14,30},{16,0},... | collective-permute-start | bytes 245768 | tf_op jit(solution)/shard_map/ppermute | solution.py:153
  75.0 6.3 %collective-permute-start.20 = (f32[160,128]{1,0:T(8,128)S(1)}, f32[160,128]{1,0:T(8,128)S(1)}, u32[]{:S(2)}, u32[]{:S(2)}) collective-permute-start(f32[160,128]{1,0:T(8,128)S(1)} %fusion.1), channel_id=1, source_target_pairs={{0,24},{2,26},{4,28},{6,30},{8,16},{10,18},{12,20},{14,22},{16,8},... | collective-permute-start | bytes 245768 | tf_op jit(solution)/shard_map/ppermute | solution.py:153
  81.4 4.5 %collective-permute-start.21 = (f32[160,128]{1,0:T(8,128)S(1)}, f32[160,128]{1,0:T(8,128)S(1)}, u32[]{:S(2)}, u32[]{:S(2)}) collective-permute-start(f32[160,128]{1,0:T(8,128)S(1)} %get-tuple-element.60), channel_id=1, source_target_pairs={{0,2},{2,0},{4,6},{6,4},{8,10},{10,8},{12,14},{14,12},{16,18},{18,... | collective-permute-start | bytes 245768 | tf_op jit(solution)/shard_map/ppermute | solution.py:153
  82.2 4.4 %collective-permute-start.22 = (f32[160,128]{1,0:T(8,128)S(1)}, f32[160,128]{1,0:T(8,128)S(1)}, u32[]{:S(2)}, u32[]{:S(2)}) collective-permute-start(f32[160,128]{1,0:T(8,128)S(1)} %get-tuple-element.60), channel_id=1, source_target_pairs={{0,4},{2,6},{4,0},{6,2},{8,12},{10,14},{12,8},{14,10},{16,20},{18,... | collective-permute-start | bytes 245768 | tf_op jit(solution)/shard_map/ppermute | solution.py:153
  83.9 5.3 %collective-permute-start.23 = (f32[160,128]{1,0:T(8,128)S(1)}, f32[160,128]{1,0:T(8,128)S(1)}, u32[]{:S(2)}, u32[]{:S(2)}) collective-permute-start(f32[160,128]{1,0:T(8,128)S(1)} %get-tuple-element.60), channel_id=1, source_target_pairs={{0,6},{2,4},{4,2},{6,0},{8,14},{10,12},{12,10},{14,8},{16,22},{18,... | collective-permute-start | bytes 245768 | tf_op jit(solution)/shard_map/ppermute | solution.py:153
  89.2 1.7 %collective-permute-start.24 = (f32[640,128]{1,0:T(8,128)S(1)}, f32[640,128]{1,0:T(8,128)S(1)}, u32[]{:S(2)}, u32[]{:S(2)}) collective-permute-start(f32[640,128]{1,0:T(8,128)S(1)} %bitcast.42), channel_id=1, source_target_pairs={{0,1},{1,0},{2,3},{3,2},{4,5},{5,4},{6,7},{7,6},{8,9},{9,8},{10,11... | collective-permute-start | bytes 983048 | tf_op jit(solution)/shard_map/ppermute | solution.py:153
  (6 other events, 17.5 us)

commit v3 on v2

--- a/solution.py
+++ b/solution.py
@@ -10,7 +10,12 @@
 DEG = 4
 SUB = 8
 LANES = 128
-VMEM_LIMIT = 8 << 20
+SLAB = 16
+STRIP = 256
+PARTS = 1
+VMEM_LIMIT = 6 << 20
+LAST_LIMIT = 6 << 20
+ORTHO_LIMIT = 6 << 20
 
 
 band_low = 4.0
@@ -18,17 +23,31 @@
 anchor = 0.0
 
 
-def vmem_call(body, out_shapes, scratch=(), flops=0):
+def vmem_call(body, out_shapes, scratch=(), flops=0, scalars=0, hbm_in=(), hbm_out=(), limit=VMEM_LIMIT):
+    def spec(in_hbm):
+        return pl.BlockSpec(memory_space=pltpu.HBM if in_hbm else pltpu.VMEM)
+
     def call(*operands):
+        operands = [
+            x
+            if n < scalars
+            else pltpu.with_memory_space_constraint(
+                x, pltpu.HBM if n in hbm_in else pltpu.VMEM
+            )
+            for n, x in enumerate(operands)
+        ]
+        outs = tuple(
+            (pltpu.HBM if n in hbm_out else pltpu.VMEM)(x.shape, x.dtype)
+            for n, x in enumerate(out_shapes)
+        )
         return pl.pallas_call(
             body,
-            out_shape=out_shapes,
-            in_specs=[pl.BlockSpec(memory_space=pltpu.VMEM)] * len(operands),
-            out_specs=jax.tree.map(
-                lambda _: pl.BlockSpec(memory_space=pltpu.VMEM), out_shapes
-            ),
+            out_shape=outs,
+            in_specs=[pl.BlockSpec(memory_space=pltpu.SMEM)] * scalars
+            + [spec(n in hbm_in) for n in range(scalars, len(operands))],
+            out_specs=tuple(spec(n in hbm_out) for n in range(len(out_shapes))),
             scratch_shapes=list(scratch),
-            compiler_params=pltpu.CompilerParams(vmem_limit_bytes=VMEM_LIMIT),
+            compiler_params=pltpu.CompilerParams(vmem_limit_bytes=limit),
             cost_estimate=pl.CostEstimate(
                 flops=flops, bytes_accessed=1 << 20, transcendentals=0
             ),
@@ -131,7 +150,8 @@
     cell_product(got, matrix, *sums)
 
 
-def last_body(image_in, y_face, x_low, current, previous, own, corr, work, *, alpha, beta):
+def last_body(mine, image_in, y_face, x_low, current, previous, own, *refs, alpha, beta):
+    *parts, corr, work, values, sem = refs
     edge = image_in.shape[0]
     width = image_in.shape[3]
     work[...] = image_in[...]
@@ -140,12 +160,20 @@
     where = lax.broadcasted_iota(jnp.int32, got.shape, 2)
     got = jnp.where(where == edge - 1, 0.0, got)
     flat = got.reshape((edge - 1) ** 2 * edge, width)
-    own[...] = flat
+    values[...] = flat
+    keep = pltpu.make_async_copy(values, own, sem)
+    keep.start()
     at = 0
-    for j in range(0, width, LANES):
-        block = exact_dot(flat[:, j:], flat[:, j : j + LANES], ((0,), (0,)))
-        corr[at : at + width - j] = block
-        at += width - j
+    for i in range(0, width, STRIP):
+        strip = exact_dot(flat[:, i : i + STRIP], flat[:, i:], ((0,), (0,)))
+        for first in range(0, STRIP, LANES):
+            for j in range(first, width - i, LANES):
+                corr[at : at + LANES] = strip[first : first + LANES, j : j + LANES]
+                at += LANES
+    rows = parts[0].shape[0]
+    for d, part in enumerate(parts):
+        part[...] = corr[pl.ds(pl.multiple_of((mine[0] ^ d) * rows, SUB), rows)]
+    keep.wait()
 
 
 def swap(block, axis, distance):
@@ -162,25 +190,51 @@
     return stages
 
 
-def summed(block):
-    rows, lanes = block.shape
-    stages = stages_of("narrow", lax.axis_size("narrow")) + stages_of(
+def all_stages():
+    return stages_of("narrow", lax.axis_size("narrow")) + stages_of(
         "wide", lax.axis_size("wide")
     )
-    cut = 1
-    for _, _, radix in stages[:-1]:
+
+
+def cut_rows(rows):
+    cut = SUB
+    for _, _, radix in all_stages()[:-1]:
         cut *= radix
-    padded = -(-rows // (cut * SUB)) * cut * SUB
-    if padded != rows:
-        block = jnp.pad(block, ((0, padded - rows), (0, 0)))
-    for axis, stride, radix in stages[:-1]:
-        mine = lax.axis_index(axis) // stride % radix
-        parts = block.reshape(radix, -1, lanes)
-        total = lax.dynamic_index_in_dim(parts, mine, 0, False)
-        for d in range(1, radix):
-            sent = lax.dynamic_index_in_dim(parts, mine ^ d, 0, False)
-            total = total + swap(sent, axis, d * stride)
-        block = total
+    return -(-rows // cut) * cut
+
+
+def cut_body(mine, *refs, count):
+    terms, (*parts, work) = refs[:count], refs[count:]
+    got = terms[0][...]
+    for term in terms[1:]:
+        got = got + term[...]
+    work[...] = got
+    rows = parts[0].shape[0]
+    for d, part in enumerate(parts):
+        part[...] = work[pl.ds(pl.multiple_of((mine[0] ^ d) * rows, SUB), rows)]
+
+
+def digit(stage):
+    axis, stride, radix = stage
+    return (lax.axis_index(axis) // stride % radix).astype(jnp.int32)[None]
+
+
+def summed(parts):
+    lanes = parts[0].shape[1]
+    stages = all_stages()
+    for stage, after in zip(stages[:-1], stages[1:]):
+        axis, stride, _ = stage
+        terms = [swap(part, axis, d * stride) for d, part in enumerate(parts)]
+        rows, radix = terms[0].shape[0], after[2]
+        if after == stages[-1]:
+            radix = 1
+        parts = vmem_call(
+            functools.partial(cut_body, count=len(terms)),
+            (f32(rows // radix, lanes),) * radix,
+            scratch=[pltpu.VMEM((rows, lanes), jnp.float32)],
+            scalars=1,
+        )(digit(after) if radix > 1 else jnp.zeros((1,), jnp.int32), *terms)
+    block = parts[0]
     axis, stride, radix = stages[-1]
     got = [block] + [swap(block, axis, d * stride) for d in range(1, radix)]
     while len(got) > 1:
@@ -195,7 +249,7 @@
                 parts, swap(block, axis, d * stride), mine ^ d, 0
             )
         block = parts.reshape(-1, lanes)
-    return block[:rows]
+    return block
 
 
 def lane_spread(tile, column):
@@ -206,99 +260,187 @@
     return jnp.broadcast_to(tile[row : row + 1, :], tile.shape)
 
 
+def total(terms):
+    while len(terms) > 1:
+        terms = [a + b for a, b in zip(terms[::2], terms[1::2])]
+    return terms[0]
+
+
 def inverse_factor(block):
     size = block.shape[0]
-    steps = size // SUB
-    left = [block[SUB * t : SUB * (t + 1)] for t in range(steps)]
+    steps, per = size // SUB, SLAB // SUB
+    tiles = [block[SUB * t : SUB * (t + 1)] for t in range(steps)]
     rows = lax.broadcasted_iota(jnp.int32, (SUB, size), 0)
     cols = lax.broadcasted_iota(jnp.int32, (SUB, size), 1)
-    right = [
-        jnp.where(cols == rows + SUB * t, 1.0, 0.0).astype(jnp.float32)
-        for t in range(steps)
-    ]
-    done = []
-    for s in range(steps):
+    done = [None] * steps
+    for s in range(0, steps, per):
         base = SUB * s
-        spread = [lane_spread(left[s], base + d) for d in range(SUB)]
-        a = {
-            (c, d): row_spread(spread[d], c)
-            for d in range(SUB)
-            for c in range(d, SUB)
-        }
-        scale, low = [], {}
-        for k in range(SUB):
-            scale.append(lax.rsqrt(a[k, k]))
-            for c in range(k + 1, SUB):
-                low[c, k] = a[c, k] * scale[k]
-            for d in range(k + 1, SUB):
-                for c in range(d, SUB):
-                    a[c, d] = a[c, d] - low[c, k] * low[d, k]
-
-        def forward(tile):
-            got = []
-            for k in range(SUB):
-                row = row_spread(tile, k)
-                for m in range(k):
-                    row = row - low[k, m] * got[m]
-                got.append(row * scale[k])
-            return got
-
-        def backward(got):
-            back = [None] * SUB
-            for k in reversed(range(SUB)):
-                row = got[k]
-                for m in range(k + 1, SUB):
-                    row = row - low[m, k] * back[m]
-                back[k] = row * scale[k]
-            return back
-
-        inverse = forward(right[s])
-        packed = inverse[0]
-        for k in range(1, SUB):
-            packed = jnp.where(rows == k, inverse[k], packed)
-        done.append(packed)
-        if s + 1 == steps:
-            break
-        upper = forward(left[s])
-        t = s + 1
-        factors = []
-        for k in range(SUB):
-            column = lane_spread(left[t], base + k)
-            for m in range(k):
-                column = column - factors[m] * low[k, m]
-            factors.append(column * scale[k])
-        for k in range(SUB):
-            left[t] = left[t] - factors[k] * upper[k]
-            right[t] = right[t] - factors[k] * inverse[k]
-        if s + 2 < steps:
-            upper, inverse = backward(upper), backward(inverse)
-        for t in range(s + 2, steps):
-            raw = [lane_spread(left[t], base + k) for k in range(SUB)]
-            for k in range(SUB):
-                left[t] = left[t] - raw[k] * upper[k]
-                right[t] = right[t] - raw[k] * inverse[k]
-    return jnp.concatenate(done, axis=0)
-
-
-def ortho_body(corr, own, out, lower, rest, *, scale):
+        own = (cols >= base) & (cols < base + SLAB)
+        col = [
+            {
+                t: lane_spread(tiles[t], base + d)
+                for t in range(s, s + per)
+                if SUB * (t - s + 1) > d
+            }
+            for d in range(SLAB)
+        ]
+        before = list(tiles)
+        for t in range(s, s + per):
+            unit = jnp.where(cols == rows + SUB * t, 1.0, 0.0)
+            tiles[t] = jnp.where(own, unit, tiles[t])
+        for t in range(s + per, steps):
+            tiles[t] = jnp.where(own, 0.0, tiles[t])
+
+        def at(column, r):
+            return row_spread(column[s + r // SUB], r % SUB)
+
+        low, scale = [], []
+        for k in range(0, SLAB, 2):
+            x, y = col[k], col[k + 1]
+            a, b, c = at(x, k), at(x, k + 1), at(y, k + 1)
+            root = lax.rsqrt(a)
+            next_root = lax.rsqrt(a * c - b * b)
+            over = next_root * next_root
+            p, q, u = {}, {}, {}
+            for t in y:
+                u[t] = a * y[t] - b * x[t]
+                p[t] = (c * x[t] - b * y[t]) * over
+                q[t] = u[t] * over
+            for d in range(k + 2, SLAB):
+                xd, yd = at(x, d), at(y, d)
+                for t in col[d]:
+                    col[d][t] = col[d][t] - (p[t] * xd + q[t] * yd)
+            both = root * next_root
+            here, r = s + k // SUB, k % SUB
+            first = row_spread(tiles[here], r)
+            second = row_spread(tiles[here], r + 1)
+            for t in y:
+                pm, qm = p[t], q[t]
+                if t == here:
+                    ratio = jnp.where(rows == r + 1, b * (root * root), 0.0)
+                    pm = jnp.where(rows > r + 1, pm, ratio)
+                    qm = jnp.where(rows > r + 1, qm, 0.0)
+                tiles[t] = tiles[t] - (pm * first + qm * second)
+            low.append({t: x[t] * root for t in y})
+            low.append({t: u[t] * both for t in y})
+            scale += [root, a * both]
+        upper = []
+        for i in range(per):
+            t = s + i
+            factors = scale[SUB * i]
+            for k in range(1, SUB):
+                factors = jnp.where(rows == k, scale[SUB * i + k], factors)
+            tiles[t] = tiles[t] * factors
+            done[t] = jnp.where(cols < base + SLAB, tiles[t], 0.0)
+            upper += [row_spread(tiles[t], k) for k in range(SUB)]
+        yield None
+        if s + per < steps:
+            solved = [None] * SLAB
+            for k in reversed(range(SLAB)):
+                row = upper[k]
+                for m in reversed(range(k + 1, SLAB)):
+                    row = row - at(low[k], m) * solved[m]
+                solved[k] = row * scale[k]
+            for t in range(s + per, steps):
+                tiles[t] = tiles[t] - total(
+                    [
+                        lane_spread(before[t], base + k) * solved[k]
+                        for k in reversed(range(SLAB))
+                    ]
+                )
+    yield jnp.concatenate(done, axis=0)
+
+
+def ortho_body(corr, own, out, blocks, rest, done, sent, sems, *, scale):
     width = own.shape[1]
     count = width // LANES
-    at = 0
-    for j in range(0, width, LANES):
-        lower[j:, j : j + LANES] = corr[at : at + width - j] * scale
-        at += width - j
-    rest[...] = own[...]
+    nodes = own.shape[0]
+    part = nodes // PARTS
+
+    def span(k):
+        return pl.ds(LANES * k, LANES)
+
+    work = []
+
+    def factored(block):
+        share = -(-len(work) // (LANES // SLAB - 1))
+        for got in inverse_factor(block):
+            if got is None:
+                for task in [work.pop(0) for _ in range(min(share, len(work)))]:
+                    task()
+        while work:
+            work.pop(0)()
+        return got
+
+    place, at = {}, 0
+    for i in range(count):
+        for j in range(i, count):
+            place[i, j] = at
+            at += 1
+
+    def piece(i, j):
+        return corr[place[i, j] * LANES : (place[i, j] + 1) * LANES] * scale
+
+    def set_up():
+        for (i, j), n in place.items():
+            if j > 0:
+                blocks[n] = piece(i, j)
+        rest[...] = own[...]
+
+    def store(k):
+        return pltpu.make_async_copy(sent.at[k], out.at[:, :, span(k)], sems.at[k])
+
+    def finish(rows, k, block):
+        done[rows, :] = block
+        first, last = rows.start // SUB, rows.stop // SUB
+        shaped = block.reshape(last - first, SUB, LANES)
+        sent[k, first:last] = shaped[:, : SUB - 1]
+
+    work.append(set_up)
+    inverse = factored(piece(0, 0))
+    for k in range(count - 1):
+        near = exact_dot(inverse, blocks[place[k, k + 1]])
+        diagonal = blocks[place[k + 1, k + 1]] - exact_dot(near, near, ((0,), (0,)))
+        ups = {k + 1: near}
+
+        def up_of(j, k=k, inverse=inverse, ups=ups):
+            ups[j] = exact_dot(inverse, blocks[place[k, j]])
+
+        def update(i, j, ups=ups):
+            n = place[i, j]
+            blocks[n] = blocks[n] - exact_dot(ups[i], ups[j], ((0,), (0,)))
+
+        def solve(rows, k=k, inverse=inverse):
+            finish(rows, k, exact_dot(rest[rows, span(k)], inverse, ((1,), (1,))))
+
+        def subtract(rows, j, ups=ups):
+            rest[rows, span(j)] = rest[rows, span(j)] - exact_dot(done[rows, :], ups[j])
+
+        strips = [slice(r, r + part) for r in range(0, nodes, part)]
+        later = range(k + 2, count)
+        work += [functools.partial(up_of, j) for j in later]
+        work += [
+            functools.partial(update, i, j)
+            for i in range(k + 1, count)
+            for j in range(max(i, k + 2), count)
+        ]
+        work += [functools.partial(solve, rows) for rows in strips]
+        work += [
+            functools.partial(subtract, rows, j)
+            for j in range(k + 1, count)
+            for rows in strips
+        ]
+        inverse = factored(diagonal)
+    last = count - 1
+    finish(
+        slice(0, nodes),
+        last,
+        exact_dot(rest[:, span(last)], inverse, ((1,), (1,))),
+    )
     for k in range(count):
-        begin, end = LANES * k, LANES * (k + 1)
-        inverse = inverse_factor(lower[begin:end, begin:end])
-        block = exact_dot(rest[:, begin:end], inverse, ((1,), (1,)))
-        out[:, :, begin:end] = block.reshape(out.shape[0], SUB, LANES)[:, : SUB - 1]
-        if k + 1 < count:
-            under = exact_dot(lower[end:, begin:end], inverse, ((1,), (1,)))
-            lower[end:, end:] = lower[end:, end:] - exact_dot(
-                under, under, ((1,), (1,))
-            )
-            rest[:, end:] = rest[:, end:] - exact_dot(block, under, ((1,), (1,)))
+        store(k).start()
+    for k in range(count):
+        store(k).wait()
 
 
 def to_next(block, axis, distance):
@@ -332,9 +474,9 @@
     plane = f32(edge, edge, width)
     sums = (box, plane, plane, f32(2, edge, edge, width))
     cell_nodes = edge**3
-    matrix = vmem_call(
+    (matrix,) = vmem_call(
         permute_body,
-        jax.ShapeDtypeStruct((cell_nodes, cell_nodes), jnp.bfloat16),
+        (jax.ShapeDtypeStruct((cell_nodes, cell_nodes), jnp.bfloat16),),
         flops=4 * cell_nodes**3,
     )(
         cell_matrix.reshape(cell_nodes, cell_nodes),
@@ -378,26 +520,39 @@
     (x_last,) = vmem_call(edge_body, (plane,))(x_last, y_low)
     x_low = to_next(x_last, "wide", 1)
     blocks = width // LANES
-    own, corr = vmem_call(
+    rows = cut_rows(blocks * (blocks + 1) // 2 * LANES)
+    first_stage = all_stages()[0]
+    radix = first_stage[2]
+    own, *parts = vmem_call(
         functools.partial(last_body, alpha=alpha, beta=beta),
-        (
-            f32(order_now**2 * edge, width),
-            f32(blocks * (blocks + 1) // 2 * LANES, LANES),
-        ),
-        scratch=[pltpu.VMEM(box.shape, jnp.float32)],
+        (f32(order_now**2 * edge, width),) + (f32(rows // radix, LANES),) * radix,
+        scratch=[
+            pltpu.VMEM((rows, LANES), jnp.float32),
+            pltpu.VMEM(box.shape, jnp.float32),
+            pltpu.VMEM((order_now**2 * edge, width), jnp.float32),
+            pltpu.SemaphoreType.DMA,
+        ],
         flops=2 * cell_nodes * width**2,
-    )(image, y_low, x_low, current, previous)
+        hbm_out=(0,),
+        scalars=1,
+        limit=LAST_LIMIT,
+    )(digit(first_stage), image, y_low, x_low, current, previous)
 
     nodes = order_now**3 * lax.axis_size("wide") * lax.axis_size("narrow")
-    corr = summed(corr)
-    out = vmem_call(
+    corr = summed(parts)
+    (out,) = vmem_call(
         functools.partial(ortho_body, scale=1.0 / nodes),
-        f32(order_now**2, order_now, width),
+        (f32(order_now**2, order_now, width),),
         scratch=[
-            pltpu.VMEM((width, width), jnp.float32),
+            pltpu.VMEM((corr.shape[0] // LANES, LANES, LANES), jnp.float32),
             pltpu.VMEM(own.shape, jnp.float32),
+            pltpu.VMEM((own.shape[0], LANES), jnp.float32),
+            pltpu.VMEM((blocks, order_now**2, order_now, LANES), jnp.float32),
+            pltpu.SemaphoreType.DMA((blocks,)),
         ],
         flops=width**3,
+        limit=ORTHO_LIMIT,
+        hbm_out=(0,),
     )(corr, own)
     return out.reshape(orbitals.shape)
 

time: 114 us -> 107 us (0.939)
  Pallas kernels: 28.4 us -> 23.5 us
  local copies, waits for them, and re-layouts: 5.37 us -> 3.59 us
    pallas_call x11 -> x13, Pallas kernels: 28.4 us -> 23.5 us  [call(): pl.pallas_call(body, out_shape=outs, in_specs=[pl.BlockSpec(memory_space=...]
    unnamed x10 -> x6, local copies, waits for them, and re-layouts: 1.75 us -> 0.02 us
    ppermute x11 -> x13, starting transfers between devices: 11.7 us -> 12.6 us  [swap(): return lax.ppermute(block, axis, [(i, i ^ distance) for i in range(count)])]
    ppermute x11 -> x13, waiting for transfers between devices: 14.6 us -> 14.8 us  [swap(): return lax.ppermute(block, axis, [(i, i ^ distance) for i in range(count)])]
  transfers between devices with their start and end apart: 25 -> 27, of which waited for: 19 -> 19; matrix products, arithmetic and copies ran while one was open for 2% -> 2% of each run, Pallas kernels for 1% -> 1%
where the time goes in v3:
time: 107 us
  waiting for transfers between devices  41.1 us (38%)
  starting transfers between devices  38.2 us (36%)
  Pallas kernels  23.5 us (22%)
  local copies, waits for them, and re-layouts  3.59 us (3%)
    ppermute x13, waiting for transfers between devices, to_next(): lax.ppermute(block, axis, [(i, (i + distance) % count) for i in range(cou...  25.6 us
    ppermute x13, starting transfers between devices, to_next(): lax.ppermute(block, axis, [(i, (i + distance) % count) for i in range(cou...  25 us
    pallas_call x13, Pallas kernels, call(): pl.pallas_call(body, out_shape=outs, in_specs=[pl.BlockSpec(memory_space=...  23.5 us
    ppermute x13, waiting for transfers between devices, swap(): return lax.ppermute(block, axis, [(i, i ^ distance) for i in range(count)])  14.8 us
    ppermute x13, starting transfers between devices, swap(): return lax.ppermute(block, axis, [(i, i ^ distance) for i in range(count)])  12.6 us
  transfers between devices with their start and end apart: 27, of which 19 were waited for; matrix products, arithmetic and copies ran while one was open for 2% of the time, Pallas kernels for 1%

profile of v3, /device:TPU:0, one launch (start us, length us, event | category | flops | bytes accessed | tf_op | source)
XLA Modules:
  0.0 106.9 jit_solution(17109392834069410659)
XLA Ops:
  1.0 6.9 %collective-permute-start = (f32[1,7,7,512]{3,2,1,0:T(8,128)S(1)}, f32[1,7,7,512]{3,2,1,0:T(8,128)S(1)}, u32[]{:S(2)}, u32[]{:S(2)}) collective-permute-start(f32[1,7,7,512]{3,2,1,0:T(8,128)S(1)} %slice.12), channel_id=1, source_target_pairs={{0,30},{2,0},{4,2},{6,4},{8,6},{10,8},{12,10},{14,12},{16,14},{18,... | collective-permute-start | bytes 301064 | tf_op jit(solution)/shard_map/ppermute | solution.py:448
  15.9 4.8 %collective-permute-start.5 = (f32[8,8,512]{2,1,0:T(8,128)S(1)}, f32[8,8,512]{2,1,0:T(8,128)S(1)}, u32[]{:S(2)}, u32[]{:S(2)}) collective-permute-start(f32[8,8,512]{2,1,0:T(8,128)S(1)} %get-tuple-element.42), channel_id=1, source_target_pairs={{0,30},{2,0},{4,2},{6,4},{8,6},{10,8},{12,10},{14,12},{16,14},{18,... | collective-permute-start | bytes 393224 | tf_op jit(solution)/shard_map/ppermute | solution.py:448
  20.7 3.7 %collective-permute-done.4.refs_2_ = f32[8,8,512]{2,1,0:T(8,128)S(1)} collective-permute-done((f32[8,8,512]{2,1,0:T(8,128)S(1)}, f32[8,8,512]{2,1,0:T(8,128)S(1)}, u32[]{:S(2)}, u32[]{:S(2)}) %collective-permute-start.4) | collective-permute-done | bytes 131104 | tf_op jit(solution)/shard_map/ppermute | solution.py:448
  25.0 1.5 %collective-permute-done.6.refs_2_.refs_1_ = f32[2,8,8,512]{3,2,1,0:T(8,128)S(1)} collective-permute-done((f32[2,8,8,512]{3,2,1,0:T(8,128)S(1)}, f32[2,8,8,512]{3,2,1,0:T(8,128)S(1)}, u32[]{:S(2)}, u32[]{:S(2)}) %collective-permute-start.6) | collective-permute-done | bytes 262176 | tf_op jit(solution)/shard_map/ppermute | solution.py:448
  26.7 5.6 %collective-permute-start.8 = (f32[8,8,512]{2,1,0:T(8,128)S(1)}, f32[8,8,512]{2,1,0:T(8,128)S(1)}, u32[]{:S(2)}, u32[]{:S(2)}) collective-permute-start(f32[8,8,512]{2,1,0:T(8,128)S(1)} %get-tuple-element.49), channel_id=1, source_target_pairs={{0,30},{2,0},{4,2},{6,4},{8,6},{10,8},{12,10},{14,12},{16,14},{18,... | collective-permute-start | bytes 393224 | tf_op jit(solution)/shard_map/ppermute | solution.py:448
  32.3 3.5 %collective-permute-done.7.refs_2_ = f32[8,8,512]{2,1,0:T(8,128)S(1)} collective-permute-done((f32[8,8,512]{2,1,0:T(8,128)S(1)}, f32[8,8,512]{2,1,0:T(8,128)S(1)}, u32[]{:S(2)}, u32[]{:S(2)}) %collective-permute-start.7) | collective-permute-done | bytes 131104 | tf_op jit(solution)/shard_map/ppermute | solution.py:448
  36.4 1.5 %collective-permute-done.9.refs_2_.refs_1_ = f32[2,8,8,512]{3,2,1,0:T(8,128)S(1)} collective-permute-done((f32[2,8,8,512]{3,2,1,0:T(8,128)S(1)}, f32[2,8,8,512]{3,2,1,0:T(8,128)S(1)}, u32[]{:S(2)}, u32[]{:S(2)}) %collective-permute-start.9) | collective-permute-done | bytes 262176 | tf_op jit(solution)/shard_map/ppermute | solution.py:448
  38.0 5.6 %collective-permute-start.11 = (f32[8,8,512]{2,1,0:T(8,128)S(1)}, f32[8,8,512]{2,1,0:T(8,128)S(1)}, u32[]{:S(2)}, u32[]{:S(2)}) collective-permute-start(f32[8,8,512]{2,1,0:T(8,128)S(1)} %get-tuple-element.56), channel_id=1, source_target_pairs={{0,30},{2,0},{4,2},{6,4},{8,6},{10,8},{12,10},{14,12},{16,14},{18,... | collective-permute-start | bytes 393224 | tf_op jit(solution)/shard_map/ppermute | solution.py:448
  43.6 3.6 %collective-permute-done.10.refs_2_ = f32[8,8,512]{2,1,0:T(8,128)S(1)} collective-permute-done((f32[8,8,512]{2,1,0:T(8,128)S(1)}, f32[8,8,512]{2,1,0:T(8,128)S(1)}, u32[]{:S(2)}, u32[]{:S(2)}) %collective-permute-start.10) | collective-permute-done | bytes 131104 | tf_op jit(solution)/shard_map/ppermute | solution.py:448
  48.4 1.3 %collective-permute-done.12.refs_1_.y_face = f32[1,8,8,512]{3,2,1,0:T(8,128)S(1)} collective-permute-done((f32[1,8,8,512]{3,2,1,0:T(8,128)S(1)}, f32[1,8,8,512]{3,2,1,0:T(8,128)S(1)}, u32[]{:S(2)}, u32[]{:S(2)}) %collective-permute-start.12) | collective-permute-done | bytes 131104 | tf_op jit(solution)/shard_map/ppermute | solution.py:448
  50.0 9.2 %collective-permute-done.13.x_low = f32[8,8,512]{2,1,0:T(8,128)S(1)} collective-permute-done((f32[8,8,512]{2,1,0:T(8,128)S(1)}, f32[8,8,512]{2,1,0:T(8,128)S(1)}, u32[]{:S(2)}, u32[]{:S(2)}) %collective-permute-start.13) | collective-permute-done | bytes 131104 | tf_op jit(solution)/shard_map/ppermute | solution.py:448
  59.2 2.8 %shard_map.46 = (f32[392,512]{1,0:T(8,128)}, f32[640,128]{1,0:T(8,128)}, f32[640,128]{1,0:T(8,128)}) custom-call(s32[1]{0:T(128)} %bitcast.1.mine, f32[8,8,8,512]{3,2,1,0:T(8,128)S(1)} %get-tuple-element.58.image_in, f32[1,8,8,512]{3,2,1,0:T(8,128)S(1)} %collective-permute-done.12.refs_1_.y_face, f32[8,8,512]{2,1,0:T(8,128)S(1)} %collective-permute-done.13.x_low, ...), custom_call_target="tpu_custom_call" | custom-call | flops 268435456 | bytes 1048576 | tf_op jit(solution)/shard_map/pallas_call | solution.py:43
  63.0 1.8 %collective-permute-done.15.refs_1_ = f32[640,128]{1,0:T(8,128)S(1)} collective-permute-done((f32[640,128]{1,0:T(8,128)}, f32[640,128]{1,0:T(8,128)S(1)}, u32[]{:S(2)}, u32[]{:S(2)}) %collective-permute-start.15) | collective-permute-done | bytes 327712 | tf_op jit(solution)/shard_map/ppermute | solution.py:181
  65.0 3.4 %collective-permute-start.19 = (f32[160,128]{1,0:T(8,128)S(1)}, f32[160,128]{1,0:T(8,128)S(1)}, u32[]{:S(2)}, u32[]{:S(2)}) collective-permute-start(f32[160,128]{1,0:T(8,128)S(1)} %get-tuple-element.67), channel_id=1, source_target_pairs={{0,6},{2,4},{4,2},{6,0},{8,14},{10,12},{12,10},{14,8},{16,22},{18,... | collective-permute-start | bytes 245768 | tf_op jit(solution)/shard_map/ppermute | solution.py:181
  68.4 1.6 %collective-permute-done.17.refs_1_ = f32[160,128]{1,0:T(8,128)S(1)} collective-permute-done((f32[160,128]{1,0:T(8,128)S(1)}, f32[160,128]{1,0:T(8,128)S(1)}, u32[]{:S(2)}, u32[]{:S(2)}) %collective-permute-start.17) | collective-permute-done | bytes 81952 | tf_op jit(solution)/shard_map/ppermute | solution.py:181
  70.0 1.3 %collective-permute-done.18.refs_2_ = f32[160,128]{1,0:T(8,128)S(1)} collective-permute-done((f32[160,128]{1,0:T(8,128)S(1)}, f32[160,128]{1,0:T(8,128)S(1)}, u32[]{:S(2)}, u32[]{:S(2)}) %collective-permute-start.18) | collective-permute-done | bytes 81952 | tf_op jit(solution)/shard_map/ppermute | solution.py:181
  71.4 2.4 %collective-permute-start.21 = (f32[160,128]{1,0:T(8,128)S(1)}, f32[160,128]{1,0:T(8,128)S(1)}, u32[]{:S(2)}, u32[]{:S(2)}) collective-permute-start(f32[160,128]{1,0:T(8,128)S(1)} %shard_map.48), channel_id=1, source_target_pairs={{0,16},{2,18},{4,20},{6,22},{8,24},{10,26},{12,28},{14,30},{16,0},... | collective-permute-start | bytes 245768 | tf_op jit(solution)/shard_map/ppermute | solution.py:181
  73.8 1.9 %collective-permute-start.22 = (f32[160,128]{1,0:T(8,128)S(1)}, f32[160,128]{1,0:T(8,128)S(1)}, u32[]{:S(2)}, u32[]{:S(2)}) collective-permute-start(f32[160,128]{1,0:T(8,128)S(1)} %shard_map.48), channel_id=1, source_target_pairs={{0,24},{2,26},{4,28},{6,30},{8,16},{10,18},{12,20},{14,22},{16,8},... | collective-permute-start | bytes 245768 | tf_op jit(solution)/shard_map/ppermute | solution.py:181
  75.8 2.8 %collective-permute-done.21 = f32[160,128]{1,0:T(8,128)S(1)} collective-permute-done((f32[160,128]{1,0:T(8,128)S(1)}, f32[160,128]{1,0:T(8,128)S(1)}, u32[]{:S(2)}, u32[]{:S(2)}) %collective-permute-start.21) | collective-permute-done | bytes 81952 | tf_op jit(solution)/shard_map/ppermute | solution.py:181
  78.6 1.6 %collective-permute-done.22 = f32[160,128]{1,0:T(8,128)S(1)} collective-permute-done((f32[160,128]{1,0:T(8,128)S(1)}, f32[160,128]{1,0:T(8,128)S(1)}, u32[]{:S(2)}, u32[]{:S(2)}) %collective-permute-start.22) | collective-permute-done | bytes 81952 | tf_op jit(solution)/shard_map/ppermute | solution.py:181
  81.0 1.7 %collective-permute-start.24 = (f32[160,128]{1,0:T(8,128)S(1)}, f32[160,128]{1,0:T(8,128)S(1)}, u32[]{:S(2)}, u32[]{:S(2)}) collective-permute-start(f32[160,128]{1,0:T(8,128)S(1)} %get-tuple-element.70), channel_id=1, source_target_pairs={{0,4},{2,6},{4,0},{6,2},{8,12},{10,14},{12,8},{14,10},{16,20},{18,... | collective-permute-start | bytes 245768 | tf_op jit(solution)/shard_map/ppermute | solution.py:181
  85.5 2.6 %collective-permute-done.25 = f32[160,128]{1,0:T(8,128)S(1)} collective-permute-done((f32[160,128]{1,0:T(8,128)S(1)}, f32[160,128]{1,0:T(8,128)S(1)}, u32[]{:S(2)}, u32[]{:S(2)}) %collective-permute-start.25) | collective-permute-done | bytes 81952 | tf_op jit(solution)/shard_map/ppermute | solution.py:181
  88.2 1.5 %collective-permute-done.26 = f32[640,128]{1,0:T(8,128)S(1)} collective-permute-done((f32[640,128]{1,0:T(8,128)S(1)}, f32[640,128]{1,0:T(8,128)S(1)}, u32[]{:S(2)}, u32[]{:S(2)}) %collective-permute-start.26) | collective-permute-done | bytes 327712 | tf_op jit(solution)/shard_map/ppermute | solution.py:181
  89.8 17.0 %shard_map.49 = f32[49,7,512]{2,1,0:T(8,128)} custom-call(f32[1280,128]{1,0:T(8,128)S(1)} %bitcast.20, f32[392,512]{1,0:T(8,128)S(1)} %copy-done.1), custom_call_target="tpu_custom_call" | custom-call | flops 134217728 | bytes 1048576 | tf_op jit(solution)/shard_map/pallas_call | solution.py:43
  (62 shorter events, 16.8 us)
Async XLA Ops:
  1.0 11.7 %collective-permute-start = (f32[1,7,7,512]{3,2,1,0:T(8,128)S(1)}, f32[1,7,7,512]{3,2,1,0:T(8,128)S(1)}, u32[]{:S(2)}, u32[]{:S(2)}) collective-permute-start(f32[1,7,7,512]{3,2,1,0:T(8,128)S(1)} %slice.12), channel_id=1, source_target_pairs={{0,30},{2,0},{4,2},{6,4},{8,6},{10,8},{12,10},{14,12},{16,14},{18,... | collective-permute-start | bytes 301064 | tf_op jit(solution)/shard_map/ppermute | solution.py:448
  8.8 3.9 %collective-permute-start.1 = (f32[7,1,7,512]{3,2,1,0:T(8,128)S(1)}, f32[7,1,7,512]{3,2,1,0:T(8,128)S(1)}, u32[]{:S(2)}, u32[]{:S(2)}) collective-permute-start(f32[7,1,7,512]{3,2,1,0:T(8,128)S(1)} %slice.13), channel_id=1, source_target_pairs={{0,1},{1,0},{2,3},{3,2},{4,5},{5,4},{6,7},{7,6},{8,9},{9,8},{10,11... | collective-permute-start | bytes 301064 | tf_op jit(solution)/shard_map/ppermute | solution.py:448
  9.5 3.2 %collective-permute-start.2 = (f32[1,1,7,512]{3,2,1,0:T(8,128)S(1)}, f32[1,1,7,512]{3,2,1,0:T(8,128)S(1)}, u32[]{:S(2)}, u32[]{:S(2)}) collective-permute-start(f32[1,1,7,512]{3,2,1,0:T(8,128)S(1)} %slice.14), channel_id=1, source_target_pairs={{3,0},{2,1},{5,2},{4,3},{7,4},{6,5},{9,6},{8,7},{11,8},{10,9},{13,... | collective-permute-start | bytes 43016 | tf_op jit(solution)/shard_map/ppermute | solution.py:458
  13.3 1.7 %collective-permute-start.3 = (f32[2,8,8,512]{3,2,1,0:T(8,128)S(1)}, f32[2,8,8,512]{3,2,1,0:T(8,128)S(1)}, u32[]{:S(2)}, u32[]{:S(2)}) collective-permute-start(f32[2,8,8,512]{3,2,1,0:T(8,128)S(1)} %get-tuple-element.38), channel_id=1, source_target_pairs={{0,1},{1,0},{2,3},{3,2},{4,5},{5,4},{6,7},{7,6},{8,9},{9,8},{10,11... | collective-permute-start | bytes 786440 | tf_op jit(solution)/shard_map/ppermute | solution.py:448
  15.0 9.4 %collective-permute-start.4 = (f32[8,8,512]{2,1,0:T(8,128)S(1)}, f32[8,8,512]{2,1,0:T(8,128)S(1)}, u32[]{:S(2)}, u32[]{:S(2)}) collective-permute-start(f32[8,8,512]{2,1,0:T(8,128)S(1)} %get-tuple-element.41), channel_id=1, source_target_pairs={{0,2},{2,4},{4,6},{6,8},{8,10},{10,12},{12,14},{14,16},{16,18},{18... | collective-permute-start | bytes 393224 | tf_op jit(solution)/shard_map/ppermute | solution.py:448
  15.9 8.6 %collective-permute-start.5 = (f32[8,8,512]{2,1,0:T(8,128)S(1)}, f32[8,8,512]{2,1,0:T(8,128)S(1)}, u32[]{:S(2)}, u32[]{:S(2)}) collective-permute-start(f32[8,8,512]{2,1,0:T(8,128)S(1)} %get-tuple-element.42), channel_id=1, source_target_pairs={{0,30},{2,0},{4,2},{6,4},{8,6},{10,8},{12,10},{14,12},{16,14},{18,... | collective-permute-start | bytes 393224 | tf_op jit(solution)/shard_map/ppermute | solution.py:448
  25.0 1.6 %collective-permute-start.6 = (f32[2,8,8,512]{3,2,1,0:T(8,128)S(1)}, f32[2,8,8,512]{3,2,1,0:T(8,128)S(1)}, u32[]{:S(2)}, u32[]{:S(2)}) collective-permute-start(f32[2,8,8,512]{3,2,1,0:T(8,128)S(1)} %get-tuple-element.45), channel_id=1, source_target_pairs={{0,1},{1,0},{2,3},{3,2},{4,5},{5,4},{6,7},{7,6},{8,9},{9,8},{10,11... | collective-permute-start | bytes 786440 | tf_op jit(solution)/shard_map/ppermute | solution.py:448
  26.6 9.2 %collective-permute-start.7 = (f32[8,8,512]{2,1,0:T(8,128)S(1)}, f32[8,8,512]{2,1,0:T(8,128)S(1)}, u32[]{:S(2)}, u32[]{:S(2)}) collective-permute-start(f32[8,8,512]{2,1,0:T(8,128)S(1)} %get-tuple-element.48), channel_id=1, source_target_pairs={{0,2},{2,4},{4,6},{6,8},{8,10},{10,12},{12,14},{14,16},{16,18},{18... | collective-permute-start | bytes 393224 | tf_op jit(solution)/shard_map/ppermute | solution.py:448
  26.7 9.1 %collective-permute-start.8 = (f32[8,8,512]{2,1,0:T(8,128)S(1)}, f32[8,8,512]{2,1,0:T(8,128)S(1)}, u32[]{:S(2)}, u32[]{:S(2)}) collective-permute-start(f32[8,8,512]{2,1,0:T(8,128)S(1)} %get-tuple-element.49), channel_id=1, source_target_pairs={{0,30},{2,0},{4,2},{6,4},{8,6},{10,8},{12,10},{14,12},{16,14},{18,... | collective-permute-start | bytes 393224 | tf_op jit(solution)/shard_map/ppermute | solution.py:448
  38.0 9.2 %collective-permute-start.10 = (f32[8,8,512]{2,1,0:T(8,128)S(1)}, f32[8,8,512]{2,1,0:T(8,128)S(1)}, u32[]{:S(2)}, u32[]{:S(2)}) collective-permute-start(f32[8,8,512]{2,1,0:T(8,128)S(1)} %get-tuple-element.55), channel_id=1, source_target_pairs={{0,2},{2,4},{4,6},{6,8},{8,10},{10,12},{12,14},{14,16},{16,18},{18... | collective-permute-start | bytes 393224 | tf_op jit(solution)/shard_map/ppermute | solution.py:448
  38.0 9.2 %collective-permute-start.11 = (f32[8,8,512]{2,1,0:T(8,128)S(1)}, f32[8,8,512]{2,1,0:T(8,128)S(1)}, u32[]{:S(2)}, u32[]{:S(2)}) collective-permute-start(f32[8,8,512]{2,1,0:T(8,128)S(1)} %get-tuple-element.56), channel_id=1, source_target_pairs={{0,30},{2,0},{4,2},{6,4},{8,6},{10,8},{12,10},{14,12},{16,14},{18,... | collective-permute-start | bytes 393224 | tf_op jit(solution)/shard_map/ppermute | solution.py:448
  49.7 9.4 %collective-permute-start.13 = (f32[8,8,512]{2,1,0:T(8,128)S(1)}, f32[8,8,512]{2,1,0:T(8,128)S(1)}, u32[]{:S(2)}, u32[]{:S(2)}) collective-permute-start(f32[8,8,512]{2,1,0:T(8,128)S(1)} %shard_map.45), channel_id=1, source_target_pairs={{0,2},{2,4},{4,6},{6,8},{8,10},{10,12},{12,14},{14,16},{16,18},{18... | collective-permute-start | bytes 393224 | tf_op jit(solution)/shard_map/ppermute | solution.py:448
  62.9 1.8 %collective-permute-start.15 = (f32[640,128]{1,0:T(8,128)}, f32[640,128]{1,0:T(8,128)S(1)}, u32[]{:S(2)}, u32[]{:S(2)}) collective-permute-start(f32[640,128]{1,0:T(8,128)} %get-tuple-element.63), channel_id=1, source_target_pairs={{0,1},{1,0},{2,3},{3,2},{4,5},{5,4},{6,7},{7,6},{8,9},{9,8},{10,11... | collective-permute-start | bytes 983048 | tf_op jit(solution)/shard_map/ppermute | solution.py:181
  64.8 3.6 %collective-permute-start.16 = (f32[160,128]{1,0:T(8,128)S(1)}, f32[160,128]{1,0:T(8,128)S(1)}, u32[]{:S(2)}, u32[]{:S(2)}) collective-permute-start(f32[160,128]{1,0:T(8,128)S(1)} %get-tuple-element.64), channel_id=1, source_target_pairs={{0,0},{2,2},{4,4},{6,6},{8,8},{10,10},{12,12},{14,14},{16,16},{18,... | collective-permute-start | bytes 245768 | tf_op jit(solution)/shard_map/ppermute | solution.py:181
  64.9 5.1 %collective-permute-start.17 = (f32[160,128]{1,0:T(8,128)S(1)}, f32[160,128]{1,0:T(8,128)S(1)}, u32[]{:S(2)}, u32[]{:S(2)}) collective-permute-start(f32[160,128]{1,0:T(8,128)S(1)} %get-tuple-element.65), channel_id=1, source_target_pairs={{0,2},{2,0},{4,6},{6,4},{8,10},{10,8},{12,14},{14,12},{16,18},{18,... | collective-permute-start | bytes 245768 | tf_op jit(solution)/shard_map/ppermute | solution.py:181
  64.9 6.3 %collective-permute-start.18 = (f32[160,128]{1,0:T(8,128)S(1)}, f32[160,128]{1,0:T(8,128)S(1)}, u32[]{:S(2)}, u32[]{:S(2)}) collective-permute-start(f32[160,128]{1,0:T(8,128)S(1)} %get-tuple-element.66), channel_id=1, source_target_pairs={{0,4},{2,6},{4,0},{6,2},{8,12},{10,14},{12,8},{14,10},{16,20},{18,... | collective-permute-start | bytes 245768 | tf_op jit(solution)/shard_map/ppermute | solution.py:181
  65.0 6.2 %collective-permute-start.19 = (f32[160,128]{1,0:T(8,128)S(1)}, f32[160,128]{1,0:T(8,128)S(1)}, u32[]{:S(2)}, u32[]{:S(2)}) collective-permute-start(f32[160,128]{1,0:T(8,128)S(1)} %get-tuple-element.67), channel_id=1, source_target_pairs={{0,6},{2,4},{4,2},{6,0},{8,14},{10,12},{12,10},{14,8},{16,22},{18,... | collective-permute-start | bytes 245768 | tf_op jit(solution)/shard_map/ppermute | solution.py:181
  71.3 4.5 %collective-permute-start.20 = (f32[160,128]{1,0:T(8,128)S(1)}, f32[160,128]{1,0:T(8,128)S(1)}, u32[]{:S(2)}, u32[]{:S(2)}) collective-permute-start(f32[160,128]{1,0:T(8,128)S(1)} %shard_map.48), channel_id=1, source_target_pairs={{0,8},{2,10},{4,12},{6,14},{8,0},{10,2},{12,4},{14,6},{16,24},{18,... | collective-permute-start | bytes 245768 | tf_op jit(solution)/shard_map/ppermute | solution.py:181
  71.4 7.2 %collective-permute-start.21 = (f32[160,128]{1,0:T(8,128)S(1)}, f32[160,128]{1,0:T(8,128)S(1)}, u32[]{:S(2)}, u32[]{:S(2)}) collective-permute-start(f32[160,128]{1,0:T(8,128)S(1)} %shard_map.48), channel_id=1, source_target_pairs={{0,16},{2,18},{4,20},{6,22},{8,24},{10,26},{12,28},{14,30},{16,0},... | collective-permute-start | bytes 245768 | tf_op jit(solution)/shard_map/ppermute | solution.py:181
  73.8 6.3 %collective-permute-start.22 = (f32[160,128]{1,0:T(8,128)S(1)}, f32[160,128]{1,0:T(8,128)S(1)}, u32[]{:S(2)}, u32[]{:S(2)}) collective-permute-start(f32[160,128]{1,0:T(8,128)S(1)} %shard_map.48), channel_id=1, source_target_pairs={{0,24},{2,26},{4,28},{6,30},{8,16},{10,18},{12,20},{14,22},{16,8},... | collective-permute-start | bytes 245768 | tf_op jit(solution)/shard_map/ppermute | solution.py:181
  80.2 4.5 %collective-permute-start.23 = (f32[160,128]{1,0:T(8,128)S(1)}, f32[160,128]{1,0:T(8,128)S(1)}, u32[]{:S(2)}, u32[]{:S(2)}) collective-permute-start(f32[160,128]{1,0:T(8,128)S(1)} %get-tuple-element.70), channel_id=1, source_target_pairs={{0,2},{2,0},{4,6},{6,4},{8,10},{10,8},{12,14},{14,12},{16,18},{18,... | collective-permute-start | bytes 245768 | tf_op jit(solution)/shard_map/ppermute | solution.py:181
  81.0 4.4 %collective-permute-start.24 = (f32[160,128]{1,0:T(8,128)S(1)}, f32[160,128]{1,0:T(8,128)S(1)}, u32[]{:S(2)}, u32[]{:S(2)}) collective-permute-start(f32[160,128]{1,0:T(8,128)S(1)} %get-tuple-element.70), channel_id=1, source_target_pairs={{0,4},{2,6},{4,0},{6,2},{8,12},{10,14},{12,8},{14,10},{16,20},{18,... | collective-permute-start | bytes 245768 | tf_op jit(solution)/shard_map/ppermute | solution.py:181
  82.7 5.3 %collective-permute-start.25 = (f32[160,128]{1,0:T(8,128)S(1)}, f32[160,128]{1,0:T(8,128)S(1)}, u32[]{:S(2)}, u32[]{:S(2)}) collective-permute-start(f32[160,128]{1,0:T(8,128)S(1)} %get-tuple-element.70), channel_id=1, source_target_pairs={{0,6},{2,4},{4,2},{6,0},{8,14},{10,12},{12,10},{14,8},{16,22},{18,... | collective-permute-start | bytes 245768 | tf_op jit(solution)/shard_map/ppermute | solution.py:181
  88.0 1.7 %collective-permute-start.26 = (f32[640,128]{1,0:T(8,128)S(1)}, f32[640,128]{1,0:T(8,128)S(1)}, u32[]{:S(2)}, u32[]{:S(2)}) collective-permute-start(f32[640,128]{1,0:T(8,128)S(1)} %bitcast.22), channel_id=1, source_target_pairs={{0,1},{1,0},{2,3},{3,2},{4,5},{5,4},{6,7},{7,6},{8,9},{9,8},{10,11... | collective-permute-start | bytes 983048 | tf_op jit(solution)/shard_map/ppermute | solution.py:181
  (6 other events, 18.3 us)

commit v4 on v3

--- a/solution.py
+++ b/solution.py
@@ -11,11 +11,8 @@
 SUB = 8
 LANES = 128
 SLAB = 16
-STRIP = 256
 PARTS = 1
 VMEM_LIMIT = 6 << 20
-LAST_LIMIT = 6 << 20
-ORTHO_LIMIT = 6 << 20
 
 
 band_low = 4.0
@@ -23,7 +20,7 @@
 anchor = 0.0
 
 
-def vmem_call(body, out_shapes, scratch=(), flops=0, scalars=0, hbm_in=(), hbm_out=(), limit=VMEM_LIMIT):
+def vmem_call(body, out_shapes, scratch=(), flops=0, scalars=0, hbm_in=(), hbm_out=()):
     def spec(in_hbm):
         return pl.BlockSpec(memory_space=pltpu.HBM if in_hbm else pltpu.VMEM)
 
@@ -47,7 +44,7 @@
             + [spec(n in hbm_in) for n in range(scalars, len(operands))],
             out_specs=tuple(spec(n in hbm_out) for n in range(len(out_shapes))),
             scratch_shapes=list(scratch),
-            compiler_params=pltpu.CompilerParams(vmem_limit_bytes=limit),
+            compiler_params=pltpu.CompilerParams(vmem_limit_bytes=VMEM_LIMIT),
             cost_estimate=pl.CostEstimate(
                 flops=flops, bytes_accessed=1 << 20, transcendentals=0
             ),
@@ -116,11 +113,15 @@
     *planes, y_faces = refs[: len(refs) // 2 + 1]
     outs = refs[len(refs) // 2 + 1 :]
     edge = planes[0].shape[0]
+    order_now = edge - 1
     for plane, out, at in zip(planes, outs, (edge - 1, 0)):
-        out[...] = plane[...]
-        out[0] = out[0] + y_faces[0, at]
-        if y_faces.shape[0] > 1:
-            out[edge - 1] = out[edge - 1] + y_faces[1, at]
+        for b in range(edge):
+            row = plane[b]
+            if b == 0:
+                row = row + y_faces[0, at]
+            if b == edge - 1 and y_faces.shape[0] > 1:
+                row = row + y_faces[1, at]
+            out[order_now * b : order_now * (b + 1)] = row[:order_now]
 
 
 def updated(image, y_faces, x_low, x_high, current, previous, alpha, beta):
@@ -129,9 +130,13 @@
     image[:, 0] = image[:, 0] + y_faces[0]
     if y_faces.shape[0] > 1:
         image[:, edge - 1] = image[:, edge - 1] + y_faces[1]
-    image[0] = image[0] + x_low[...]
-    if x_high is not None:
-        image[edge - 1] = image[edge - 1] + x_high[...]
+    order_now = edge - 1
+    for at, got in ((0, x_low), (edge - 1, x_high)):
+        if got is not None:
+            for b in range(edge):
+                first = order_now * b
+                image[at, b, :order_now] += got[first : first + order_now]
+                image[at, b, order_now:] += got[first : first + 1]
     got = (image[...] - center * current[...]) * alpha
     if previous is not None:
         got = got - beta * previous[...]
@@ -150,8 +155,50 @@
     cell_product(got, matrix, *sums)
 
 
-def last_body(mine, image_in, y_face, x_low, current, previous, own, *refs, alpha, beta):
-    *parts, corr, work, values, sem = refs
+def block_places(count, half_rows):
+    pairs = [(i, j) for i in range(count) for j in range(i, count)]
+    size = -(-len(pairs) // 2)
+    return {
+        pair: n // size * half_rows + n % size * LANES for n, pair in enumerate(pairs)
+    }
+
+
+def half_correlation(which, values, out):
+    width = values.shape[1]
+    half_rows = out.shape[0]
+    high = values.astype(jnp.bfloat16)
+    low = (values - high.astype(jnp.float32)).astype(jnp.bfloat16)
+
+    def product(a, b):
+        return lax.dot_general(
+            a, b, (((0,), (0,)), ((), ())), preferred_element_type=jnp.float32
+        )
+
+    strips = {}
+    for (i, j), at in block_places(width // LANES, half_rows).items():
+        if at // half_rows == which:
+            strips.setdefault(i, []).append((j, at - which * half_rows))
+    for i, found in strips.items():
+        rows = slice(i * LANES, (i + 1) * LANES)
+        cols = slice(found[0][0] * LANES, (found[-1][0] + 1) * LANES)
+        strip = (
+            product(high[:, rows], low[:, cols]) + product(low[:, rows], high[:, cols])
+        ) + product(high[:, rows], high[:, cols])
+        for n, (_, at) in enumerate(found):
+            out[at : at + LANES] = strip[:, n * LANES : (n + 1) * LANES]
+
+
+def chosen_half(number, values, out):
+    for which in range(2):
+
+        @pl.when(number == which)
+        def _():
+            half_correlation(which, values[...], out)
+
+
+def last_body(
+    mine, image_in, y_face, x_low, current, previous, stored, other, work, own, sem, *, alpha, beta
+):
     edge = image_in.shape[0]
     width = image_in.shape[3]
     work[...] = image_in[...]
@@ -159,21 +206,18 @@
     got = got[: edge - 1, : edge - 1]
     where = lax.broadcasted_iota(jnp.int32, got.shape, 2)
     got = jnp.where(where == edge - 1, 0.0, got)
-    flat = got.reshape((edge - 1) ** 2 * edge, width)
-    values[...] = flat
-    keep = pltpu.make_async_copy(values, own, sem)
+    own[...] = got.reshape((edge - 1) ** 2 * edge, width)
+    keep = pltpu.make_async_copy(own, stored, sem)
     keep.start()
-    at = 0
-    for i in range(0, width, STRIP):
-        strip = exact_dot(flat[:, i : i + STRIP], flat[:, i:], ((0,), (0,)))
-        for first in range(0, STRIP, LANES):
-            for j in range(first, width - i, LANES):
-                corr[at : at + LANES] = strip[first : first + LANES, j : j + LANES]
-                at += LANES
-    rows = parts[0].shape[0]
-    for d, part in enumerate(parts):
-        part[...] = corr[pl.ds(pl.multiple_of((mine[0] ^ d) * rows, SUB), rows)]
+    chosen_half(1 - mine[0], own, other)
     keep.wait()
+
+
+def kept_body(mine, stored, half, own, sem):
+    load = pltpu.make_async_copy(stored, own, sem)
+    load.start()
+    load.wait()
+    chosen_half(mine[0], own, half)
 
 
 def swap(block, axis, distance):
@@ -184,7 +228,8 @@
 def stages_of(axis, size):
     stages, stride = [], 1
     while stride < size:
-        radix = 4 if size // stride >= 4 else 2
+        radix = 2 if axis == "narrow" and stride == 1 else 4
+        radix = min(radix, size // stride)
         stages.append((axis, stride, radix))
         stride *= radix
     return stages
@@ -219,12 +264,15 @@
     return (lax.axis_index(axis) // stride % radix).astype(jnp.int32)[None]
 
 
-def summed(parts):
-    lanes = parts[0].shape[1]
+def summed(kept, other):
+    lanes = kept.shape[1]
     stages = all_stages()
+    parts = [kept, other]
     for stage, after in zip(stages[:-1], stages[1:]):
         axis, stride, _ = stage
-        terms = [swap(part, axis, d * stride) for d, part in enumerate(parts)]
+        terms = [parts[0]] + [
+            swap(part, axis, d * stride) for d, part in enumerate(parts[1:], 1)
+        ]
         rows, radix = terms[0].shape[0], after[2]
         if after == stages[-1]:
             radix = 1
@@ -351,7 +399,7 @@
     yield jnp.concatenate(done, axis=0)
 
 
-def ortho_body(corr, own, out, blocks, rest, done, sent, sems, *, scale):
+def ortho_body(corr, own, out, blocks, rest, done, sent, sems, *, root_nodes):
     width = own.shape[1]
     count = width // LANES
     nodes = own.shape[0]
@@ -372,20 +420,29 @@
             work.pop(0)()
         return got
 
-    place, at = {}, 0
+    rows_of = block_places(count, corr.shape[0] // 2)
+    place = {pair: n for n, pair in enumerate(rows_of)}
+
+    on_diagonal = lax.broadcasted_iota(
+        jnp.int32, (LANES, LANES), 0
+    ) == lax.broadcasted_iota(jnp.int32, (LANES, LANES), 1)
+    over_row, over_col = [], []
     for i in range(count):
-        for j in range(i, count):
-            place[i, j] = at
-            at += 1
+        at = rows_of[i, i]
+        kept = jnp.where(on_diagonal, corr[at : at + LANES], 0.0)
+        over_row.append(lax.rsqrt(jnp.sum(kept, axis=1, keepdims=True)))
+        over_col.append(lax.rsqrt(jnp.sum(kept, axis=0, keepdims=True)))
 
     def piece(i, j):
-        return corr[place[i, j] * LANES : (place[i, j] + 1) * LANES] * scale
+        at = rows_of[i, j]
+        return corr[at : at + LANES] * over_row[i] * over_col[j]
 
     def set_up():
         for (i, j), n in place.items():
             if j > 0:
                 blocks[n] = piece(i, j)
-        rest[...] = own[...]
+        for j in range(count):
+            rest[:, span(j)] = own[:, span(j)] * (over_col[j] * root_nodes)
 
     def store(k):
         return pltpu.make_async_copy(sent.at[k], out.at[:, :, span(k)], sems.at[k])
@@ -471,7 +528,7 @@
     edge = order_now + 1
     width = orbitals.shape[3]
     box = f32(edge, edge, edge, width)
-    plane = f32(edge, edge, width)
+    plane, sent = f32(edge, edge, width), f32(edge * order_now, width)
     sums = (box, plane, plane, f32(2, edge, edge, width))
     cell_nodes = edge**3
     (matrix,) = vmem_call(
@@ -497,11 +554,11 @@
     alpha, beta, previous = sigma_now / half_width, None, None
     for degree_step in range(1, DEG):
         y_faces = y_exchange(y_sent)
-        x_last, x_first = vmem_call(edge_body, (plane, plane))(
+        x_last, x_first = vmem_call(edge_body, (sent, sent))(
             x_last, x_first, y_faces
         )
+        x_high = to_next(x_first, "wide", -1)
         x_low = to_next(x_last, "wide", 1)
-        x_high = to_next(x_first, "wide", -1)
         operands = [image, y_faces, x_low, x_high, current]
         if previous is not None:
             operands.append(previous)
@@ -517,43 +574,53 @@
         sigma_now = sigma_new
 
     y_low = to_next(y_sent[:1], "narrow", 1)
-    (x_last,) = vmem_call(edge_body, (plane,))(x_last, y_low)
+    (x_last,) = vmem_call(edge_body, (sent,))(x_last, y_low)
     x_low = to_next(x_last, "wide", 1)
     blocks = width // LANES
     rows = cut_rows(blocks * (blocks + 1) // 2 * LANES)
     first_stage = all_stages()[0]
-    radix = first_stage[2]
-    own, *parts = vmem_call(
+    assert first_stage[2] == 2
+    block_shape, half_shape = f32(order_now**2 * edge, width), f32(rows // 2, LANES)
+    half_flops = 3 * cell_nodes * width**2
+    stored, other = vmem_call(
         functools.partial(last_body, alpha=alpha, beta=beta),
-        (f32(order_now**2 * edge, width),) + (f32(rows // radix, LANES),) * radix,
+        (block_shape, half_shape),
         scratch=[
-            pltpu.VMEM((rows, LANES), jnp.float32),
             pltpu.VMEM(box.shape, jnp.float32),
-            pltpu.VMEM((order_now**2 * edge, width), jnp.float32),
+            pltpu.VMEM(block_shape.shape, jnp.float32),
             pltpu.SemaphoreType.DMA,
         ],
-        flops=2 * cell_nodes * width**2,
+        flops=half_flops,
+        scalars=1,
         hbm_out=(0,),
+    )(digit(first_stage), image, y_low, x_low, current, previous)
+    (kept,) = vmem_call(
+        kept_body,
+        (half_shape,),
+        scratch=[
+            pltpu.VMEM(block_shape.shape, jnp.float32),
+            pltpu.SemaphoreType.DMA,
+        ],
+        flops=half_flops,
         scalars=1,
-        limit=LAST_LIMIT,
-    )(digit(first_stage), image, y_low, x_low, current, previous)
+        hbm_in=(1,),
+    )(digit(first_stage), stored)
 
     nodes = order_now**3 * lax.axis_size("wide") * lax.axis_size("narrow")
-    corr = summed(parts)
+    corr = summed(kept, other)
     (out,) = vmem_call(
-        functools.partial(ortho_body, scale=1.0 / nodes),
+        functools.partial(ortho_body, root_nodes=nodes**0.5),
         (f32(order_now**2, order_now, width),),
         scratch=[
-            pltpu.VMEM((corr.shape[0] // LANES, LANES, LANES), jnp.float32),
-            pltpu.VMEM(own.shape, jnp.float32),
-            pltpu.VMEM((own.shape[0], LANES), jnp.float32),
+            pltpu.VMEM((blocks * (blocks + 1) // 2, LANES, LANES), jnp.float32),
+            pltpu.VMEM(block_shape.shape, jnp.float32),
+            pltpu.VMEM((block_shape.shape[0], LANES), jnp.float32),
             pltpu.VMEM((blocks, order_now**2, order_now, LANES), jnp.float32),
             pltpu.SemaphoreType.DMA((blocks,)),
         ],
         flops=width**3,
-        limit=ORTHO_LIMIT,
         hbm_out=(0,),
-    )(corr, own)
+    )(corr, stored)
     return out.reshape(orbitals.shape)
 
 

time: 107 us -> 105 us (0.981)
  waiting for transfers between devices: 41.1 us -> 38.2 us
  Pallas kernels: 23.5 us -> 25.1 us
  starting transfers between devices: 38.2 us -> 37.1 us
    pallas_call x13 -> x14, Pallas kernels: 23.5 us -> 25.1 us  [call(): pl.pallas_call(body, out_shape=outs, in_specs=[pl.BlockSpec(memory_space=...]
    ppermute x13 -> x11, waiting for transfers between devices: 14.8 us -> 13.3 us  [swap(): return lax.ppermute(block, axis, [(i, i ^ distance) for i in range(count)])]
    ppermute x13, waiting for transfers between devices: 25.6 us -> 24.2 us  [to_next(): lax.ppermute(block, axis, [(i, (i + distance) % count) for i in range(cou...]
    ppermute x13 -> x11, starting transfers between devices: 12.6 us -> 11.7 us  [swap(): return lax.ppermute(block, axis, [(i, i ^ distance) for i in range(count)])]
  transfers between devices with their start and end apart: 27 -> 25, of which waited for: 19 -> 17; matrix products, arithmetic and copies ran while one was open for 2% -> 2% of each run, Pallas kernels for 1% -> 3%
where the time goes in v4:
time: 105 us
  waiting for transfers between devices  38.2 us (36%)
  starting transfers between devices  37.1 us (35%)
  Pallas kernels  25.1 us (24%)
  local copies, waits for them, and re-layouts  3.59 us (3%)
    pallas_call x14, Pallas kernels, call(): pl.pallas_call(body, out_shape=outs, in_specs=[pl.BlockSpec(memory_space=...  25.1 us
    ppermute x13, starting transfers between devices, to_next(): lax.ppermute(block, axis, [(i, (i + distance) % count) for i in range(cou...  24.8 us
    ppermute x13, waiting for transfers between devices, to_next(): lax.ppermute(block, axis, [(i, (i + distance) % count) for i in range(cou...  24.2 us
    ppermute x11, waiting for transfers between devices, swap(): return lax.ppermute(block, axis, [(i, i ^ distance) for i in range(count)])  13.3 us
    ppermute x11, starting transfers between devices, swap(): return lax.ppermute(block, axis, [(i, i ^ distance) for i in range(count)])  11.7 us
  transfers between devices with their start and end apart: 25, of which 17 were waited for; matrix products, arithmetic and copies ran while one was open for 2% of the time, Pallas kernels for 3%

profile of v4, /device:TPU:0, one launch (start us, length us, event | category | flops | bytes accessed | tf_op | source)
XLA Modules:
  0.0 104.6 jit_solution(7547622079923681358)
XLA Ops:
  1.0 6.9 %collective-permute-start = (f32[1,7,7,512]{3,2,1,0:T(8,128)S(1)}, f32[1,7,7,512]{3,2,1,0:T(8,128)S(1)}, u32[]{:S(2)}, u32[]{:S(2)}) collective-permute-start(f32[1,7,7,512]{3,2,1,0:T(8,128)S(1)} %slice.12), channel_id=1, source_target_pairs={{0,30},{2,0},{4,2},{6,4},{8,6},{10,8},{12,10},{14,12},{16,14},{18,... | collective-permute-start | bytes 301064 | tf_op jit(solution)/shard_map/ppermute | solution.py:505
  15.9 4.8 %collective-permute-start.5 = (f32[56,512]{1,0:T(8,128)S(1)}, f32[56,512]{1,0:T(8,128)S(1)}, u32[]{:S(2)}, u32[]{:S(2)}) collective-permute-start(f32[56,512]{1,0:T(8,128)S(1)} %get-tuple-element.41), channel_id=1, source_target_pairs={{0,30},{2,0},{4,2},{6,4},{8,6},{10,8},{12,10},{14,12},{16,14},{18,... | collective-permute-start | bytes 344072 | tf_op jit(solution)/shard_map/ppermute | solution.py:505
  20.7 3.4 %collective-permute-done.4.refs_2_ = f32[56,512]{1,0:T(8,128)S(1)} collective-permute-done((f32[56,512]{1,0:T(8,128)S(1)}, f32[56,512]{1,0:T(8,128)S(1)}, u32[]{:S(2)}, u32[]{:S(2)}) %collective-permute-start.4) | collective-permute-done | bytes 114720 | tf_op jit(solution)/shard_map/ppermute | solution.py:505
  24.8 1.5 %collective-permute-done.6.refs_2_.refs_1_ = f32[2,8,8,512]{3,2,1,0:T(8,128)S(1)} collective-permute-done((f32[2,8,8,512]{3,2,1,0:T(8,128)S(1)}, f32[2,8,8,512]{3,2,1,0:T(8,128)S(1)}, u32[]{:S(2)}, u32[]{:S(2)}) %collective-permute-start.6) | collective-permute-done | bytes 262176 | tf_op jit(solution)/shard_map/ppermute | solution.py:505
  26.4 5.6 %collective-permute-start.8 = (f32[56,512]{1,0:T(8,128)S(1)}, f32[56,512]{1,0:T(8,128)S(1)}, u32[]{:S(2)}, u32[]{:S(2)}) collective-permute-start(f32[56,512]{1,0:T(8,128)S(1)} %get-tuple-element.48), channel_id=1, source_target_pairs={{0,30},{2,0},{4,2},{6,4},{8,6},{10,8},{12,10},{14,12},{16,14},{18,... | collective-permute-start | bytes 344072 | tf_op jit(solution)/shard_map/ppermute | solution.py:505
  32.0 3.2 %collective-permute-done.7.refs_2_ = f32[56,512]{1,0:T(8,128)S(1)} collective-permute-done((f32[56,512]{1,0:T(8,128)S(1)}, f32[56,512]{1,0:T(8,128)S(1)}, u32[]{:S(2)}, u32[]{:S(2)}) %collective-permute-start.7) | collective-permute-done | bytes 114720 | tf_op jit(solution)/shard_map/ppermute | solution.py:505
  35.9 1.5 %collective-permute-done.9.refs_2_.refs_1_ = f32[2,8,8,512]{3,2,1,0:T(8,128)S(1)} collective-permute-done((f32[2,8,8,512]{3,2,1,0:T(8,128)S(1)}, f32[2,8,8,512]{3,2,1,0:T(8,128)S(1)}, u32[]{:S(2)}, u32[]{:S(2)}) %collective-permute-start.9) | collective-permute-done | bytes 262176 | tf_op jit(solution)/shard_map/ppermute | solution.py:505
  37.5 5.6 %collective-permute-start.11 = (f32[56,512]{1,0:T(8,128)S(1)}, f32[56,512]{1,0:T(8,128)S(1)}, u32[]{:S(2)}, u32[]{:S(2)}) collective-permute-start(f32[56,512]{1,0:T(8,128)S(1)} %get-tuple-element.55), channel_id=1, source_target_pairs={{0,30},{2,0},{4,2},{6,4},{8,6},{10,8},{12,10},{14,12},{16,14},{18,... | collective-permute-start | bytes 344072 | tf_op jit(solution)/shard_map/ppermute | solution.py:505
  43.1 3.2 %collective-permute-done.10.refs_2_ = f32[56,512]{1,0:T(8,128)S(1)} collective-permute-done((f32[56,512]{1,0:T(8,128)S(1)}, f32[56,512]{1,0:T(8,128)S(1)}, u32[]{:S(2)}, u32[]{:S(2)}) %collective-permute-start.10) | collective-permute-done | bytes 114720 | tf_op jit(solution)/shard_map/ppermute | solution.py:505
  49.1 8.8 %collective-permute-done.13.x_low = f32[56,512]{1,0:T(8,128)S(1)} collective-permute-done((f32[56,512]{1,0:T(8,128)S(1)}, f32[56,512]{1,0:T(8,128)S(1)}, u32[]{:S(2)}, u32[]{:S(2)}) %collective-permute-start.13) | collective-permute-done | bytes 114720 | tf_op jit(solution)/shard_map/ppermute | solution.py:505
  57.9 2.0 %shard_map.46 = (f32[392,512]{1,0:T(8,128)}, f32[640,128]{1,0:T(8,128)}) custom-call(s32[1]{0:T(128)} %bitcast.1.mine, f32[8,8,8,512]{3,2,1,0:T(8,128)S(1)} %get-tuple-element.57.image_in, f32[1,8,8,512]{3,2,1,0:T(8,128)S(1)} %collective-permute-done.12.refs_1_.y_face, f32[56,512]{1,0:T(8,128)S(1)} %collective-permute-done.13.x_low, ...), custom_call_target="tpu_custom_call" | custom-call | flops 402653184 | bytes 1048576 | tf_op jit(solution)/shard_map/pallas_call | solution.py:40
  60.1 1.8 %shard_map.47.refs_0_ = f32[640,128]{1,0:T(8,128)S(1)} custom-call(s32[1]{0:T(128)} %bitcast.1.mine, f32[392,512]{1,0:T(8,128)} %get-tuple-element.61.stored.own), custom_call_target="tpu_custom_call" | custom-call | flops 402653184 | bytes 1048576 | tf_op jit(solution)/shard_map/pallas_call | solution.py:40
  62.2 3.4 %collective-permute-start.17 = (f32[160,128]{1,0:T(8,128)S(1)}, f32[160,128]{1,0:T(8,128)S(1)}, u32[]{:S(2)}, u32[]{:S(2)}) collective-permute-start(f32[160,128]{1,0:T(8,128)S(1)} %get-tuple-element.66), channel_id=1, source_target_pairs={{0,6},{2,4},{4,2},{6,0},{8,14},{10,12},{12,10},{14,8},{16,22},{18,... | collective-permute-start | bytes 245768 | tf_op jit(solution)/shard_map/ppermute | solution.py:225
  65.6 1.8 %collective-permute-done.15.refs_1_ = f32[160,128]{1,0:T(8,128)S(1)} collective-permute-done((f32[160,128]{1,0:T(8,128)S(1)}, f32[160,128]{1,0:T(8,128)S(1)}, u32[]{:S(2)}, u32[]{:S(2)}) %collective-permute-start.15) | collective-permute-done | bytes 81952 | tf_op jit(solution)/shard_map/ppermute | solution.py:225
  67.3 1.4 %collective-permute-done.16.refs_2_ = f32[160,128]{1,0:T(8,128)S(1)} collective-permute-done((f32[160,128]{1,0:T(8,128)S(1)}, f32[160,128]{1,0:T(8,128)S(1)}, u32[]{:S(2)}, u32[]{:S(2)}) %collective-permute-start.16) | collective-permute-done | bytes 81952 | tf_op jit(solution)/shard_map/ppermute | solution.py:225
  68.8 2.1 %collective-permute-start.19 = (f32[160,128]{1,0:T(8,128)S(1)}, f32[160,128]{1,0:T(8,128)S(1)}, u32[]{:S(2)}, u32[]{:S(2)}) collective-permute-start(f32[160,128]{1,0:T(8,128)S(1)} %shard_map.49), channel_id=1, source_target_pairs={{0,16},{2,18},{4,20},{6,22},{8,24},{10,26},{12,28},{14,30},{16,0},... | collective-permute-start | bytes 245768 | tf_op jit(solution)/shard_map/ppermute | solution.py:225
  70.9 2.3 %collective-permute-start.20 = (f32[160,128]{1,0:T(8,128)S(1)}, f32[160,128]{1,0:T(8,128)S(1)}, u32[]{:S(2)}, u32[]{:S(2)}) collective-permute-start(f32[160,128]{1,0:T(8,128)S(1)} %shard_map.49), channel_id=1, source_target_pairs={{0,24},{2,26},{4,28},{6,30},{8,16},{10,18},{12,20},{14,22},{16,8},... | collective-permute-start | bytes 245768 | tf_op jit(solution)/shard_map/ppermute | solution.py:225
  73.8 4.4 %collective-permute-done.19 = f32[160,128]{1,0:T(8,128)S(1)} collective-permute-done((f32[160,128]{1,0:T(8,128)S(1)}, f32[160,128]{1,0:T(8,128)S(1)}, u32[]{:S(2)}, u32[]{:S(2)}) %collective-permute-start.19) | collective-permute-done | bytes 81952 | tf_op jit(solution)/shard_map/ppermute | solution.py:225
  78.3 1.4 %collective-permute-start.21 = (f32[160,128]{1,0:T(8,128)S(1)}, f32[160,128]{1,0:T(8,128)S(1)}, u32[]{:S(2)}, u32[]{:S(2)}) collective-permute-start(f32[160,128]{1,0:T(8,128)S(1)} %get-tuple-element.68), channel_id=1, source_target_pairs={{0,2},{2,0},{4,6},{6,4},{8,10},{10,8},{12,14},{14,12},{16,18},{18,... | collective-permute-start | bytes 245768 | tf_op jit(solution)/shard_map/ppermute | solution.py:225
  80.2 1.7 %collective-permute-start.23 = (f32[160,128]{1,0:T(8,128)S(1)}, f32[160,128]{1,0:T(8,128)S(1)}, u32[]{:S(2)}, u32[]{:S(2)}) collective-permute-start(f32[160,128]{1,0:T(8,128)S(1)} %get-tuple-element.68), channel_id=1, source_target_pairs={{0,6},{2,4},{4,2},{6,0},{8,14},{10,12},{12,10},{14,8},{16,22},{18,... | collective-permute-start | bytes 245768 | tf_op jit(solution)/shard_map/ppermute | solution.py:225
  82.8 1.3 %collective-permute-done.22 = f32[160,128]{1,0:T(8,128)S(1)} collective-permute-done((f32[160,128]{1,0:T(8,128)S(1)}, f32[160,128]{1,0:T(8,128)S(1)}, u32[]{:S(2)}, u32[]{:S(2)}) %collective-permute-start.22) | collective-permute-done | bytes 81952 | tf_op jit(solution)/shard_map/ppermute | solution.py:225
  84.2 1.3 %collective-permute-done.23 = f32[160,128]{1,0:T(8,128)S(1)} collective-permute-done((f32[160,128]{1,0:T(8,128)S(1)}, f32[160,128]{1,0:T(8,128)S(1)}, u32[]{:S(2)}, u32[]{:S(2)}) %collective-permute-start.23) | collective-permute-done | bytes 81952 | tf_op jit(solution)/shard_map/ppermute | solution.py:225
  85.7 1.5 %collective-permute-done.24 = f32[640,128]{1,0:T(8,128)S(1)} collective-permute-done((f32[640,128]{1,0:T(8,128)S(1)}, f32[640,128]{1,0:T(8,128)S(1)}, u32[]{:S(2)}, u32[]{:S(2)}) %collective-permute-start.24) | collective-permute-done | bytes 327712 | tf_op jit(solution)/shard_map/ppermute | solution.py:225
  87.3 17.1 %shard_map.50 = f32[49,7,512]{2,1,0:T(8,128)} custom-call(f32[1280,128]{1,0:T(8,128)S(1)} %bitcast.20, f32[392,512]{1,0:T(8,128)S(1)} %copy-done.1), custom_call_target="tpu_custom_call" | custom-call | flops 134217728 | bytes 1048576 | tf_op jit(solution)/shard_map/pallas_call | solution.py:40
  (59 shorter events, 15.8 us)
Async XLA Ops:
  1.0 11.7 %collective-permute-start = (f32[1,7,7,512]{3,2,1,0:T(8,128)S(1)}, f32[1,7,7,512]{3,2,1,0:T(8,128)S(1)}, u32[]{:S(2)}, u32[]{:S(2)}) collective-permute-start(f32[1,7,7,512]{3,2,1,0:T(8,128)S(1)} %slice.12), channel_id=1, source_target_pairs={{0,30},{2,0},{4,2},{6,4},{8,6},{10,8},{12,10},{14,12},{16,14},{18,... | collective-permute-start | bytes 301064 | tf_op jit(solution)/shard_map/ppermute | solution.py:505
  8.8 3.9 %collective-permute-start.1 = (f32[7,1,7,512]{3,2,1,0:T(8,128)S(1)}, f32[7,1,7,512]{3,2,1,0:T(8,128)S(1)}, u32[]{:S(2)}, u32[]{:S(2)}) collective-permute-start(f32[7,1,7,512]{3,2,1,0:T(8,128)S(1)} %slice.13), channel_id=1, source_target_pairs={{0,1},{1,0},{2,3},{3,2},{4,5},{5,4},{6,7},{7,6},{8,9},{9,8},{10,11... | collective-permute-start | bytes 301064 | tf_op jit(solution)/shard_map/ppermute | solution.py:505
  9.5 3.2 %collective-permute-start.2 = (f32[1,1,7,512]{3,2,1,0:T(8,128)S(1)}, f32[1,1,7,512]{3,2,1,0:T(8,128)S(1)}, u32[]{:S(2)}, u32[]{:S(2)}) collective-permute-start(f32[1,1,7,512]{3,2,1,0:T(8,128)S(1)} %slice.14), channel_id=1, source_target_pairs={{3,0},{2,1},{5,2},{4,3},{7,4},{6,5},{9,6},{8,7},{11,8},{10,9},{13,... | collective-permute-start | bytes 43016 | tf_op jit(solution)/shard_map/ppermute | solution.py:515
  13.3 1.7 %collective-permute-start.3 = (f32[2,8,8,512]{3,2,1,0:T(8,128)S(1)}, f32[2,8,8,512]{3,2,1,0:T(8,128)S(1)}, u32[]{:S(2)}, u32[]{:S(2)}) collective-permute-start(f32[2,8,8,512]{3,2,1,0:T(8,128)S(1)} %get-tuple-element.37), channel_id=1, source_target_pairs={{0,1},{1,0},{2,3},{3,2},{4,5},{5,4},{6,7},{7,6},{8,9},{9,8},{10,11... | collective-permute-start | bytes 786440 | tf_op jit(solution)/shard_map/ppermute | solution.py:505
  15.0 9.1 %collective-permute-start.4 = (f32[56,512]{1,0:T(8,128)S(1)}, f32[56,512]{1,0:T(8,128)S(1)}, u32[]{:S(2)}, u32[]{:S(2)}) collective-permute-start(f32[56,512]{1,0:T(8,128)S(1)} %get-tuple-element.40), channel_id=1, source_target_pairs={{0,2},{2,4},{4,6},{6,8},{8,10},{10,12},{12,14},{14,16},{16,18},{18... | collective-permute-start | bytes 344072 | tf_op jit(solution)/shard_map/ppermute | solution.py:505
  15.9 8.2 %collective-permute-start.5 = (f32[56,512]{1,0:T(8,128)S(1)}, f32[56,512]{1,0:T(8,128)S(1)}, u32[]{:S(2)}, u32[]{:S(2)}) collective-permute-start(f32[56,512]{1,0:T(8,128)S(1)} %get-tuple-element.41), channel_id=1, source_target_pairs={{0,30},{2,0},{4,2},{6,4},{8,6},{10,8},{12,10},{14,12},{16,14},{18,... | collective-permute-start | bytes 344072 | tf_op jit(solution)/shard_map/ppermute | solution.py:505
  24.7 1.6 %collective-permute-start.6 = (f32[2,8,8,512]{3,2,1,0:T(8,128)S(1)}, f32[2,8,8,512]{3,2,1,0:T(8,128)S(1)}, u32[]{:S(2)}, u32[]{:S(2)}) collective-permute-start(f32[2,8,8,512]{3,2,1,0:T(8,128)S(1)} %get-tuple-element.44), channel_id=1, source_target_pairs={{0,1},{1,0},{2,3},{3,2},{4,5},{5,4},{6,7},{7,6},{8,9},{9,8},{10,11... | collective-permute-start | bytes 786440 | tf_op jit(solution)/shard_map/ppermute | solution.py:505
  26.3 8.8 %collective-permute-start.7 = (f32[56,512]{1,0:T(8,128)S(1)}, f32[56,512]{1,0:T(8,128)S(1)}, u32[]{:S(2)}, u32[]{:S(2)}) collective-permute-start(f32[56,512]{1,0:T(8,128)S(1)} %get-tuple-element.47), channel_id=1, source_target_pairs={{0,2},{2,4},{4,6},{6,8},{8,10},{10,12},{12,14},{14,16},{16,18},{18... | collective-permute-start | bytes 344072 | tf_op jit(solution)/shard_map/ppermute | solution.py:505
  26.4 8.8 %collective-permute-start.8 = (f32[56,512]{1,0:T(8,128)S(1)}, f32[56,512]{1,0:T(8,128)S(1)}, u32[]{:S(2)}, u32[]{:S(2)}) collective-permute-start(f32[56,512]{1,0:T(8,128)S(1)} %get-tuple-element.48), channel_id=1, source_target_pairs={{0,30},{2,0},{4,2},{6,4},{8,6},{10,8},{12,10},{14,12},{16,14},{18,... | collective-permute-start | bytes 344072 | tf_op jit(solution)/shard_map/ppermute | solution.py:505
  35.8 1.6 %collective-permute-start.9 = (f32[2,8,8,512]{3,2,1,0:T(8,128)S(1)}, f32[2,8,8,512]{3,2,1,0:T(8,128)S(1)}, u32[]{:S(2)}, u32[]{:S(2)}) collective-permute-start(f32[2,8,8,512]{3,2,1,0:T(8,128)S(1)} %get-tuple-element.51), channel_id=1, source_target_pairs={{0,1},{1,0},{2,3},{3,2},{4,5},{5,4},{6,7},{7,6},{8,9},{9,8},{10,11... | collective-permute-start | bytes 786440 | tf_op jit(solution)/shard_map/ppermute | solution.py:505
  37.5 8.9 %collective-permute-start.10 = (f32[56,512]{1,0:T(8,128)S(1)}, f32[56,512]{1,0:T(8,128)S(1)}, u32[]{:S(2)}, u32[]{:S(2)}) collective-permute-start(f32[56,512]{1,0:T(8,128)S(1)} %get-tuple-element.54), channel_id=1, source_target_pairs={{0,2},{2,4},{4,6},{6,8},{8,10},{10,12},{12,14},{14,16},{16,18},{18... | collective-permute-start | bytes 344072 | tf_op jit(solution)/shard_map/ppermute | solution.py:505
  37.5 8.8 %collective-permute-start.11 = (f32[56,512]{1,0:T(8,128)S(1)}, f32[56,512]{1,0:T(8,128)S(1)}, u32[]{:S(2)}, u32[]{:S(2)}) collective-permute-start(f32[56,512]{1,0:T(8,128)S(1)} %get-tuple-element.55), channel_id=1, source_target_pairs={{0,30},{2,0},{4,2},{6,4},{8,6},{10,8},{12,10},{14,12},{16,14},{18,... | collective-permute-start | bytes 344072 | tf_op jit(solution)/shard_map/ppermute | solution.py:505
  49.0 8.9 %collective-permute-start.13 = (f32[56,512]{1,0:T(8,128)S(1)}, f32[56,512]{1,0:T(8,128)S(1)}, u32[]{:S(2)}, u32[]{:S(2)}) collective-permute-start(f32[56,512]{1,0:T(8,128)S(1)} %shard_map.45), channel_id=1, source_target_pairs={{0,2},{2,4},{4,6},{6,8},{8,10},{10,12},{12,14},{14,16},{16,18},{18... | collective-permute-start | bytes 344072 | tf_op jit(solution)/shard_map/ppermute | solution.py:505
  60.0 1.9 %collective-permute-start.14 = (f32[640,128]{1,0:T(8,128)}, f32[640,128]{1,0:T(8,128)S(1)}, u32[]{:S(2)}, u32[]{:S(2)}) collective-permute-start(f32[640,128]{1,0:T(8,128)} %get-tuple-element.62), channel_id=1, source_target_pairs={{0,1},{1,0},{2,3},{3,2},{4,5},{5,4},{6,7},{7,6},{8,9},{9,8},{10,11... | collective-permute-start | bytes 983048 | tf_op jit(solution)/shard_map/ppermute | solution.py:225
  62.0 5.3 %collective-permute-start.15 = (f32[160,128]{1,0:T(8,128)S(1)}, f32[160,128]{1,0:T(8,128)S(1)}, u32[]{:S(2)}, u32[]{:S(2)}) collective-permute-start(f32[160,128]{1,0:T(8,128)S(1)} %get-tuple-element.64), channel_id=1, source_target_pairs={{0,2},{2,0},{4,6},{6,4},{8,10},{10,8},{12,14},{14,12},{16,18},{18,... | collective-permute-start | bytes 245768 | tf_op jit(solution)/shard_map/ppermute | solution.py:225
  62.1 6.6 %collective-permute-start.16 = (f32[160,128]{1,0:T(8,128)S(1)}, f32[160,128]{1,0:T(8,128)S(1)}, u32[]{:S(2)}, u32[]{:S(2)}) collective-permute-start(f32[160,128]{1,0:T(8,128)S(1)} %get-tuple-element.65), channel_id=1, source_target_pairs={{0,4},{2,6},{4,0},{6,2},{8,12},{10,14},{12,8},{14,10},{16,20},{18,... | collective-permute-start | bytes 245768 | tf_op jit(solution)/shard_map/ppermute | solution.py:225
  62.2 6.6 %collective-permute-start.17 = (f32[160,128]{1,0:T(8,128)S(1)}, f32[160,128]{1,0:T(8,128)S(1)}, u32[]{:S(2)}, u32[]{:S(2)}) collective-permute-start(f32[160,128]{1,0:T(8,128)S(1)} %get-tuple-element.66), channel_id=1, source_target_pairs={{0,6},{2,4},{4,2},{6,0},{8,14},{10,12},{12,10},{14,8},{16,22},{18,... | collective-permute-start | bytes 245768 | tf_op jit(solution)/shard_map/ppermute | solution.py:225
  68.8 5.1 %collective-permute-start.18 = (f32[160,128]{1,0:T(8,128)S(1)}, f32[160,128]{1,0:T(8,128)S(1)}, u32[]{:S(2)}, u32[]{:S(2)}) collective-permute-start(f32[160,128]{1,0:T(8,128)S(1)} %shard_map.49), channel_id=1, source_target_pairs={{0,8},{2,10},{4,12},{6,14},{8,0},{10,2},{12,4},{14,6},{16,24},{18,... | collective-permute-start | bytes 245768 | tf_op jit(solution)/shard_map/ppermute | solution.py:225
  68.8 9.4 %collective-permute-start.19 = (f32[160,128]{1,0:T(8,128)S(1)}, f32[160,128]{1,0:T(8,128)S(1)}, u32[]{:S(2)}, u32[]{:S(2)}) collective-permute-start(f32[160,128]{1,0:T(8,128)S(1)} %shard_map.49), channel_id=1, source_target_pairs={{0,16},{2,18},{4,20},{6,22},{8,24},{10,26},{12,28},{14,30},{16,0},... | collective-permute-start | bytes 245768 | tf_op jit(solution)/shard_map/ppermute | solution.py:225
  70.9 7.3 %collective-permute-start.20 = (f32[160,128]{1,0:T(8,128)S(1)}, f32[160,128]{1,0:T(8,128)S(1)}, u32[]{:S(2)}, u32[]{:S(2)}) collective-permute-start(f32[160,128]{1,0:T(8,128)S(1)} %shard_map.49), channel_id=1, source_target_pairs={{0,24},{2,26},{4,28},{6,30},{8,16},{10,18},{12,20},{14,22},{16,8},... | collective-permute-start | bytes 245768 | tf_op jit(solution)/shard_map/ppermute | solution.py:225
  78.3 4.5 %collective-permute-start.21 = (f32[160,128]{1,0:T(8,128)S(1)}, f32[160,128]{1,0:T(8,128)S(1)}, u32[]{:S(2)}, u32[]{:S(2)}) collective-permute-start(f32[160,128]{1,0:T(8,128)S(1)} %get-tuple-element.68), channel_id=1, source_target_pairs={{0,2},{2,0},{4,6},{6,4},{8,10},{10,8},{12,14},{14,12},{16,18},{18,... | collective-permute-start | bytes 245768 | tf_op jit(solution)/shard_map/ppermute | solution.py:225
  79.7 4.4 %collective-permute-start.22 = (f32[160,128]{1,0:T(8,128)S(1)}, f32[160,128]{1,0:T(8,128)S(1)}, u32[]{:S(2)}, u32[]{:S(2)}) collective-permute-start(f32[160,128]{1,0:T(8,128)S(1)} %get-tuple-element.68), channel_id=1, source_target_pairs={{0,4},{2,6},{4,0},{6,2},{8,12},{10,14},{12,8},{14,10},{16,20},{18,... | collective-permute-start | bytes 245768 | tf_op jit(solution)/shard_map/ppermute | solution.py:225
  80.2 5.3 %collective-permute-start.23 = (f32[160,128]{1,0:T(8,128)S(1)}, f32[160,128]{1,0:T(8,128)S(1)}, u32[]{:S(2)}, u32[]{:S(2)}) collective-permute-start(f32[160,128]{1,0:T(8,128)S(1)} %get-tuple-element.68), channel_id=1, source_target_pairs={{0,6},{2,4},{4,2},{6,0},{8,14},{10,12},{12,10},{14,8},{16,22},{18,... | collective-permute-start | bytes 245768 | tf_op jit(solution)/shard_map/ppermute | solution.py:225
  85.5 1.7 %collective-permute-start.24 = (f32[640,128]{1,0:T(8,128)S(1)}, f32[640,128]{1,0:T(8,128)S(1)}, u32[]{:S(2)}, u32[]{:S(2)}) collective-permute-start(f32[640,128]{1,0:T(8,128)S(1)} %bitcast.22), channel_id=1, source_target_pairs={{0,1},{1,0},{2,3},{3,2},{4,5},{5,4},{6,7},{7,6},{8,9},{9,8},{10,11... | collective-permute-start | bytes 983048 | tf_op jit(solution)/shard_map/ppermute | solution.py:225
  (4 other events, 15.7 us)

commit v5 on v4

--- a/solution.py
+++ b/solution.py
@@ -57,12 +57,20 @@
     return jax.ShapeDtypeStruct(shape, jnp.float32)
 
 
-def exact_dot(a, b, dims=((1,), (0,))):
+def parts_of(x):
+    high = x.astype(jnp.bfloat16)
+    left = x - high.astype(jnp.float32)
+    middle = left.astype(jnp.bfloat16)
+    low = (left - middle.astype(jnp.float32)).astype(jnp.bfloat16)
+    return high, middle, low
+
+
+def exact_dot(a, b, dims=(1, 0)):
+    (ah, am, al), (bh, bm, bl) = a, b
     return lax.dot_general(
-        a,
-        b,
-        (dims, ((), ())),
-        precision=lax.Precision.HIGHEST,
+        jnp.concatenate([ah, ah, am, am, ah, al], axis=dims[0]),
+        jnp.concatenate([bh, bm, bh, bm, bl, bh], axis=dims[1]),
+        (((dims[0],), (dims[1],)), ((), ())),
         preferred_element_type=jnp.float32,
     )
 
@@ -271,7 +279,7 @@
     for stage, after in zip(stages[:-1], stages[1:]):
         axis, stride, _ = stage
         terms = [parts[0]] + [
-            swap(part, axis, d * stride) for d, part in enumerate(parts[1:], 1)
+            swap(parts[d], axis, d * stride) for d in reversed(range(1, len(parts)))
         ]
         rows, radix = terms[0].shape[0], after[2]
         if after == stages[-1]:
@@ -284,7 +292,8 @@
         )(digit(after) if radix > 1 else jnp.zeros((1,), jnp.int32), *terms)
     block = parts[0]
     axis, stride, radix = stages[-1]
-    got = [block] + [swap(block, axis, d * stride) for d in range(1, radix)]
+    got = [swap(block, axis, d * stride) for d in reversed(range(1, radix))]
+    got = [block] + got[::-1]
     while len(got) > 1:
         got = [a + b for a, b in zip(got[::2], got[1::2])]
     block = got[0]
@@ -292,7 +301,7 @@
         mine = lax.axis_index(axis) // stride % radix
         parts = jnp.zeros((radix,) + block.shape, block.dtype)
         parts = lax.dynamic_update_index_in_dim(parts, block, mine, 0)
-        for d in range(1, radix):
+        for d in reversed(range(1, radix)):
             parts = lax.dynamic_update_index_in_dim(
                 parts, swap(block, axis, d * stride), mine ^ d, 0
             )
@@ -456,22 +465,24 @@
     work.append(set_up)
     inverse = factored(piece(0, 0))
     for k in range(count - 1):
-        near = exact_dot(inverse, blocks[place[k, k + 1]])
-        diagonal = blocks[place[k + 1, k + 1]] - exact_dot(near, near, ((0,), (0,)))
+        inverse = parts_of(inverse)
+        near = parts_of(exact_dot(inverse, parts_of(blocks[place[k, k + 1]])))
+        diagonal = blocks[place[k + 1, k + 1]] - exact_dot(near, near, (0, 0))
         ups = {k + 1: near}
 
         def up_of(j, k=k, inverse=inverse, ups=ups):
-            ups[j] = exact_dot(inverse, blocks[place[k, j]])
+            ups[j] = parts_of(exact_dot(inverse, parts_of(blocks[place[k, j]])))
 
         def update(i, j, ups=ups):
             n = place[i, j]
-            blocks[n] = blocks[n] - exact_dot(ups[i], ups[j], ((0,), (0,)))
+            blocks[n] = blocks[n] - exact_dot(ups[i], ups[j], (0, 0))
 
         def solve(rows, k=k, inverse=inverse):
-            finish(rows, k, exact_dot(rest[rows, span(k)], inverse, ((1,), (1,))))
+            finish(rows, k, exact_dot(parts_of(rest[rows, span(k)]), inverse, (1, 1)))
 
         def subtract(rows, j, ups=ups):
-            rest[rows, span(j)] = rest[rows, span(j)] - exact_dot(done[rows, :], ups[j])
+            step = exact_dot(parts_of(done[rows, :]), ups[j])
+            rest[rows, span(j)] = rest[rows, span(j)] - step
 
         strips = [slice(r, r + part) for r in range(0, nodes, part)]
         later = range(k + 2, count)
@@ -487,13 +498,12 @@
             for j in range(k + 1, count)
             for rows in strips
         ]
+        ahead = []
+        if k + 2 == count:
+            work.append(lambda: ahead.append(parts_of(rest[:, span(count - 1)])))
         inverse = factored(diagonal)
     last = count - 1
-    finish(
-        slice(0, nodes),
-        last,
-        exact_dot(rest[:, span(last)], inverse, ((1,), (1,))),
-    )
+    finish(slice(0, nodes), last, exact_dot(ahead[0], parts_of(inverse), (1, 1)))
     for k in range(count):
         store(k).start()
     for k in range(count):

time: 105 us -> 103 us (0.981)
  Pallas kernels: 25.1 us -> 24 us
    pallas_call x14, Pallas kernels: 25.1 us -> 24 us  [call(): pl.pallas_call(body, out_shape=outs, in_specs=[pl.BlockSpec(memory_space=...]
  transfers between devices with their start and end apart: 25 -> 25, of which waited for: 17 -> 16; matrix products, arithmetic and copies ran while one was open for 2% -> 2% of each run, Pallas kernels for 3% -> 3%
where the time goes in v5:
time: 103 us
  waiting for transfers between devices  37.3 us (36%)
  starting transfers between devices  37.1 us (36%)
  Pallas kernels  24 us (23%)
  local copies, waits for them, and re-layouts  3.59 us (3%)
    ppermute x13, starting transfers between devices, to_next(): lax.ppermute(block, axis, [(i, (i + distance) % count) for i in range(cou...  24.8 us
    ppermute x13, waiting for transfers between devices, to_next(): lax.ppermute(block, axis, [(i, (i + distance) % count) for i in range(cou...  24.2 us
    pallas_call x14, Pallas kernels, call(): pl.pallas_call(body, out_shape=outs, in_specs=[pl.BlockSpec(memory_space=...  24 us
    ppermute x11, waiting for transfers between devices, swap(): return lax.ppermute(block, axis, [(i, i ^ distance) for i in range(count)])  12.4 us
    ppermute x11, starting transfers between devices, swap(): return lax.ppermute(block, axis, [(i, i ^ distance) for i in range(count)])  11.7 us
  transfers between devices with their start and end apart: 25, of which 16 were waited for; matrix products, arithmetic and copies ran while one was open for 2% of the time, Pallas kernels for 3%

profile of v5, /device:TPU:0, one launch (start us, length us, event | category | flops | bytes accessed | tf_op | source)
XLA Modules:
  0.0 102.5 jit_solution(11883571247326087673)
XLA Ops:
  1.0 6.9 %collective-permute-start = (f32[1,7,7,512]{3,2,1,0:T(8,128)S(1)}, f32[1,7,7,512]{3,2,1,0:T(8,128)S(1)}, u32[]{:S(2)}, u32[]{:S(2)}) collective-permute-start(f32[1,7,7,512]{3,2,1,0:T(8,128)S(1)} %slice.12), channel_id=1, source_target_pairs={{0,30},{2,0},{4,2},{6,4},{8,6},{10,8},{12,10},{14,12},{16,14},{18,... | collective-permute-start | bytes 301064 | tf_op jit(solution)/shard_map/ppermute | solution.py:515
  13.8 1.2 %collective-permute-done.3.refs_2_.refs_1_ = f32[2,8,8,512]{3,2,1,0:T(8,128)S(1)} collective-permute-done((f32[2,8,8,512]{3,2,1,0:T(8,128)S(1)}, f32[2,8,8,512]{3,2,1,0:T(8,128)S(1)}, u32[]{:S(2)}, u32[]{:S(2)}) %collective-permute-start.3) | collective-permute-done | bytes 262176 | tf_op jit(solution)/shard_map/ppermute | solution.py:515
  15.9 4.8 %collective-permute-start.5 = (f32[56,512]{1,0:T(8,128)S(1)}, f32[56,512]{1,0:T(8,128)S(1)}, u32[]{:S(2)}, u32[]{:S(2)}) collective-permute-start(f32[56,512]{1,0:T(8,128)S(1)} %get-tuple-element.41), channel_id=1, source_target_pairs={{0,30},{2,0},{4,2},{6,4},{8,6},{10,8},{12,10},{14,12},{16,14},{18,... | collective-permute-start | bytes 344072 | tf_op jit(solution)/shard_map/ppermute | solution.py:515
  20.7 3.4 %collective-permute-done.4.refs_2_ = f32[56,512]{1,0:T(8,128)S(1)} collective-permute-done((f32[56,512]{1,0:T(8,128)S(1)}, f32[56,512]{1,0:T(8,128)S(1)}, u32[]{:S(2)}, u32[]{:S(2)}) %collective-permute-start.4) | collective-permute-done | bytes 114720 | tf_op jit(solution)/shard_map/ppermute | solution.py:515
  24.8 1.5 %collective-permute-done.6.refs_2_.refs_1_ = f32[2,8,8,512]{3,2,1,0:T(8,128)S(1)} collective-permute-done((f32[2,8,8,512]{3,2,1,0:T(8,128)S(1)}, f32[2,8,8,512]{3,2,1,0:T(8,128)S(1)}, u32[]{:S(2)}, u32[]{:S(2)}) %collective-permute-start.6) | collective-permute-done | bytes 262176 | tf_op jit(solution)/shard_map/ppermute | solution.py:515
  26.4 5.6 %collective-permute-start.8 = (f32[56,512]{1,0:T(8,128)S(1)}, f32[56,512]{1,0:T(8,128)S(1)}, u32[]{:S(2)}, u32[]{:S(2)}) collective-permute-start(f32[56,512]{1,0:T(8,128)S(1)} %get-tuple-element.48), channel_id=1, source_target_pairs={{0,30},{2,0},{4,2},{6,4},{8,6},{10,8},{12,10},{14,12},{16,14},{18,... | collective-permute-start | bytes 344072 | tf_op jit(solution)/shard_map/ppermute | solution.py:515
  32.0 3.2 %collective-permute-done.7.refs_2_ = f32[56,512]{1,0:T(8,128)S(1)} collective-permute-done((f32[56,512]{1,0:T(8,128)S(1)}, f32[56,512]{1,0:T(8,128)S(1)}, u32[]{:S(2)}, u32[]{:S(2)}) %collective-permute-start.7) | collective-permute-done | bytes 114720 | tf_op jit(solution)/shard_map/ppermute | solution.py:515
  35.9 1.5 %collective-permute-done.9.refs_2_.refs_1_ = f32[2,8,8,512]{3,2,1,0:T(8,128)S(1)} collective-permute-done((f32[2,8,8,512]{3,2,1,0:T(8,128)S(1)}, f32[2,8,8,512]{3,2,1,0:T(8,128)S(1)}, u32[]{:S(2)}, u32[]{:S(2)}) %collective-permute-start.9) | collective-permute-done | bytes 262176 | tf_op jit(solution)/shard_map/ppermute | solution.py:515
  37.5 5.6 %collective-permute-start.11 = (f32[56,512]{1,0:T(8,128)S(1)}, f32[56,512]{1,0:T(8,128)S(1)}, u32[]{:S(2)}, u32[]{:S(2)}) collective-permute-start(f32[56,512]{1,0:T(8,128)S(1)} %get-tuple-element.55), channel_id=1, source_target_pairs={{0,30},{2,0},{4,2},{6,4},{8,6},{10,8},{12,10},{14,12},{16,14},{18,... | collective-permute-start | bytes 344072 | tf_op jit(solution)/shard_map/ppermute | solution.py:515
  43.1 3.2 %collective-permute-done.10.refs_2_ = f32[56,512]{1,0:T(8,128)S(1)} collective-permute-done((f32[56,512]{1,0:T(8,128)S(1)}, f32[56,512]{1,0:T(8,128)S(1)}, u32[]{:S(2)}, u32[]{:S(2)}) %collective-permute-start.10) | collective-permute-done | bytes 114720 | tf_op jit(solution)/shard_map/ppermute | solution.py:515
  46.3 1.2 %shard_map.44 = (f32[8,8,8,512]{3,2,1,0:T(8,128)S(1)}, f32[8,8,8,512]{3,2,1,0:T(8,128)S(1)}, f32[8,8,512]{2,1,0:T(8,128)}, f32[8,8,512]{2,1,0:T(8,128)S(1)}, f32[2,8,8,512]{3,2,1,0:T(8,128)S(1)}) custom-call(f32[8,8,8,512]{3,2,1,0:T(8,128)S(1)} %get-tuple-element.50.refs_0_, f32[2,8,8,512]{3,2,1,0:T(8,128)S(1)} %collective-permute-done.9.refs_2_.refs_1_, ...), custom_call_target="tpu_custom_call" | custom-call | flops 268435456 | bytes 1048576 | tf_op jit(solution)/shard_map/pallas_call | solution.py:40
  47.7 1.3 %collective-permute-done.12.refs_1_.y_face = f32[1,8,8,512]{3,2,1,0:T(8,128)S(1)} collective-permute-done((f32[1,8,8,512]{3,2,1,0:T(8,128)S(1)}, f32[1,8,8,512]{3,2,1,0:T(8,128)S(1)}, u32[]{:S(2)}, u32[]{:S(2)}) %collective-permute-start.12) | collective-permute-done | bytes 131104 | tf_op jit(solution)/shard_map/ppermute | solution.py:515
  49.1 8.8 %collective-permute-done.13.x_low = f32[56,512]{1,0:T(8,128)S(1)} collective-permute-done((f32[56,512]{1,0:T(8,128)S(1)}, f32[56,512]{1,0:T(8,128)S(1)}, u32[]{:S(2)}, u32[]{:S(2)}) %collective-permute-start.13) | collective-permute-done | bytes 114720 | tf_op jit(solution)/shard_map/ppermute | solution.py:515
  57.9 2.0 %shard_map.46 = (f32[392,512]{1,0:T(8,128)}, f32[640,128]{1,0:T(8,128)}) custom-call(s32[1]{0:T(128)} %bitcast.1.mine, f32[8,8,8,512]{3,2,1,0:T(8,128)S(1)} %get-tuple-element.57.image_in, f32[1,8,8,512]{3,2,1,0:T(8,128)S(1)} %collective-permute-done.12.refs_1_.y_face, f32[56,512]{1,0:T(8,128)S(1)} %collective-permute-done.13.x_low, ...), custom_call_target="tpu_custom_call" | custom-call | flops 402653184 | bytes 1048576 | tf_op jit(solution)/shard_map/pallas_call | solution.py:40
  60.1 1.8 %shard_map.47.refs_0_ = f32[640,128]{1,0:T(8,128)S(1)} custom-call(s32[1]{0:T(128)} %bitcast.1.mine, f32[392,512]{1,0:T(8,128)} %get-tuple-element.61.stored.own), custom_call_target="tpu_custom_call" | custom-call | flops 402653184 | bytes 1048576 | tf_op jit(solution)/shard_map/pallas_call | solution.py:40
  62.2 3.4 %collective-permute-start.17 = (f32[160,128]{1,0:T(8,128)S(1)}, f32[160,128]{1,0:T(8,128)S(1)}, u32[]{:S(2)}, u32[]{:S(2)}) collective-permute-start(f32[160,128]{1,0:T(8,128)S(1)} %get-tuple-element.66), channel_id=1, source_target_pairs={{0,2},{2,0},{4,6},{6,4},{8,10},{10,8},{12,14},{14,12},{16,18},{18,... | collective-permute-start | bytes 245768 | tf_op jit(solution)/shard_map/ppermute | solution.py:233
  65.6 2.7 %collective-permute-done.15.refs_1_ = f32[160,128]{1,0:T(8,128)S(1)} collective-permute-done((f32[160,128]{1,0:T(8,128)S(1)}, f32[160,128]{1,0:T(8,128)S(1)}, u32[]{:S(2)}, u32[]{:S(2)}) %collective-permute-start.15) | collective-permute-done | bytes 81952 | tf_op jit(solution)/shard_map/ppermute | solution.py:233
  68.8 1.3 %collective-permute-start.19 = (f32[160,128]{1,0:T(8,128)S(1)}, f32[160,128]{1,0:T(8,128)S(1)}, u32[]{:S(2)}, u32[]{:S(2)}) collective-permute-start(f32[160,128]{1,0:T(8,128)S(1)} %shard_map.49), channel_id=1, source_target_pairs={{0,16},{2,18},{4,20},{6,22},{8,24},{10,26},{12,28},{14,30},{16,0},... | collective-permute-start | bytes 245768 | tf_op jit(solution)/shard_map/ppermute | solution.py:233
  70.2 3.0 %collective-permute-start.20 = (f32[160,128]{1,0:T(8,128)S(1)}, f32[160,128]{1,0:T(8,128)S(1)}, u32[]{:S(2)}, u32[]{:S(2)}) collective-permute-start(f32[160,128]{1,0:T(8,128)S(1)} %shard_map.49), channel_id=1, source_target_pairs={{0,24},{2,26},{4,28},{6,30},{8,16},{10,18},{12,20},{14,22},{16,8},... | collective-permute-start | bytes 245768 | tf_op jit(solution)/shard_map/ppermute | solution.py:233
  73.8 4.4 %collective-permute-done.19 = f32[160,128]{1,0:T(8,128)S(1)} collective-permute-done((f32[160,128]{1,0:T(8,128)S(1)}, f32[160,128]{1,0:T(8,128)S(1)}, u32[]{:S(2)}, u32[]{:S(2)}) %collective-permute-start.19) | collective-permute-done | bytes 81952 | tf_op jit(solution)/shard_map/ppermute | solution.py:233
  80.2 1.7 %collective-permute-start.23 = (f32[160,128]{1,0:T(8,128)S(1)}, f32[160,128]{1,0:T(8,128)S(1)}, u32[]{:S(2)}, u32[]{:S(2)}) collective-permute-start(f32[160,128]{1,0:T(8,128)S(1)} %get-tuple-element.68), channel_id=1, source_target_pairs={{0,2},{2,0},{4,6},{6,4},{8,10},{10,8},{12,14},{14,12},{16,18},{18,... | collective-permute-start | bytes 245768 | tf_op jit(solution)/shard_map/ppermute | solution.py:233
  81.9 1.9 %collective-permute-done.21 = f32[160,128]{1,0:T(8,128)S(1)} collective-permute-done((f32[160,128]{1,0:T(8,128)S(1)}, f32[160,128]{1,0:T(8,128)S(1)}, u32[]{:S(2)}, u32[]{:S(2)}) %collective-permute-start.21) | collective-permute-done | bytes 81952 | tf_op jit(solution)/shard_map/ppermute | solution.py:233
  84.8 1.5 %collective-permute-done.24 = f32[640,128]{1,0:T(8,128)S(1)} collective-permute-done((f32[640,128]{1,0:T(8,128)S(1)}, f32[640,128]{1,0:T(8,128)S(1)}, u32[]{:S(2)}, u32[]{:S(2)}) %collective-permute-start.24) | collective-permute-done | bytes 327712 | tf_op jit(solution)/shard_map/ppermute | solution.py:233
  86.4 16.0 %shard_map.50 = f32[49,7,512]{2,1,0:T(8,128)} custom-call(f32[1280,128]{1,0:T(8,128)S(1)} %bitcast.20, f32[392,512]{1,0:T(8,128)S(1)} %copy-done.1), custom_call_target="tpu_custom_call" | custom-call | flops 134217728 | bytes 1048576 | tf_op jit(solution)/shard_map/pallas_call | solution.py:40
  (59 shorter events, 13.8 us)
Async XLA Ops:
  1.0 11.7 %collective-permute-start = (f32[1,7,7,512]{3,2,1,0:T(8,128)S(1)}, f32[1,7,7,512]{3,2,1,0:T(8,128)S(1)}, u32[]{:S(2)}, u32[]{:S(2)}) collective-permute-start(f32[1,7,7,512]{3,2,1,0:T(8,128)S(1)} %slice.12), channel_id=1, source_target_pairs={{0,30},{2,0},{4,2},{6,4},{8,6},{10,8},{12,10},{14,12},{16,14},{18,... | collective-permute-start | bytes 301064 | tf_op jit(solution)/shard_map/ppermute | solution.py:515
  8.8 3.9 %collective-permute-start.1 = (f32[7,1,7,512]{3,2,1,0:T(8,128)S(1)}, f32[7,1,7,512]{3,2,1,0:T(8,128)S(1)}, u32[]{:S(2)}, u32[]{:S(2)}) collective-permute-start(f32[7,1,7,512]{3,2,1,0:T(8,128)S(1)} %slice.13), channel_id=1, source_target_pairs={{0,1},{1,0},{2,3},{3,2},{4,5},{5,4},{6,7},{7,6},{8,9},{9,8},{10,11... | collective-permute-start | bytes 301064 | tf_op jit(solution)/shard_map/ppermute | solution.py:515
  9.5 3.2 %collective-permute-start.2 = (f32[1,1,7,512]{3,2,1,0:T(8,128)S(1)}, f32[1,1,7,512]{3,2,1,0:T(8,128)S(1)}, u32[]{:S(2)}, u32[]{:S(2)}) collective-permute-start(f32[1,1,7,512]{3,2,1,0:T(8,128)S(1)} %slice.14), channel_id=1, source_target_pairs={{3,0},{2,1},{5,2},{4,3},{7,4},{6,5},{9,6},{8,7},{11,8},{10,9},{13,... | collective-permute-start | bytes 43016 | tf_op jit(solution)/shard_map/ppermute | solution.py:525
  13.3 1.7 %collective-permute-start.3 = (f32[2,8,8,512]{3,2,1,0:T(8,128)S(1)}, f32[2,8,8,512]{3,2,1,0:T(8,128)S(1)}, u32[]{:S(2)}, u32[]{:S(2)}) collective-permute-start(f32[2,8,8,512]{3,2,1,0:T(8,128)S(1)} %get-tuple-element.37), channel_id=1, source_target_pairs={{0,1},{1,0},{2,3},{3,2},{4,5},{5,4},{6,7},{7,6},{8,9},{9,8},{10,11... | collective-permute-start | bytes 786440 | tf_op jit(solution)/shard_map/ppermute | solution.py:515
  15.0 9.1 %collective-permute-start.4 = (f32[56,512]{1,0:T(8,128)S(1)}, f32[56,512]{1,0:T(8,128)S(1)}, u32[]{:S(2)}, u32[]{:S(2)}) collective-permute-start(f32[56,512]{1,0:T(8,128)S(1)} %get-tuple-element.40), channel_id=1, source_target_pairs={{0,2},{2,4},{4,6},{6,8},{8,10},{10,12},{12,14},{14,16},{16,18},{18... | collective-permute-start | bytes 344072 | tf_op jit(solution)/shard_map/ppermute | solution.py:515
  15.9 8.2 %collective-permute-start.5 = (f32[56,512]{1,0:T(8,128)S(1)}, f32[56,512]{1,0:T(8,128)S(1)}, u32[]{:S(2)}, u32[]{:S(2)}) collective-permute-start(f32[56,512]{1,0:T(8,128)S(1)} %get-tuple-element.41), channel_id=1, source_target_pairs={{0,30},{2,0},{4,2},{6,4},{8,6},{10,8},{12,10},{14,12},{16,14},{18,... | collective-permute-start | bytes 344072 | tf_op jit(solution)/shard_map/ppermute | solution.py:515
  24.7 1.6 %collective-permute-start.6 = (f32[2,8,8,512]{3,2,1,0:T(8,128)S(1)}, f32[2,8,8,512]{3,2,1,0:T(8,128)S(1)}, u32[]{:S(2)}, u32[]{:S(2)}) collective-permute-start(f32[2,8,8,512]{3,2,1,0:T(8,128)S(1)} %get-tuple-element.44), channel_id=1, source_target_pairs={{0,1},{1,0},{2,3},{3,2},{4,5},{5,4},{6,7},{7,6},{8,9},{9,8},{10,11... | collective-permute-start | bytes 786440 | tf_op jit(solution)/shard_map/ppermute | solution.py:515
  26.3 8.8 %collective-permute-start.7 = (f32[56,512]{1,0:T(8,128)S(1)}, f32[56,512]{1,0:T(8,128)S(1)}, u32[]{:S(2)}, u32[]{:S(2)}) collective-permute-start(f32[56,512]{1,0:T(8,128)S(1)} %get-tuple-element.47), channel_id=1, source_target_pairs={{0,2},{2,4},{4,6},{6,8},{8,10},{10,12},{12,14},{14,16},{16,18},{18... | collective-permute-start | bytes 344072 | tf_op jit(solution)/shard_map/ppermute | solution.py:515
  26.4 8.8 %collective-permute-start.8 = (f32[56,512]{1,0:T(8,128)S(1)}, f32[56,512]{1,0:T(8,128)S(1)}, u32[]{:S(2)}, u32[]{:S(2)}) collective-permute-start(f32[56,512]{1,0:T(8,128)S(1)} %get-tuple-element.48), channel_id=1, source_target_pairs={{0,30},{2,0},{4,2},{6,4},{8,6},{10,8},{12,10},{14,12},{16,14},{18,... | collective-permute-start | bytes 344072 | tf_op jit(solution)/shard_map/ppermute | solution.py:515
  35.8 1.6 %collective-permute-start.9 = (f32[2,8,8,512]{3,2,1,0:T(8,128)S(1)}, f32[2,8,8,512]{3,2,1,0:T(8,128)S(1)}, u32[]{:S(2)}, u32[]{:S(2)}) collective-permute-start(f32[2,8,8,512]{3,2,1,0:T(8,128)S(1)} %get-tuple-element.51), channel_id=1, source_target_pairs={{0,1},{1,0},{2,3},{3,2},{4,5},{5,4},{6,7},{7,6},{8,9},{9,8},{10,11... | collective-permute-start | bytes 786440 | tf_op jit(solution)/shard_map/ppermute | solution.py:515
  37.5 8.9 %collective-permute-start.10 = (f32[56,512]{1,0:T(8,128)S(1)}, f32[56,512]{1,0:T(8,128)S(1)}, u32[]{:S(2)}, u32[]{:S(2)}) collective-permute-start(f32[56,512]{1,0:T(8,128)S(1)} %get-tuple-element.54), channel_id=1, source_target_pairs={{0,2},{2,4},{4,6},{6,8},{8,10},{10,12},{12,14},{14,16},{16,18},{18... | collective-permute-start | bytes 344072 | tf_op jit(solution)/shard_map/ppermute | solution.py:515
  37.5 8.8 %collective-permute-start.11 = (f32[56,512]{1,0:T(8,128)S(1)}, f32[56,512]{1,0:T(8,128)S(1)}, u32[]{:S(2)}, u32[]{:S(2)}) collective-permute-start(f32[56,512]{1,0:T(8,128)S(1)} %get-tuple-element.55), channel_id=1, source_target_pairs={{0,30},{2,0},{4,2},{6,4},{8,6},{10,8},{12,10},{14,12},{16,14},{18,... | collective-permute-start | bytes 344072 | tf_op jit(solution)/shard_map/ppermute | solution.py:515
  49.0 8.9 %collective-permute-start.13 = (f32[56,512]{1,0:T(8,128)S(1)}, f32[56,512]{1,0:T(8,128)S(1)}, u32[]{:S(2)}, u32[]{:S(2)}) collective-permute-start(f32[56,512]{1,0:T(8,128)S(1)} %shard_map.45), channel_id=1, source_target_pairs={{0,2},{2,4},{4,6},{6,8},{8,10},{10,12},{12,14},{14,16},{16,18},{18... | collective-permute-start | bytes 344072 | tf_op jit(solution)/shard_map/ppermute | solution.py:515
  60.0 1.9 %collective-permute-start.14 = (f32[640,128]{1,0:T(8,128)}, f32[640,128]{1,0:T(8,128)S(1)}, u32[]{:S(2)}, u32[]{:S(2)}) collective-permute-start(f32[640,128]{1,0:T(8,128)} %get-tuple-element.62), channel_id=1, source_target_pairs={{0,1},{1,0},{2,3},{3,2},{4,5},{5,4},{6,7},{7,6},{8,9},{9,8},{10,11... | collective-permute-start | bytes 983048 | tf_op jit(solution)/shard_map/ppermute | solution.py:233
  62.0 6.3 %collective-permute-start.15 = (f32[160,128]{1,0:T(8,128)S(1)}, f32[160,128]{1,0:T(8,128)S(1)}, u32[]{:S(2)}, u32[]{:S(2)}) collective-permute-start(f32[160,128]{1,0:T(8,128)S(1)} %get-tuple-element.64), channel_id=1, source_target_pairs={{0,6},{2,4},{4,2},{6,0},{8,14},{10,12},{12,10},{14,8},{16,22},{18,... | collective-permute-start | bytes 245768 | tf_op jit(solution)/shard_map/ppermute | solution.py:233
  62.1 6.6 %collective-permute-start.16 = (f32[160,128]{1,0:T(8,128)S(1)}, f32[160,128]{1,0:T(8,128)S(1)}, u32[]{:S(2)}, u32[]{:S(2)}) collective-permute-start(f32[160,128]{1,0:T(8,128)S(1)} %get-tuple-element.65), channel_id=1, source_target_pairs={{0,4},{2,6},{4,0},{6,2},{8,12},{10,14},{12,8},{14,10},{16,20},{18,... | collective-permute-start | bytes 245768 | tf_op jit(solution)/shard_map/ppermute | solution.py:233
  62.2 6.6 %collective-permute-start.17 = (f32[160,128]{1,0:T(8,128)S(1)}, f32[160,128]{1,0:T(8,128)S(1)}, u32[]{:S(2)}, u32[]{:S(2)}) collective-permute-start(f32[160,128]{1,0:T(8,128)S(1)} %get-tuple-element.66), channel_id=1, source_target_pairs={{0,2},{2,0},{4,6},{6,4},{8,10},{10,8},{12,14},{14,12},{16,18},{18,... | collective-permute-start | bytes 245768 | tf_op jit(solution)/shard_map/ppermute | solution.py:233
  68.8 5.1 %collective-permute-start.18 = (f32[160,128]{1,0:T(8,128)S(1)}, f32[160,128]{1,0:T(8,128)S(1)}, u32[]{:S(2)}, u32[]{:S(2)}) collective-permute-start(f32[160,128]{1,0:T(8,128)S(1)} %shard_map.49), channel_id=1, source_target_pairs={{0,8},{2,10},{4,12},{6,14},{8,0},{10,2},{12,4},{14,6},{16,24},{18,... | collective-permute-start | bytes 245768 | tf_op jit(solution)/shard_map/ppermute | solution.py:233
  68.8 9.4 %collective-permute-start.19 = (f32[160,128]{1,0:T(8,128)S(1)}, f32[160,128]{1,0:T(8,128)S(1)}, u32[]{:S(2)}, u32[]{:S(2)}) collective-permute-start(f32[160,128]{1,0:T(8,128)S(1)} %shard_map.49), channel_id=1, source_target_pairs={{0,16},{2,18},{4,20},{6,22},{8,24},{10,26},{12,28},{14,30},{16,0},... | collective-permute-start | bytes 245768 | tf_op jit(solution)/shard_map/ppermute | solution.py:233
  70.2 8.1 %collective-permute-start.20 = (f32[160,128]{1,0:T(8,128)S(1)}, f32[160,128]{1,0:T(8,128)S(1)}, u32[]{:S(2)}, u32[]{:S(2)}) collective-permute-start(f32[160,128]{1,0:T(8,128)S(1)} %shard_map.49), channel_id=1, source_target_pairs={{0,24},{2,26},{4,28},{6,30},{8,16},{10,18},{12,20},{14,22},{16,8},... | collective-permute-start | bytes 245768 | tf_op jit(solution)/shard_map/ppermute | solution.py:233
  78.3 5.5 %collective-permute-start.21 = (f32[160,128]{1,0:T(8,128)S(1)}, f32[160,128]{1,0:T(8,128)S(1)}, u32[]{:S(2)}, u32[]{:S(2)}) collective-permute-start(f32[160,128]{1,0:T(8,128)S(1)} %get-tuple-element.68), channel_id=1, source_target_pairs={{0,6},{2,4},{4,2},{6,0},{8,14},{10,12},{12,10},{14,8},{16,22},{18,... | collective-permute-start | bytes 245768 | tf_op jit(solution)/shard_map/ppermute | solution.py:233
  79.4 5.1 %collective-permute-start.22 = (f32[160,128]{1,0:T(8,128)S(1)}, f32[160,128]{1,0:T(8,128)S(1)}, u32[]{:S(2)}, u32[]{:S(2)}) collective-permute-start(f32[160,128]{1,0:T(8,128)S(1)} %get-tuple-element.68), channel_id=1, source_target_pairs={{0,4},{2,6},{4,0},{6,2},{8,12},{10,14},{12,8},{14,10},{16,20},{18,... | collective-permute-start | bytes 245768 | tf_op jit(solution)/shard_map/ppermute | solution.py:233
  80.2 4.4 %collective-permute-start.23 = (f32[160,128]{1,0:T(8,128)S(1)}, f32[160,128]{1,0:T(8,128)S(1)}, u32[]{:S(2)}, u32[]{:S(2)}) collective-permute-start(f32[160,128]{1,0:T(8,128)S(1)} %get-tuple-element.68), channel_id=1, source_target_pairs={{0,2},{2,0},{4,6},{6,4},{8,10},{10,8},{12,14},{14,12},{16,18},{18,... | collective-permute-start | bytes 245768 | tf_op jit(solution)/shard_map/ppermute | solution.py:233
  84.6 1.7 %collective-permute-start.24 = (f32[640,128]{1,0:T(8,128)S(1)}, f32[640,128]{1,0:T(8,128)S(1)}, u32[]{:S(2)}, u32[]{:S(2)}) collective-permute-start(f32[640,128]{1,0:T(8,128)S(1)} %bitcast.22), channel_id=1, source_target_pairs={{0,1},{1,0},{2,3},{3,2},{4,5},{5,4},{6,7},{7,6},{8,9},{9,8},{10,11... | collective-permute-start | bytes 983048 | tf_op jit(solution)/shard_map/ppermute | solution.py:233
  (4 other events, 15.7 us)

commit v6 on v5

--- a/solution.py
+++ b/solution.py
@@ -91,7 +91,7 @@
     ).astype(jnp.bfloat16)
 
 
-def cell_product(values, matrix, image, x_first, x_last, y_sent):
+def cell_product(values, matrix, image, *planes):
     edge = values.shape[0]
     width = values.shape[3]
     rows = values.reshape(edge**3, width).astype(jnp.bfloat16)
@@ -101,35 +101,34 @@
     where = lax.broadcasted_iota(jnp.int32, products.shape, 2)
     products = jnp.where((where == 0) | (where == edge - 1), wrap, products)
     image[...] = products
-    x_first[...] = products[0]
+    x_last, *x_first, y_sent = planes
     x_last[...] = products[edge - 1]
     y_sent[0] = products[:, edge - 1]
-    y_sent[1] = products[:, 0]
-
-
-def first_body(own, x_next, y_next, corner, matrix, values, *sums):
+    if x_first:
+        x_first[0][...] = products[0]
+        y_sent[1] = products[:, 0]
+
+
+def first_body(own, x_next, y_next, matrix, values, *sums):
     order_now = own.shape[0]
     values[:order_now, :order_now, :order_now] = own[...]
     values[order_now:, :order_now, :order_now] = x_next[...]
-    values[:order_now, order_now:, :order_now] = y_next[...]
-    values[order_now:, order_now:, :order_now] = corner[...]
+    values[:, order_now:, :order_now] = y_next[...]
     values[:, :, order_now:] = values[:, :, :1]
     cell_product(values[...], matrix, *sums)
 
 
-def edge_body(*refs):
-    *planes, y_faces = refs[: len(refs) // 2 + 1]
-    outs = refs[len(refs) // 2 + 1 :]
-    edge = planes[0].shape[0]
+def edge_body(plane, y_faces, *refs, at):
+    out = refs[-1]
+    edge = plane.shape[0]
     order_now = edge - 1
-    for plane, out, at in zip(planes, outs, (edge - 1, 0)):
-        for b in range(edge):
-            row = plane[b]
-            if b == 0:
-                row = row + y_faces[0, at]
-            if b == edge - 1 and y_faces.shape[0] > 1:
-                row = row + y_faces[1, at]
-            out[order_now * b : order_now * (b + 1)] = row[:order_now]
+    for b in range(edge):
+        row = plane[b]
+        if b == 0:
+            row = row + y_faces[0, at]
+        if b == edge - 1 and y_faces.shape[0] > 1:
+            row = row + y_faces[1, at]
+        out[order_now * b : order_now * (b + 1)] = row[:order_now]
 
 
 def updated(image, y_faces, x_low, x_high, current, previous, alpha, beta):
@@ -515,16 +514,6 @@
     return lax.ppermute(block, axis, [(i, (i + distance) % count) for i in range(count)])
 
 
-def from_next_both(block):
-    rows, columns = lax.axis_size("wide"), lax.axis_size("narrow")
-    route = [
-        ((i + 1) % rows * columns + (j + 1) % columns, i * columns + j)
-        for i in range(rows)
-        for j in range(columns)
-    ]
-    return lax.ppermute(block, ("wide", "narrow"), route)
-
-
 def y_exchange(sent):
     if lax.axis_size("narrow") == 2:
         return to_next(sent, "narrow", 1)
@@ -551,12 +540,12 @@
     )
 
     x_next = to_next(orbitals[:1], "wide", -1)
-    corner = from_next_both(orbitals[:1, :1])
-    y_next = to_next(orbitals[:, :1], "narrow", -1)
+    first_rows = jnp.concatenate([orbitals[:, :1], x_next[:, :1]], axis=0)
+    y_next = to_next(first_rows, "narrow", -1)
     product_flops = 2 * cell_nodes**2 * width
-    current, image, x_first, x_last, y_sent = vmem_call(
+    current, image, x_last, x_first, y_sent = vmem_call(
         first_body, (box, *sums), flops=product_flops
-    )(orbitals, x_next, y_next, corner, matrix)
+    )(orbitals, x_next, y_next, matrix)
 
     half_width = (band_high - band_low) / 2.0
     sigma_now = half_width / (anchor - (band_low + band_high) / 2.0)
@@ -564,27 +553,35 @@
     alpha, beta, previous = sigma_now / half_width, None, None
     for degree_step in range(1, DEG):
         y_faces = y_exchange(y_sent)
-        x_last, x_first = vmem_call(edge_body, (sent, sent))(
-            x_last, x_first, y_faces
+        (x_first,) = vmem_call(functools.partial(edge_body, at=0), (sent,))(
+            x_first, y_faces
+        )
+        (x_last,) = vmem_call(functools.partial(edge_body, at=edge - 1), (sent,))(
+            x_last, y_faces, x_first
         )
         x_high = to_next(x_first, "wide", -1)
         x_low = to_next(x_last, "wide", 1)
         operands = [image, y_faces, x_low, x_high, current]
         if previous is not None:
             operands.append(previous)
-        next_values, image, x_first, x_last, y_sent = vmem_call(
+        if degree_step == DEG - 1:
+            sums = (box, plane, f32(1, edge, edge, width))
+        next_values, image, x_last, *rest, y_sent = vmem_call(
             functools.partial(middle_body, alpha=alpha, beta=beta),
             (box, *sums),
             scratch=[pltpu.VMEM(box.shape, jnp.float32)],
             flops=product_flops,
         )(*operands, matrix)
         previous, current = current, next_values
+        x_first = rest[0] if rest else None
         sigma_new = 1.0 / (tau_value - sigma_now)
         alpha, beta = 2.0 * sigma_new / half_width, sigma_now * sigma_new
         sigma_now = sigma_new
 
-    y_low = to_next(y_sent[:1], "narrow", 1)
-    (x_last,) = vmem_call(edge_body, (sent,))(x_last, y_low)
+    y_low = to_next(y_sent, "narrow", 1)
+    (x_last,) = vmem_call(functools.partial(edge_body, at=edge - 1), (sent,))(
+        x_last, y_low
+    )
     x_low = to_next(x_last, "wide", 1)
     blocks = width // LANES
     rows = cut_rows(blocks * (blocks + 1) // 2 * LANES)

time: 103 us -> 102 us (level)
  local copies, waits for them, and re-layouts: 3.59 us -> 1.24 us
  waiting for transfers between devices: 37.3 us -> 39.5 us
    ppermute x13, waiting for transfers between devices: 24.2 us -> 27 us  [to_next(): lax.ppermute(block, axis, [(i, (i + distance) % count) for i in range(cou...]
    slice x3, local copies, waits for them, and re-layouts: 1.64 us -> 0.01 us  [on_device(): first_rows = jnp.concatenate([orbitals[:, :1], x_next[:, :1]], axis=0)]
    pallas_call x14 -> x17, Pallas kernels: 24 us -> 23.4 us  [call(): pl.pallas_call(body, out_shape=outs, in_specs=[pl.BlockSpec(memory_space=...]
  transfers between devices with their start and end apart: 25 -> 24, of which waited for: 16 -> 17; matrix products, arithmetic and copies ran while one was open for 2% -> 0% of each run, Pallas kernels for 3% -> 3%
where the time goes in v6:
time: 102 us
  waiting for transfers between devices  39.5 us (39%)
  starting transfers between devices  37.1 us (36%)
  Pallas kernels  23.4 us (23%)
  local copies, waits for them, and re-layouts  1.24 us (1%)
    ppermute x13, waiting for transfers between devices, to_next(): lax.ppermute(block, axis, [(i, (i + distance) % count) for i in range(cou...  27 us
    ppermute x13, starting transfers between devices, to_next(): lax.ppermute(block, axis, [(i, (i + distance) % count) for i in range(cou...  25.4 us
    pallas_call x17, Pallas kernels, call(): pl.pallas_call(body, out_shape=outs, in_specs=[pl.BlockSpec(memory_space=...  23.4 us
    ppermute x11, waiting for transfers between devices, swap(): return lax.ppermute(block, axis, [(i, i ^ distance) for i in range(count)])  12.4 us
    ppermute x11, starting transfers between devices, swap(): return lax.ppermute(block, axis, [(i, i ^ distance) for i in range(count)])  11.7 us
  transfers between devices with their start and end apart: 24, of which 17 were waited for; matrix products, arithmetic and copies ran while one was open for 0% of the time, Pallas kernels for 3%

profile of v6, /device:TPU:0, one launch (start us, length us, event | category | flops | bytes accessed | tf_op | source)
XLA Modules:
  0.0 101.8 jit_solution(13409339203589547021)
XLA Ops:
  0.9 7.0 %collective-permute-start = (f32[1,7,7,512]{3,2,1,0:T(8,128)S(1)}, f32[1,7,7,512]{3,2,1,0:T(8,128)S(1)}, u32[]{:S(2)}, u32[]{:S(2)}) collective-permute-start(f32[1,7,7,512]{3,2,1,0:T(8,128)S(1)} %slice.9), channel_id=1, source_target_pairs={{0,30},{2,0},{4,2},{6,4},{8,6},{10,8},{12,10},{14,12},{16,14},{18,... | collective-permute-start | bytes 301064 | tf_op jit(solution)/shard_map/ppermute | solution.py:514
  7.9 2.4 %collective-permute-done.x_next = f32[1,7,7,512]{3,2,1,0:T(8,128)S(1)} collective-permute-done((f32[1,7,7,512]{3,2,1,0:T(8,128)S(1)}, f32[1,7,7,512]{3,2,1,0:T(8,128)S(1)}, u32[]{:S(2)}, u32[]{:S(2)}) %collective-permute-start) | collective-permute-done | bytes 100384 | tf_op jit(solution)/shard_map/ppermute | solution.py:514
  12.9 1.2 %collective-permute-done.2.y_faces.refs_1_ = f32[2,8,8,512]{3,2,1,0:T(8,128)S(1)} collective-permute-done((f32[2,8,8,512]{3,2,1,0:T(8,128)S(1)}, f32[2,8,8,512]{3,2,1,0:T(8,128)S(1)}, u32[]{:S(2)}, u32[]{:S(2)}) %collective-permute-start.2) | collective-permute-done | bytes 262176 | tf_op jit(solution)/shard_map/ppermute | solution.py:514
  14.1 6.1 %collective-permute-start.4 = (f32[56,512]{1,0:T(8,128)S(1)}, f32[56,512]{1,0:T(8,128)S(1)}, u32[]{:S(2)}, u32[]{:S(2)}) collective-permute-start(f32[56,512]{1,0:T(8,128)S(1)} %shard_map.39.refs_0_), channel_id=1, source_target_pairs={{0,30},{2,0},{4,2},{6,4},{8,6},{10,8},{12,10},{14,12},{16,14},{18,... | collective-permute-start | bytes 344072 | tf_op jit(solution)/shard_map/ppermute | solution.py:514
  20.3 3.6 %collective-permute-done.3.refs_2_ = f32[56,512]{1,0:T(8,128)S(1)} collective-permute-done((f32[56,512]{1,0:T(8,128)S(1)}, f32[56,512]{1,0:T(8,128)S(1)}, u32[]{:S(2)}, u32[]{:S(2)}) %collective-permute-start.3) | collective-permute-done | bytes 114720 | tf_op jit(solution)/shard_map/ppermute | solution.py:514
  24.5 1.5 %collective-permute-done.5.y_faces.refs_1_ = f32[2,8,8,512]{3,2,1,0:T(8,128)S(1)} collective-permute-done((f32[2,8,8,512]{3,2,1,0:T(8,128)S(1)}, f32[2,8,8,512]{3,2,1,0:T(8,128)S(1)}, u32[]{:S(2)}, u32[]{:S(2)}) %collective-permute-start.5) | collective-permute-done | bytes 262176 | tf_op jit(solution)/shard_map/ppermute | solution.py:514
  26.2 5.6 %collective-permute-start.7 = (f32[56,512]{1,0:T(8,128)S(1)}, f32[56,512]{1,0:T(8,128)S(1)}, u32[]{:S(2)}, u32[]{:S(2)}) collective-permute-start(f32[56,512]{1,0:T(8,128)S(1)} %shard_map.42.refs_0_), channel_id=1, source_target_pairs={{0,30},{2,0},{4,2},{6,4},{8,6},{10,8},{12,10},{14,12},{16,14},{18,... | collective-permute-start | bytes 344072 | tf_op jit(solution)/shard_map/ppermute | solution.py:514
  31.8 3.2 %collective-permute-done.6.refs_2_ = f32[56,512]{1,0:T(8,128)S(1)} collective-permute-done((f32[56,512]{1,0:T(8,128)S(1)}, f32[56,512]{1,0:T(8,128)S(1)}, u32[]{:S(2)}, u32[]{:S(2)}) %collective-permute-start.6) | collective-permute-done | bytes 114720 | tf_op jit(solution)/shard_map/ppermute | solution.py:514
  35.7 1.5 %collective-permute-done.8.y_faces.refs_1_ = f32[2,8,8,512]{3,2,1,0:T(8,128)S(1)} collective-permute-done((f32[2,8,8,512]{3,2,1,0:T(8,128)S(1)}, f32[2,8,8,512]{3,2,1,0:T(8,128)S(1)}, u32[]{:S(2)}, u32[]{:S(2)}) %collective-permute-start.8) | collective-permute-done | bytes 262176 | tf_op jit(solution)/shard_map/ppermute | solution.py:514
  37.4 5.6 %collective-permute-start.10 = (f32[56,512]{1,0:T(8,128)S(1)}, f32[56,512]{1,0:T(8,128)S(1)}, u32[]{:S(2)}, u32[]{:S(2)}) collective-permute-start(f32[56,512]{1,0:T(8,128)S(1)} %shard_map.45.refs_0_), channel_id=1, source_target_pairs={{0,30},{2,0},{4,2},{6,4},{8,6},{10,8},{12,10},{14,12},{16,14},{18,... | collective-permute-start | bytes 344072 | tf_op jit(solution)/shard_map/ppermute | solution.py:514
  43.0 3.2 %collective-permute-done.9.refs_2_ = f32[56,512]{1,0:T(8,128)S(1)} collective-permute-done((f32[56,512]{1,0:T(8,128)S(1)}, f32[56,512]{1,0:T(8,128)S(1)}, u32[]{:S(2)}, u32[]{:S(2)}) %collective-permute-start.9) | collective-permute-done | bytes 114720 | tf_op jit(solution)/shard_map/ppermute | solution.py:514
  46.9 1.3 %collective-permute-done.11.y_faces.y_face = f32[1,8,8,512]{3,2,1,0:T(8,128)S(1)} collective-permute-done((f32[1,8,8,512]{3,2,1,0:T(8,128)S(1)}, f32[1,8,8,512]{3,2,1,0:T(8,128)S(1)}, u32[]{:S(2)}, u32[]{:S(2)}) %collective-permute-start.11) | collective-permute-done | bytes 131104 | tf_op jit(solution)/shard_map/ppermute | solution.py:514
  48.4 8.8 %collective-permute-done.12.x_low = f32[56,512]{1,0:T(8,128)S(1)} collective-permute-done((f32[56,512]{1,0:T(8,128)S(1)}, f32[56,512]{1,0:T(8,128)S(1)}, u32[]{:S(2)}, u32[]{:S(2)}) %collective-permute-start.12) | collective-permute-done | bytes 114720 | tf_op jit(solution)/shard_map/ppermute | solution.py:514
  57.2 2.0 %shard_map.49 = (f32[392,512]{1,0:T(8,128)}, f32[640,128]{1,0:T(8,128)}) custom-call(s32[1]{0:T(128)} %bitcast.1.mine, f32[8,8,8,512]{3,2,1,0:T(8,128)S(1)} %get-tuple-element.45.image_in, f32[1,8,8,512]{3,2,1,0:T(8,128)S(1)} %collective-permute-done.11.y_faces.y_face, f32[56,512]{1,0:T(8,128)S(1)} %collective-permute-done.12.x_low, ...), custom_call_target="tpu_custom_call" | custom-call | flops 402653184 | bytes 1048576 | tf_op jit(solution)/shard_map/pallas_call | solution.py:40
  59.3 1.8 %shard_map.50.refs_0_ = f32[640,128]{1,0:T(8,128)S(1)} custom-call(s32[1]{0:T(128)} %bitcast.1.mine, f32[392,512]{1,0:T(8,128)} %get-tuple-element.49.stored.own), custom_call_target="tpu_custom_call" | custom-call | flops 402653184 | bytes 1048576 | tf_op jit(solution)/shard_map/pallas_call | solution.py:40
  61.4 3.4 %collective-permute-start.16 = (f32[160,128]{1,0:T(8,128)S(1)}, f32[160,128]{1,0:T(8,128)S(1)}, u32[]{:S(2)}, u32[]{:S(2)}) collective-permute-start(f32[160,128]{1,0:T(8,128)S(1)} %get-tuple-element.54), channel_id=1, source_target_pairs={{0,2},{2,0},{4,6},{6,4},{8,10},{10,8},{12,14},{14,12},{16,18},{18,... | collective-permute-start | bytes 245768 | tf_op jit(solution)/shard_map/ppermute | solution.py:232
  64.8 2.7 %collective-permute-done.14.refs_1_ = f32[160,128]{1,0:T(8,128)S(1)} collective-permute-done((f32[160,128]{1,0:T(8,128)S(1)}, f32[160,128]{1,0:T(8,128)S(1)}, u32[]{:S(2)}, u32[]{:S(2)}) %collective-permute-start.14) | collective-permute-done | bytes 81952 | tf_op jit(solution)/shard_map/ppermute | solution.py:232
  68.1 1.3 %collective-permute-start.18 = (f32[160,128]{1,0:T(8,128)S(1)}, f32[160,128]{1,0:T(8,128)S(1)}, u32[]{:S(2)}, u32[]{:S(2)}) collective-permute-start(f32[160,128]{1,0:T(8,128)S(1)} %shard_map.52), channel_id=1, source_target_pairs={{0,16},{2,18},{4,20},{6,22},{8,24},{10,26},{12,28},{14,30},{16,0},... | collective-permute-start | bytes 245768 | tf_op jit(solution)/shard_map/ppermute | solution.py:232
  69.4 3.0 %collective-permute-start.19 = (f32[160,128]{1,0:T(8,128)S(1)}, f32[160,128]{1,0:T(8,128)S(1)}, u32[]{:S(2)}, u32[]{:S(2)}) collective-permute-start(f32[160,128]{1,0:T(8,128)S(1)} %shard_map.52), channel_id=1, source_target_pairs={{0,24},{2,26},{4,28},{6,30},{8,16},{10,18},{12,20},{14,22},{16,8},... | collective-permute-start | bytes 245768 | tf_op jit(solution)/shard_map/ppermute | solution.py:232
  73.1 4.4 %collective-permute-done.18 = f32[160,128]{1,0:T(8,128)S(1)} collective-permute-done((f32[160,128]{1,0:T(8,128)S(1)}, f32[160,128]{1,0:T(8,128)S(1)}, u32[]{:S(2)}, u32[]{:S(2)}) %collective-permute-start.18) | collective-permute-done | bytes 81952 | tf_op jit(solution)/shard_map/ppermute | solution.py:232
  79.4 1.7 %collective-permute-start.22 = (f32[160,128]{1,0:T(8,128)S(1)}, f32[160,128]{1,0:T(8,128)S(1)}, u32[]{:S(2)}, u32[]{:S(2)}) collective-permute-start(f32[160,128]{1,0:T(8,128)S(1)} %get-tuple-element.56), channel_id=1, source_target_pairs={{0,2},{2,0},{4,6},{6,4},{8,10},{10,8},{12,14},{14,12},{16,18},{18,... | collective-permute-start | bytes 245768 | tf_op jit(solution)/shard_map/ppermute | solution.py:232
  81.1 1.9 %collective-permute-done.20 = f32[160,128]{1,0:T(8,128)S(1)} collective-permute-done((f32[160,128]{1,0:T(8,128)S(1)}, f32[160,128]{1,0:T(8,128)S(1)}, u32[]{:S(2)}, u32[]{:S(2)}) %collective-permute-start.20) | collective-permute-done | bytes 81952 | tf_op jit(solution)/shard_map/ppermute | solution.py:232
  84.1 1.5 %collective-permute-done.23 = f32[640,128]{1,0:T(8,128)S(1)} collective-permute-done((f32[640,128]{1,0:T(8,128)S(1)}, f32[640,128]{1,0:T(8,128)S(1)}, u32[]{:S(2)}, u32[]{:S(2)}) %collective-permute-start.23) | collective-permute-done | bytes 327712 | tf_op jit(solution)/shard_map/ppermute | solution.py:232
  85.6 16.0 %shard_map.53 = f32[49,7,512]{2,1,0:T(8,128)} custom-call(f32[1280,128]{1,0:T(8,128)S(1)} %bitcast.20, f32[392,512]{1,0:T(8,128)S(1)} %copy-done.1), custom_call_target="tpu_custom_call" | custom-call | flops 134217728 | bytes 1048576 | tf_op jit(solution)/shard_map/pallas_call | solution.py:40
  (63 shorter events, 10.2 us)
Async XLA Ops:
  0.9 9.4 %collective-permute-start = (f32[1,7,7,512]{3,2,1,0:T(8,128)S(1)}, f32[1,7,7,512]{3,2,1,0:T(8,128)S(1)}, u32[]{:S(2)}, u32[]{:S(2)}) collective-permute-start(f32[1,7,7,512]{3,2,1,0:T(8,128)S(1)} %slice.9), channel_id=1, source_target_pairs={{0,30},{2,0},{4,2},{6,4},{8,6},{10,8},{12,10},{14,12},{16,14},{18,... | collective-permute-start | bytes 301064 | tf_op jit(solution)/shard_map/ppermute | solution.py:514
  10.4 1.4 %collective-permute-start.1 = (f32[8,1,7,512]{3,2,1,0:T(8,128)S(1)}, f32[8,1,7,512]{3,2,1,0:T(8,128)S(1)}, u32[]{:S(2)}, u32[]{:S(2)}) collective-permute-start(f32[8,1,7,512]{3,2,1,0:T(8,128)S(1)} %pad_maximum_fusion), channel_id=1, source_target_pairs={{0,1},{1,0},{2,3},{3,2},{4,5},{5,4},{6,7},{7,6},{8,9},{9,8},{10,11... | collective-permute-start | bytes 344072 | tf_op jit(solution)/shard_map/ppermute | solution.py:514
  12.3 1.7 %collective-permute-start.2 = (f32[2,8,8,512]{3,2,1,0:T(8,128)S(1)}, f32[2,8,8,512]{3,2,1,0:T(8,128)S(1)}, u32[]{:S(2)}, u32[]{:S(2)}) collective-permute-start(f32[2,8,8,512]{3,2,1,0:T(8,128)S(1)} %get-tuple-element.31), channel_id=1, source_target_pairs={{0,1},{1,0},{2,3},{3,2},{4,5},{5,4},{6,7},{7,6},{8,9},{9,8},{10,11... | collective-permute-start | bytes 786440 | tf_op jit(solution)/shard_map/ppermute | solution.py:514
  14.1 9.8 %collective-permute-start.3 = (f32[56,512]{1,0:T(8,128)S(1)}, f32[56,512]{1,0:T(8,128)S(1)}, u32[]{:S(2)}, u32[]{:S(2)}) collective-permute-start(f32[56,512]{1,0:T(8,128)S(1)} %shard_map.40), channel_id=1, source_target_pairs={{0,2},{2,4},{4,6},{6,8},{8,10},{10,12},{12,14},{14,16},{16,18},{18... | collective-permute-start | bytes 344072 | tf_op jit(solution)/shard_map/ppermute | solution.py:514
  14.1 9.8 %collective-permute-start.4 = (f32[56,512]{1,0:T(8,128)S(1)}, f32[56,512]{1,0:T(8,128)S(1)}, u32[]{:S(2)}, u32[]{:S(2)}) collective-permute-start(f32[56,512]{1,0:T(8,128)S(1)} %shard_map.39.refs_0_), channel_id=1, source_target_pairs={{0,30},{2,0},{4,2},{6,4},{8,6},{10,8},{12,10},{14,12},{16,14},{18,... | collective-permute-start | bytes 344072 | tf_op jit(solution)/shard_map/ppermute | solution.py:514
  24.5 1.6 %collective-permute-start.5 = (f32[2,8,8,512]{3,2,1,0:T(8,128)S(1)}, f32[2,8,8,512]{3,2,1,0:T(8,128)S(1)}, u32[]{:S(2)}, u32[]{:S(2)}) collective-permute-start(f32[2,8,8,512]{3,2,1,0:T(8,128)S(1)} %get-tuple-element.36), channel_id=1, source_target_pairs={{0,1},{1,0},{2,3},{3,2},{4,5},{5,4},{6,7},{7,6},{8,9},{9,8},{10,11... | collective-permute-start | bytes 786440 | tf_op jit(solution)/shard_map/ppermute | solution.py:514
  26.1 8.9 %collective-permute-start.6 = (f32[56,512]{1,0:T(8,128)S(1)}, f32[56,512]{1,0:T(8,128)S(1)}, u32[]{:S(2)}, u32[]{:S(2)}) collective-permute-start(f32[56,512]{1,0:T(8,128)S(1)} %shard_map.43), channel_id=1, source_target_pairs={{0,2},{2,4},{4,6},{6,8},{8,10},{10,12},{12,14},{14,16},{16,18},{18... | collective-permute-start | bytes 344072 | tf_op jit(solution)/shard_map/ppermute | solution.py:514
  26.2 8.8 %collective-permute-start.7 = (f32[56,512]{1,0:T(8,128)S(1)}, f32[56,512]{1,0:T(8,128)S(1)}, u32[]{:S(2)}, u32[]{:S(2)}) collective-permute-start(f32[56,512]{1,0:T(8,128)S(1)} %shard_map.42.refs_0_), channel_id=1, source_target_pairs={{0,30},{2,0},{4,2},{6,4},{8,6},{10,8},{12,10},{14,12},{16,14},{18,... | collective-permute-start | bytes 344072 | tf_op jit(solution)/shard_map/ppermute | solution.py:514
  35.6 1.6 %collective-permute-start.8 = (f32[2,8,8,512]{3,2,1,0:T(8,128)S(1)}, f32[2,8,8,512]{3,2,1,0:T(8,128)S(1)}, u32[]{:S(2)}, u32[]{:S(2)}) collective-permute-start(f32[2,8,8,512]{3,2,1,0:T(8,128)S(1)} %get-tuple-element.41), channel_id=1, source_target_pairs={{0,1},{1,0},{2,3},{3,2},{4,5},{5,4},{6,7},{7,6},{8,9},{9,8},{10,11... | collective-permute-start | bytes 786440 | tf_op jit(solution)/shard_map/ppermute | solution.py:514
  37.3 8.9 %collective-permute-start.9 = (f32[56,512]{1,0:T(8,128)S(1)}, f32[56,512]{1,0:T(8,128)S(1)}, u32[]{:S(2)}, u32[]{:S(2)}) collective-permute-start(f32[56,512]{1,0:T(8,128)S(1)} %shard_map.46), channel_id=1, source_target_pairs={{0,2},{2,4},{4,6},{6,8},{8,10},{10,12},{12,14},{14,16},{16,18},{18... | collective-permute-start | bytes 344072 | tf_op jit(solution)/shard_map/ppermute | solution.py:514
  37.4 8.8 %collective-permute-start.10 = (f32[56,512]{1,0:T(8,128)S(1)}, f32[56,512]{1,0:T(8,128)S(1)}, u32[]{:S(2)}, u32[]{:S(2)}) collective-permute-start(f32[56,512]{1,0:T(8,128)S(1)} %shard_map.45.refs_0_), channel_id=1, source_target_pairs={{0,30},{2,0},{4,2},{6,4},{8,6},{10,8},{12,10},{14,12},{16,14},{18,... | collective-permute-start | bytes 344072 | tf_op jit(solution)/shard_map/ppermute | solution.py:514
  46.9 1.4 %collective-permute-start.11 = (f32[1,8,8,512]{3,2,1,0:T(8,128)S(1)}, f32[1,8,8,512]{3,2,1,0:T(8,128)S(1)}, u32[]{:S(2)}, u32[]{:S(2)}) collective-permute-start(f32[1,8,8,512]{3,2,1,0:T(8,128)S(1)} %get-tuple-element.46), channel_id=1, source_target_pairs={{0,1},{1,0},{2,3},{3,2},{4,5},{5,4},{6,7},{7,6},{8,9},{9,8},{10,11... | collective-permute-start | bytes 393224 | tf_op jit(solution)/shard_map/ppermute | solution.py:514
  48.3 8.9 %collective-permute-start.12 = (f32[56,512]{1,0:T(8,128)S(1)}, f32[56,512]{1,0:T(8,128)S(1)}, u32[]{:S(2)}, u32[]{:S(2)}) collective-permute-start(f32[56,512]{1,0:T(8,128)S(1)} %shard_map.48), channel_id=1, source_target_pairs={{0,2},{2,4},{4,6},{6,8},{8,10},{10,12},{12,14},{14,16},{16,18},{18... | collective-permute-start | bytes 344072 | tf_op jit(solution)/shard_map/ppermute | solution.py:514
  59.2 1.9 %collective-permute-start.13 = (f32[640,128]{1,0:T(8,128)}, f32[640,128]{1,0:T(8,128)S(1)}, u32[]{:S(2)}, u32[]{:S(2)}) collective-permute-start(f32[640,128]{1,0:T(8,128)} %get-tuple-element.50), channel_id=1, source_target_pairs={{0,1},{1,0},{2,3},{3,2},{4,5},{5,4},{6,7},{7,6},{8,9},{9,8},{10,11... | collective-permute-start | bytes 983048 | tf_op jit(solution)/shard_map/ppermute | solution.py:232
  61.3 6.3 %collective-permute-start.14 = (f32[160,128]{1,0:T(8,128)S(1)}, f32[160,128]{1,0:T(8,128)S(1)}, u32[]{:S(2)}, u32[]{:S(2)}) collective-permute-start(f32[160,128]{1,0:T(8,128)S(1)} %get-tuple-element.52), channel_id=1, source_target_pairs={{0,6},{2,4},{4,2},{6,0},{8,14},{10,12},{12,10},{14,8},{16,22},{18,... | collective-permute-start | bytes 245768 | tf_op jit(solution)/shard_map/ppermute | solution.py:232
  61.3 6.6 %collective-permute-start.15 = (f32[160,128]{1,0:T(8,128)S(1)}, f32[160,128]{1,0:T(8,128)S(1)}, u32[]{:S(2)}, u32[]{:S(2)}) collective-permute-start(f32[160,128]{1,0:T(8,128)S(1)} %get-tuple-element.53), channel_id=1, source_target_pairs={{0,4},{2,6},{4,0},{6,2},{8,12},{10,14},{12,8},{14,10},{16,20},{18,... | collective-permute-start | bytes 245768 | tf_op jit(solution)/shard_map/ppermute | solution.py:232
  61.4 6.6 %collective-permute-start.16 = (f32[160,128]{1,0:T(8,128)S(1)}, f32[160,128]{1,0:T(8,128)S(1)}, u32[]{:S(2)}, u32[]{:S(2)}) collective-permute-start(f32[160,128]{1,0:T(8,128)S(1)} %get-tuple-element.54), channel_id=1, source_target_pairs={{0,2},{2,0},{4,6},{6,4},{8,10},{10,8},{12,14},{14,12},{16,18},{18,... | collective-permute-start | bytes 245768 | tf_op jit(solution)/shard_map/ppermute | solution.py:232
  68.0 5.1 %collective-permute-start.17 = (f32[160,128]{1,0:T(8,128)S(1)}, f32[160,128]{1,0:T(8,128)S(1)}, u32[]{:S(2)}, u32[]{:S(2)}) collective-permute-start(f32[160,128]{1,0:T(8,128)S(1)} %shard_map.52), channel_id=1, source_target_pairs={{0,8},{2,10},{4,12},{6,14},{8,0},{10,2},{12,4},{14,6},{16,24},{18,... | collective-permute-start | bytes 245768 | tf_op jit(solution)/shard_map/ppermute | solution.py:232
  68.1 9.4 %collective-permute-start.18 = (f32[160,128]{1,0:T(8,128)S(1)}, f32[160,128]{1,0:T(8,128)S(1)}, u32[]{:S(2)}, u32[]{:S(2)}) collective-permute-start(f32[160,128]{1,0:T(8,128)S(1)} %shard_map.52), channel_id=1, source_target_pairs={{0,16},{2,18},{4,20},{6,22},{8,24},{10,26},{12,28},{14,30},{16,0},... | collective-permute-start | bytes 245768 | tf_op jit(solution)/shard_map/ppermute | solution.py:232
  69.4 8.1 %collective-permute-start.19 = (f32[160,128]{1,0:T(8,128)S(1)}, f32[160,128]{1,0:T(8,128)S(1)}, u32[]{:S(2)}, u32[]{:S(2)}) collective-permute-start(f32[160,128]{1,0:T(8,128)S(1)} %shard_map.52), channel_id=1, source_target_pairs={{0,24},{2,26},{4,28},{6,30},{8,16},{10,18},{12,20},{14,22},{16,8},... | collective-permute-start | bytes 245768 | tf_op jit(solution)/shard_map/ppermute | solution.py:232
  77.6 5.5 %collective-permute-start.20 = (f32[160,128]{1,0:T(8,128)S(1)}, f32[160,128]{1,0:T(8,128)S(1)}, u32[]{:S(2)}, u32[]{:S(2)}) collective-permute-start(f32[160,128]{1,0:T(8,128)S(1)} %get-tuple-element.56), channel_id=1, source_target_pairs={{0,6},{2,4},{4,2},{6,0},{8,14},{10,12},{12,10},{14,8},{16,22},{18,... | collective-permute-start | bytes 245768 | tf_op jit(solution)/shard_map/ppermute | solution.py:232
  78.7 5.1 %collective-permute-start.21 = (f32[160,128]{1,0:T(8,128)S(1)}, f32[160,128]{1,0:T(8,128)S(1)}, u32[]{:S(2)}, u32[]{:S(2)}) collective-permute-start(f32[160,128]{1,0:T(8,128)S(1)} %get-tuple-element.56), channel_id=1, source_target_pairs={{0,4},{2,6},{4,0},{6,2},{8,12},{10,14},{12,8},{14,10},{16,20},{18,... | collective-permute-start | bytes 245768 | tf_op jit(solution)/shard_map/ppermute | solution.py:232
  79.4 4.4 %collective-permute-start.22 = (f32[160,128]{1,0:T(8,128)S(1)}, f32[160,128]{1,0:T(8,128)S(1)}, u32[]{:S(2)}, u32[]{:S(2)}) collective-permute-start(f32[160,128]{1,0:T(8,128)S(1)} %get-tuple-element.56), channel_id=1, source_target_pairs={{0,2},{2,0},{4,6},{6,4},{8,10},{10,8},{12,14},{14,12},{16,18},{18,... | collective-permute-start | bytes 245768 | tf_op jit(solution)/shard_map/ppermute | solution.py:232
  83.9 1.7 %collective-permute-start.23 = (f32[640,128]{1,0:T(8,128)S(1)}, f32[640,128]{1,0:T(8,128)S(1)}, u32[]{:S(2)}, u32[]{:S(2)}) collective-permute-start(f32[640,128]{1,0:T(8,128)S(1)} %bitcast.22), channel_id=1, source_target_pairs={{0,1},{1,0},{2,3},{3,2},{4,5},{5,4},{6,7},{7,6},{8,9},{9,8},{10,11... | collective-permute-start | bytes 983048 | tf_op jit(solution)/shard_map/ppermute | solution.py:232
  (5 other events, 32.3 us)

commit v7 on v6

--- a/solution.py
+++ b/solution.py
@@ -170,7 +170,7 @@
     }
 
 
-def half_correlation(which, values, out):
+def half_correlation(which, values, out, sofar=None):
     width = values.shape[1]
     half_rows = out.shape[0]
     high = values.astype(jnp.bfloat16)
@@ -192,39 +192,72 @@
             product(high[:, rows], low[:, cols]) + product(low[:, rows], high[:, cols])
         ) + product(high[:, rows], high[:, cols])
         for n, (_, at) in enumerate(found):
-            out[at : at + LANES] = strip[:, n * LANES : (n + 1) * LANES]
-
-
-def chosen_half(number, values, out):
+            block = strip[:, n * LANES : (n + 1) * LANES]
+            if sofar is not None:
+                block = block + sofar[at : at + LANES]
+            out[at : at + LANES] = block
+
+
+def chosen_half(number, values, out, sofar=None):
     for which in range(2):
 
         @pl.when(number == which)
         def _():
-            half_correlation(which, values[...], out)
-
-
-def last_body(
-    mine, image_in, y_face, x_low, current, previous, stored, other, work, own, sem, *, alpha, beta
-):
-    edge = image_in.shape[0]
-    width = image_in.shape[3]
-    work[...] = image_in[...]
-    got = updated(work, y_face, x_low, None, current, previous, alpha, beta)
-    got = got[: edge - 1, : edge - 1]
-    where = lax.broadcasted_iota(jnp.int32, got.shape, 2)
-    got = jnp.where(where == edge - 1, 0.0, got)
-    own[...] = got.reshape((edge - 1) ** 2 * edge, width)
+            half_correlation(which, values[...], out, sofar)
+
+
+def last_planes(image, x_low, current, previous, y_face, planes, alpha, beta):
+    center = (band_low + band_high) / 2.0
+    order_now = image.shape[0] - 1
+    width = image.shape[3]
+    rows = []
+    for a in planes:
+        summed_up = image[a, :order_now]
+        first = summed_up[:1] + y_face[0, a][None]
+        if a == 0:
+            first = first + spread_plane(x_low, 0, order_now)[None]
+            others = [
+                summed_up[b : b + 1] + spread_plane(x_low, b, order_now)[None]
+                for b in range(1, order_now)
+            ]
+            summed_up = jnp.concatenate([first] + others, axis=0)
+        else:
+            summed_up = jnp.concatenate([first, summed_up[1:]], axis=0)
+        got = (summed_up - center * current[a, :order_now]) * alpha
+        got = got - beta * previous[a, :order_now]
+        where = lax.broadcasted_iota(jnp.int32, got.shape, 1)
+        got = jnp.where(where == order_now, 0.0, got)
+        rows.append(got.reshape(order_now * (order_now + 1), width))
+    return rows
+
+
+def spread_plane(received, b, order_now):
+    first = order_now * b
+    return jnp.concatenate(
+        [received[first : first + order_now], received[first : first + 1]], axis=0
+    )
+
+
+def inner_body(mine, image, y_face, current, previous, stored, other, kept, own, sem, *, alpha, beta):
+    edge = image.shape[0]
+    planes = range(1, edge - 1)
+    found = last_planes(image, None, current, previous, y_face, planes, alpha, beta)
+    own[...] = jnp.concatenate(found, axis=0)
     keep = pltpu.make_async_copy(own, stored, sem)
     keep.start()
     chosen_half(1 - mine[0], own, other)
+    chosen_half(mine[0], own, kept)
     keep.wait()
 
 
-def kept_body(mine, stored, half, own, sem):
-    load = pltpu.make_async_copy(stored, own, sem)
-    load.start()
-    load.wait()
-    chosen_half(mine[0], own, half)
+def last_body(mine, image, y_face, x_low, current, previous, sofar, own, other, *, alpha, beta):
+    (found,) = last_planes(image, x_low, current, previous, y_face, (0,), alpha, beta)
+    own[...] = found
+    chosen_half(1 - mine[0], own, other, sofar)
+
+
+def kept_body(mine, own, sofar, kept):
+    chosen_half(mine[0], own, kept, sofar)
 
 
 def swap(block, axis, distance):
@@ -407,10 +440,11 @@
     yield jnp.concatenate(done, axis=0)
 
 
-def ortho_body(corr, own, out, blocks, rest, done, sent, sems, *, root_nodes):
-    width = own.shape[1]
+def ortho_body(corr, first, inner, out, blocks, rest, done, sent, sems, *, root_nodes):
+    width = first.shape[1]
     count = width // LANES
-    nodes = own.shape[0]
+    plane = first.shape[0]
+    nodes = plane + inner.shape[0]
     part = nodes // PARTS
 
     def span(k):
@@ -450,7 +484,9 @@
             if j > 0:
                 blocks[n] = piece(i, j)
         for j in range(count):
-            rest[:, span(j)] = own[:, span(j)] * (over_col[j] * root_nodes)
+            over = over_col[j] * root_nodes
+            rest[:plane, span(j)] = first[:, span(j)] * over
+            rest[plane:, span(j)] = inner[:, span(j)] * over
 
     def store(k):
         return pltpu.make_async_copy(sent.at[k], out.at[:, :, span(k)], sems.at[k])
@@ -587,31 +623,29 @@
     rows = cut_rows(blocks * (blocks + 1) // 2 * LANES)
     first_stage = all_stages()[0]
     assert first_stage[2] == 2
-    block_shape, half_shape = f32(order_now**2 * edge, width), f32(rows // 2, LANES)
-    half_flops = 3 * cell_nodes * width**2
-    stored, other = vmem_call(
-        functools.partial(last_body, alpha=alpha, beta=beta),
-        (block_shape, half_shape),
+    plane_rows = order_now * edge
+    inner_shape = f32((order_now - 1) * plane_rows, width)
+    half_shape = f32(rows // 2, LANES)
+    stored, other, kept = vmem_call(
+        functools.partial(inner_body, alpha=alpha, beta=beta),
+        (inner_shape, half_shape, half_shape),
         scratch=[
-            pltpu.VMEM(box.shape, jnp.float32),
-            pltpu.VMEM(block_shape.shape, jnp.float32),
+            pltpu.VMEM(inner_shape.shape, jnp.float32),
             pltpu.SemaphoreType.DMA,
         ],
-        flops=half_flops,
+        flops=6 * cell_nodes * width**2,
         scalars=1,
         hbm_out=(0,),
-    )(digit(first_stage), image, y_low, x_low, current, previous)
+    )(digit(first_stage), image, y_low, current, previous)
+    own, other = vmem_call(
+        functools.partial(last_body, alpha=alpha, beta=beta),
+        (f32(plane_rows, width), half_shape),
+        flops=6 * plane_rows * width**2,
+        scalars=1,
+    )(digit(first_stage), image, y_low, x_low, current, previous, other)
     (kept,) = vmem_call(
-        kept_body,
-        (half_shape,),
-        scratch=[
-            pltpu.VMEM(block_shape.shape, jnp.float32),
-            pltpu.SemaphoreType.DMA,
-        ],
-        flops=half_flops,
-        scalars=1,
-        hbm_in=(1,),
-    )(digit(first_stage), stored)
+        kept_body, (half_shape,), flops=6 * plane_rows * width**2, scalars=1
+    )(digit(first_stage), own, kept)
 
     nodes = order_now**3 * lax.axis_size("wide") * lax.axis_size("narrow")
     corr = summed(kept, other)
@@ -620,14 +654,14 @@
         (f32(order_now**2, order_now, width),),
         scratch=[
             pltpu.VMEM((blocks * (blocks + 1) // 2, LANES, LANES), jnp.float32),
-            pltpu.VMEM(block_shape.shape, jnp.float32),
-            pltpu.VMEM((block_shape.shape[0], LANES), jnp.float32),
+            pltpu.VMEM((order_now * plane_rows, width), jnp.float32),
+            pltpu.VMEM((order_now * plane_rows, LANES), jnp.float32),
             pltpu.VMEM((blocks, order_now**2, order_now, LANES), jnp.float32),
             pltpu.SemaphoreType.DMA((blocks,)),
         ],
         flops=width**3,
         hbm_out=(0,),
-    )(corr, stored)
+    )(corr, own, stored)
     return out.reshape(orbitals.shape)
 
 

time: 102 us -> 101 us (level)
  waiting for transfers between devices: 39.5 us -> 38.3 us
  Pallas kernels: 23.4 us -> 22.3 us
    ppermute x13, waiting for transfers between devices: 27 us -> 25.9 us  [to_next(): lax.ppermute(block, axis, [(i, (i + distance) % count) for i in range(cou...]
    pallas_call x17 -> x18, Pallas kernels: 23.4 us -> 22.3 us  [call(): pl.pallas_call(body, out_shape=outs, in_specs=[pl.BlockSpec(memory_space=...]
  transfers between devices with their start and end apart: 24 -> 24, of which waited for: 17 -> 19; matrix products, arithmetic and copies ran while one was open for 0% -> 0% of each run, Pallas kernels for 3% -> 3%
where the time goes in v7:
time: 101 us; the launch traced here: 100 us
  waiting for transfers between devices  38.3 us (38%)
  starting transfers between devices  37.1 us (37%)
  Pallas kernels  22.3 us (22%)
  local copies, waits for them, and re-layouts  2.22 us (2%)
    ppermute x13, waiting for transfers between devices, to_next(): lax.ppermute(block, axis, [(i, (i + distance) % count) for i in range(cou...  25.9 us
    ppermute x13, starting transfers between devices, to_next(): lax.ppermute(block, axis, [(i, (i + distance) % count) for i in range(cou...  25.4 us
    pallas_call x18, Pallas kernels, call(): pl.pallas_call(body, out_shape=outs, in_specs=[pl.BlockSpec(memory_space=...  22.3 us
    ppermute x11, waiting for transfers between devices, swap(): return lax.ppermute(block, axis, [(i, i ^ distance) for i in range(count)])  12.4 us
    ppermute x11, starting transfers between devices, swap(): return lax.ppermute(block, axis, [(i, i ^ distance) for i in range(count)])  11.7 us
  transfers between devices with their start and end apart: 24, of which 19 were waited for; matrix products, arithmetic and copies ran while one was open for 0% of the time, Pallas kernels for 3%

profile of v7, /device:TPU:0, one launch (start us, length us, event | category | flops | bytes accessed | tf_op | source)
XLA Modules:
  0.0 100.4 jit_solution(13254408560589534780)
XLA Ops:
  0.9 7.0 %collective-permute-start = (f32[1,7,7,512]{3,2,1,0:T(8,128)S(1)}, f32[1,7,7,512]{3,2,1,0:T(8,128)S(1)}, u32[]{:S(2)}, u32[]{:S(2)}) collective-permute-start(f32[1,7,7,512]{3,2,1,0:T(8,128)S(1)} %slice.9), channel_id=1, source_target_pairs={{0,30},{2,0},{4,2},{6,4},{8,6},{10,8},{12,10},{14,12},{16,14},{18,... | collective-permute-start | bytes 301064 | tf_op jit(solution)/shard_map/ppermute | solution.py:550
  7.9 2.4 %collective-permute-done.x_next = f32[1,7,7,512]{3,2,1,0:T(8,128)S(1)} collective-permute-done((f32[1,7,7,512]{3,2,1,0:T(8,128)S(1)}, f32[1,7,7,512]{3,2,1,0:T(8,128)S(1)}, u32[]{:S(2)}, u32[]{:S(2)}) %collective-permute-start) | collective-permute-done | bytes 100384 | tf_op jit(solution)/shard_map/ppermute | solution.py:550
  12.9 1.2 %collective-permute-done.2.y_faces.refs_1_ = f32[2,8,8,512]{3,2,1,0:T(8,128)S(1)} collective-permute-done((f32[2,8,8,512]{3,2,1,0:T(8,128)S(1)}, f32[2,8,8,512]{3,2,1,0:T(8,128)S(1)}, u32[]{:S(2)}, u32[]{:S(2)}) %collective-permute-start.2) | collective-permute-done | bytes 262176 | tf_op jit(solution)/shard_map/ppermute | solution.py:550
  14.1 6.1 %collective-permute-start.4 = (f32[56,512]{1,0:T(8,128)S(1)}, f32[56,512]{1,0:T(8,128)S(1)}, u32[]{:S(2)}, u32[]{:S(2)}) collective-permute-start(f32[56,512]{1,0:T(8,128)S(1)} %shard_map.39.refs_0_), channel_id=1, source_target_pairs={{0,30},{2,0},{4,2},{6,4},{8,6},{10,8},{12,10},{14,12},{16,14},{18,... | collective-permute-start | bytes 344072 | tf_op jit(solution)/shard_map/ppermute | solution.py:550
  20.3 3.6 %collective-permute-done.3.refs_2_ = f32[56,512]{1,0:T(8,128)S(1)} collective-permute-done((f32[56,512]{1,0:T(8,128)S(1)}, f32[56,512]{1,0:T(8,128)S(1)}, u32[]{:S(2)}, u32[]{:S(2)}) %collective-permute-start.3) | collective-permute-done | bytes 114720 | tf_op jit(solution)/shard_map/ppermute | solution.py:550
  24.5 1.5 %collective-permute-done.5.y_faces.refs_1_ = f32[2,8,8,512]{3,2,1,0:T(8,128)S(1)} collective-permute-done((f32[2,8,8,512]{3,2,1,0:T(8,128)S(1)}, f32[2,8,8,512]{3,2,1,0:T(8,128)S(1)}, u32[]{:S(2)}, u32[]{:S(2)}) %collective-permute-start.5) | collective-permute-done | bytes 262176 | tf_op jit(solution)/shard_map/ppermute | solution.py:550
  26.2 5.6 %collective-permute-start.7 = (f32[56,512]{1,0:T(8,128)S(1)}, f32[56,512]{1,0:T(8,128)S(1)}, u32[]{:S(2)}, u32[]{:S(2)}) collective-permute-start(f32[56,512]{1,0:T(8,128)S(1)} %shard_map.42.refs_0_), channel_id=1, source_target_pairs={{0,30},{2,0},{4,2},{6,4},{8,6},{10,8},{12,10},{14,12},{16,14},{18,... | collective-permute-start | bytes 344072 | tf_op jit(solution)/shard_map/ppermute | solution.py:550
  31.8 3.2 %collective-permute-done.6.refs_2_ = f32[56,512]{1,0:T(8,128)S(1)} collective-permute-done((f32[56,512]{1,0:T(8,128)S(1)}, f32[56,512]{1,0:T(8,128)S(1)}, u32[]{:S(2)}, u32[]{:S(2)}) %collective-permute-start.6) | collective-permute-done | bytes 114720 | tf_op jit(solution)/shard_map/ppermute | solution.py:550
  35.7 1.5 %collective-permute-done.8.y_faces.refs_1_ = f32[2,8,8,512]{3,2,1,0:T(8,128)S(1)} collective-permute-done((f32[2,8,8,512]{3,2,1,0:T(8,128)S(1)}, f32[2,8,8,512]{3,2,1,0:T(8,128)S(1)}, u32[]{:S(2)}, u32[]{:S(2)}) %collective-permute-start.8) | collective-permute-done | bytes 262176 | tf_op jit(solution)/shard_map/ppermute | solution.py:550
  37.4 5.6 %collective-permute-start.10 = (f32[56,512]{1,0:T(8,128)S(1)}, f32[56,512]{1,0:T(8,128)S(1)}, u32[]{:S(2)}, u32[]{:S(2)}) collective-permute-start(f32[56,512]{1,0:T(8,128)S(1)} %shard_map.45.refs_0_), channel_id=1, source_target_pairs={{0,30},{2,0},{4,2},{6,4},{8,6},{10,8},{12,10},{14,12},{16,14},{18,... | collective-permute-start | bytes 344072 | tf_op jit(solution)/shard_map/ppermute | solution.py:550
  43.0 3.2 %collective-permute-done.9.refs_2_ = f32[56,512]{1,0:T(8,128)S(1)} collective-permute-done((f32[56,512]{1,0:T(8,128)S(1)}, f32[56,512]{1,0:T(8,128)S(1)}, u32[]{:S(2)}, u32[]{:S(2)}) %collective-permute-start.9) | collective-permute-done | bytes 114720 | tf_op jit(solution)/shard_map/ppermute | solution.py:550
  46.9 1.3 %collective-permute-done.11.y_faces.y_face = f32[1,8,8,512]{3,2,1,0:T(8,128)S(1)} collective-permute-done((f32[1,8,8,512]{3,2,1,0:T(8,128)S(1)}, f32[1,8,8,512]{3,2,1,0:T(8,128)S(1)}, u32[]{:S(2)}, u32[]{:S(2)}) %collective-permute-start.11) | collective-permute-done | bytes 131104 | tf_op jit(solution)/shard_map/ppermute | solution.py:550
  48.4 1.2 %shard_map.49 = (f32[336,512]{1,0:T(8,128)}, f32[640,128]{1,0:T(8,128)S(1)}, f32[640,128]{1,0:T(8,128)S(1)}) custom-call(s32[1]{0:T(128)} %bitcast.1.mine, f32[8,8,8,512]{3,2,1,0:T(8,128)S(1)} %get-tuple-element.48.image, f32[1,8,8,512]{3,2,1,0:T(8,128)S(1)} %collective-permute-done.11.y_faces.y_face, f32[8,8,8,512]{3,2,1,0:T(8,128)S(1)} %get-tuple-element.51.current, ...), custom_call_target="tpu_custom_call" | custom-call | flops 805306368 | bytes 1048576 | tf_op jit(solution)/shard_map/pallas_call | solution.py:40
  49.6 7.6 %collective-permute-done.12.x_low = f32[56,512]{1,0:T(8,128)S(1)} collective-permute-done((f32[56,512]{1,0:T(8,128)S(1)}, f32[56,512]{1,0:T(8,128)S(1)}, u32[]{:S(2)}, u32[]{:S(2)}) %collective-permute-start.12) | collective-permute-done | bytes 114720 | tf_op jit(solution)/shard_map/ppermute | solution.py:550
  57.2 1.1 %shard_map.50 = (f32[56,512]{1,0:T(8,128)S(1)}, f32[640,128]{1,0:T(8,128)}) custom-call(s32[1]{0:T(128)} %bitcast.1.mine, f32[8,8,8,512]{3,2,1,0:T(8,128)S(1)} %get-tuple-element.48.image, f32[1,8,8,512]{3,2,1,0:T(8,128)S(1)} %collective-permute-done.11.y_faces.y_face, f32[56,512]{1,0:T(8,128)S(1)} %collective-permute-done.12.x_low, ...), custom_call_target="tpu_custom_call" | custom-call | flops 88080384 | bytes 1048576 | tf_op jit(solution)/shard_map/pallas_call | solution.py:40
  60.4 3.4 %collective-permute-start.16 = (f32[160,128]{1,0:T(8,128)S(1)}, f32[160,128]{1,0:T(8,128)S(1)}, u32[]{:S(2)}, u32[]{:S(2)}) collective-permute-start(f32[160,128]{1,0:T(8,128)S(1)} %get-tuple-element.59), channel_id=1, source_target_pairs={{0,2},{2,0},{4,6},{6,4},{8,10},{10,8},{12,14},{14,12},{16,18},{18,... | collective-permute-start | bytes 245768 | tf_op jit(solution)/shard_map/ppermute | solution.py:265
  63.8 2.7 %collective-permute-done.14.refs_1_ = f32[160,128]{1,0:T(8,128)S(1)} collective-permute-done((f32[160,128]{1,0:T(8,128)S(1)}, f32[160,128]{1,0:T(8,128)S(1)}, u32[]{:S(2)}, u32[]{:S(2)}) %collective-permute-start.14) | collective-permute-done | bytes 81952 | tf_op jit(solution)/shard_map/ppermute | solution.py:265
  66.7 1.3 %collective-permute-start.18 = (f32[160,128]{1,0:T(8,128)S(1)}, f32[160,128]{1,0:T(8,128)S(1)}, u32[]{:S(2)}, u32[]{:S(2)}) collective-permute-start(f32[160,128]{1,0:T(8,128)S(1)} %shard_map.53), channel_id=1, source_target_pairs={{0,16},{2,18},{4,20},{6,22},{8,24},{10,26},{12,28},{14,30},{16,0},... | collective-permute-start | bytes 245768 | tf_op jit(solution)/shard_map/ppermute | solution.py:265
  68.1 3.0 %collective-permute-start.19 = (f32[160,128]{1,0:T(8,128)S(1)}, f32[160,128]{1,0:T(8,128)S(1)}, u32[]{:S(2)}, u32[]{:S(2)}) collective-permute-start(f32[160,128]{1,0:T(8,128)S(1)} %shard_map.53), channel_id=1, source_target_pairs={{0,24},{2,26},{4,28},{6,30},{8,16},{10,18},{12,20},{14,22},{16,8},... | collective-permute-start | bytes 245768 | tf_op jit(solution)/shard_map/ppermute | solution.py:265
  71.2 4.0 %collective-permute-done.18 = f32[160,128]{1,0:T(8,128)S(1)} collective-permute-done((f32[160,128]{1,0:T(8,128)S(1)}, f32[160,128]{1,0:T(8,128)S(1)}, u32[]{:S(2)}, u32[]{:S(2)}) %collective-permute-start.18) | collective-permute-done | bytes 81952 | tf_op jit(solution)/shard_map/ppermute | solution.py:265
  75.2 1.8 %collective-permute-start.20 = (f32[160,128]{1,0:T(8,128)S(1)}, f32[160,128]{1,0:T(8,128)S(1)}, u32[]{:S(2)}, u32[]{:S(2)}) collective-permute-start(f32[160,128]{1,0:T(8,128)S(1)} %get-tuple-element.62), channel_id=1, source_target_pairs={{0,6},{2,4},{4,2},{6,0},{8,14},{10,12},{12,10},{14,8},{16,22},{18,... | collective-permute-start | bytes 245768 | tf_op jit(solution)/shard_map/ppermute | solution.py:265
  78.8 1.8 %collective-permute-done.20 = f32[160,128]{1,0:T(8,128)S(1)} collective-permute-done((f32[160,128]{1,0:T(8,128)S(1)}, f32[160,128]{1,0:T(8,128)S(1)}, u32[]{:S(2)}, u32[]{:S(2)}) %collective-permute-start.20) | collective-permute-done | bytes 81952 | tf_op jit(solution)/shard_map/ppermute | solution.py:265
  82.7 1.5 %collective-permute-done.23 = f32[640,128]{1,0:T(8,128)S(1)} collective-permute-done((f32[640,128]{1,0:T(8,128)S(1)}, f32[640,128]{1,0:T(8,128)S(1)}, u32[]{:S(2)}, u32[]{:S(2)}) %collective-permute-start.23) | collective-permute-done | bytes 327712 | tf_op jit(solution)/shard_map/ppermute | solution.py:265
  84.2 16.0 %shard_map.54 = f32[49,7,512]{2,1,0:T(8,128)} custom-call(f32[1280,128]{1,0:T(8,128)S(1)} %bitcast.20, f32[56,512]{1,0:T(8,128)S(1)} %get-tuple-element.53.own.first, f32[336,512]{1,0:T(8,128)S(1)} %copy-done.1), custom_call_target="tpu_custom_call" | custom-call | flops 134217728 | bytes 1048576 | tf_op jit(solution)/shard_map/pallas_call | solution.py:40
  (68 shorter events, 12.1 us)
Async XLA Ops:
  0.9 9.4 %collective-permute-start = (f32[1,7,7,512]{3,2,1,0:T(8,128)S(1)}, f32[1,7,7,512]{3,2,1,0:T(8,128)S(1)}, u32[]{:S(2)}, u32[]{:S(2)}) collective-permute-start(f32[1,7,7,512]{3,2,1,0:T(8,128)S(1)} %slice.9), channel_id=1, source_target_pairs={{0,30},{2,0},{4,2},{6,4},{8,6},{10,8},{12,10},{14,12},{16,14},{18,... | collective-permute-start | bytes 301064 | tf_op jit(solution)/shard_map/ppermute | solution.py:550
  10.4 1.4 %collective-permute-start.1 = (f32[8,1,7,512]{3,2,1,0:T(8,128)S(1)}, f32[8,1,7,512]{3,2,1,0:T(8,128)S(1)}, u32[]{:S(2)}, u32[]{:S(2)}) collective-permute-start(f32[8,1,7,512]{3,2,1,0:T(8,128)S(1)} %pad_maximum_fusion), channel_id=1, source_target_pairs={{0,1},{1,0},{2,3},{3,2},{4,5},{5,4},{6,7},{7,6},{8,9},{9,8},{10,11... | collective-permute-start | bytes 344072 | tf_op jit(solution)/shard_map/ppermute | solution.py:550
  12.3 1.7 %collective-permute-start.2 = (f32[2,8,8,512]{3,2,1,0:T(8,128)S(1)}, f32[2,8,8,512]{3,2,1,0:T(8,128)S(1)}, u32[]{:S(2)}, u32[]{:S(2)}) collective-permute-start(f32[2,8,8,512]{3,2,1,0:T(8,128)S(1)} %get-tuple-element.34), channel_id=1, source_target_pairs={{0,1},{1,0},{2,3},{3,2},{4,5},{5,4},{6,7},{7,6},{8,9},{9,8},{10,11... | collective-permute-start | bytes 786440 | tf_op jit(solution)/shard_map/ppermute | solution.py:550
  14.1 9.8 %collective-permute-start.3 = (f32[56,512]{1,0:T(8,128)S(1)}, f32[56,512]{1,0:T(8,128)S(1)}, u32[]{:S(2)}, u32[]{:S(2)}) collective-permute-start(f32[56,512]{1,0:T(8,128)S(1)} %shard_map.40), channel_id=1, source_target_pairs={{0,2},{2,4},{4,6},{6,8},{8,10},{10,12},{12,14},{14,16},{16,18},{18... | collective-permute-start | bytes 344072 | tf_op jit(solution)/shard_map/ppermute | solution.py:550
  14.1 9.8 %collective-permute-start.4 = (f32[56,512]{1,0:T(8,128)S(1)}, f32[56,512]{1,0:T(8,128)S(1)}, u32[]{:S(2)}, u32[]{:S(2)}) collective-permute-start(f32[56,512]{1,0:T(8,128)S(1)} %shard_map.39.refs_0_), channel_id=1, source_target_pairs={{0,30},{2,0},{4,2},{6,4},{8,6},{10,8},{12,10},{14,12},{16,14},{18,... | collective-permute-start | bytes 344072 | tf_op jit(solution)/shard_map/ppermute | solution.py:550
  24.5 1.6 %collective-permute-start.5 = (f32[2,8,8,512]{3,2,1,0:T(8,128)S(1)}, f32[2,8,8,512]{3,2,1,0:T(8,128)S(1)}, u32[]{:S(2)}, u32[]{:S(2)}) collective-permute-start(f32[2,8,8,512]{3,2,1,0:T(8,128)S(1)} %get-tuple-element.39), channel_id=1, source_target_pairs={{0,1},{1,0},{2,3},{3,2},{4,5},{5,4},{6,7},{7,6},{8,9},{9,8},{10,11... | collective-permute-start | bytes 786440 | tf_op jit(solution)/shard_map/ppermute | solution.py:550
  26.1 8.9 %collective-permute-start.6 = (f32[56,512]{1,0:T(8,128)S(1)}, f32[56,512]{1,0:T(8,128)S(1)}, u32[]{:S(2)}, u32[]{:S(2)}) collective-permute-start(f32[56,512]{1,0:T(8,128)S(1)} %shard_map.43), channel_id=1, source_target_pairs={{0,2},{2,4},{4,6},{6,8},{8,10},{10,12},{12,14},{14,16},{16,18},{18... | collective-permute-start | bytes 344072 | tf_op jit(solution)/shard_map/ppermute | solution.py:550
  26.2 8.8 %collective-permute-start.7 = (f32[56,512]{1,0:T(8,128)S(1)}, f32[56,512]{1,0:T(8,128)S(1)}, u32[]{:S(2)}, u32[]{:S(2)}) collective-permute-start(f32[56,512]{1,0:T(8,128)S(1)} %shard_map.42.refs_0_), channel_id=1, source_target_pairs={{0,30},{2,0},{4,2},{6,4},{8,6},{10,8},{12,10},{14,12},{16,14},{18,... | collective-permute-start | bytes 344072 | tf_op jit(solution)/shard_map/ppermute | solution.py:550
  35.6 1.6 %collective-permute-start.8 = (f32[2,8,8,512]{3,2,1,0:T(8,128)S(1)}, f32[2,8,8,512]{3,2,1,0:T(8,128)S(1)}, u32[]{:S(2)}, u32[]{:S(2)}) collective-permute-start(f32[2,8,8,512]{3,2,1,0:T(8,128)S(1)} %get-tuple-element.44), channel_id=1, source_target_pairs={{0,1},{1,0},{2,3},{3,2},{4,5},{5,4},{6,7},{7,6},{8,9},{9,8},{10,11... | collective-permute-start | bytes 786440 | tf_op jit(solution)/shard_map/ppermute | solution.py:550
  37.3 8.9 %collective-permute-start.9 = (f32[56,512]{1,0:T(8,128)S(1)}, f32[56,512]{1,0:T(8,128)S(1)}, u32[]{:S(2)}, u32[]{:S(2)}) collective-permute-start(f32[56,512]{1,0:T(8,128)S(1)} %shard_map.46), channel_id=1, source_target_pairs={{0,2},{2,4},{4,6},{6,8},{8,10},{10,12},{12,14},{14,16},{16,18},{18... | collective-permute-start | bytes 344072 | tf_op jit(solution)/shard_map/ppermute | solution.py:550
  37.4 8.8 %collective-permute-start.10 = (f32[56,512]{1,0:T(8,128)S(1)}, f32[56,512]{1,0:T(8,128)S(1)}, u32[]{:S(2)}, u32[]{:S(2)}) collective-permute-start(f32[56,512]{1,0:T(8,128)S(1)} %shard_map.45.refs_0_), channel_id=1, source_target_pairs={{0,30},{2,0},{4,2},{6,4},{8,6},{10,8},{12,10},{14,12},{16,14},{18,... | collective-permute-start | bytes 344072 | tf_op jit(solution)/shard_map/ppermute | solution.py:550
  46.9 1.4 %collective-permute-start.11 = (f32[1,8,8,512]{3,2,1,0:T(8,128)S(1)}, f32[1,8,8,512]{3,2,1,0:T(8,128)S(1)}, u32[]{:S(2)}, u32[]{:S(2)}) collective-permute-start(f32[1,8,8,512]{3,2,1,0:T(8,128)S(1)} %get-tuple-element.49), channel_id=1, source_target_pairs={{0,1},{1,0},{2,3},{3,2},{4,5},{5,4},{6,7},{7,6},{8,9},{9,8},{10,11... | collective-permute-start | bytes 393224 | tf_op jit(solution)/shard_map/ppermute | solution.py:550
  48.3 8.9 %collective-permute-start.12 = (f32[56,512]{1,0:T(8,128)S(1)}, f32[56,512]{1,0:T(8,128)S(1)}, u32[]{:S(2)}, u32[]{:S(2)}) collective-permute-start(f32[56,512]{1,0:T(8,128)S(1)} %shard_map.48), channel_id=1, source_target_pairs={{0,2},{2,4},{4,6},{6,8},{8,10},{10,12},{12,14},{14,16},{16,18},{18... | collective-permute-start | bytes 344072 | tf_op jit(solution)/shard_map/ppermute | solution.py:550
  58.3 1.8 %collective-permute-start.13 = (f32[640,128]{1,0:T(8,128)}, f32[640,128]{1,0:T(8,128)S(1)}, u32[]{:S(2)}, u32[]{:S(2)}) collective-permute-start(f32[640,128]{1,0:T(8,128)} %get-tuple-element.55), channel_id=1, source_target_pairs={{0,1},{1,0},{2,3},{3,2},{4,5},{5,4},{6,7},{7,6},{8,9},{9,8},{10,11... | collective-permute-start | bytes 983048 | tf_op jit(solution)/shard_map/ppermute | solution.py:265
  60.2 6.3 %collective-permute-start.14 = (f32[160,128]{1,0:T(8,128)S(1)}, f32[160,128]{1,0:T(8,128)S(1)}, u32[]{:S(2)}, u32[]{:S(2)}) collective-permute-start(f32[160,128]{1,0:T(8,128)S(1)} %get-tuple-element.57), channel_id=1, source_target_pairs={{0,6},{2,4},{4,2},{6,0},{8,14},{10,12},{12,10},{14,8},{16,22},{18,... | collective-permute-start | bytes 245768 | tf_op jit(solution)/shard_map/ppermute | solution.py:265
  60.3 6.3 %collective-permute-start.15 = (f32[160,128]{1,0:T(8,128)S(1)}, f32[160,128]{1,0:T(8,128)S(1)}, u32[]{:S(2)}, u32[]{:S(2)}) collective-permute-start(f32[160,128]{1,0:T(8,128)S(1)} %get-tuple-element.58), channel_id=1, source_target_pairs={{0,4},{2,6},{4,0},{6,2},{8,12},{10,14},{12,8},{14,10},{16,20},{18,... | collective-permute-start | bytes 245768 | tf_op jit(solution)/shard_map/ppermute | solution.py:265
  60.4 6.3 %collective-permute-start.16 = (f32[160,128]{1,0:T(8,128)S(1)}, f32[160,128]{1,0:T(8,128)S(1)}, u32[]{:S(2)}, u32[]{:S(2)}) collective-permute-start(f32[160,128]{1,0:T(8,128)S(1)} %get-tuple-element.59), channel_id=1, source_target_pairs={{0,2},{2,0},{4,6},{6,4},{8,10},{10,8},{12,14},{14,12},{16,18},{18,... | collective-permute-start | bytes 245768 | tf_op jit(solution)/shard_map/ppermute | solution.py:265
  66.7 4.5 %collective-permute-start.17 = (f32[160,128]{1,0:T(8,128)S(1)}, f32[160,128]{1,0:T(8,128)S(1)}, u32[]{:S(2)}, u32[]{:S(2)}) collective-permute-start(f32[160,128]{1,0:T(8,128)S(1)} %shard_map.53), channel_id=1, source_target_pairs={{0,8},{2,10},{4,12},{6,14},{8,0},{10,2},{12,4},{14,6},{16,24},{18,... | collective-permute-start | bytes 245768 | tf_op jit(solution)/shard_map/ppermute | solution.py:265
  66.7 8.4 %collective-permute-start.18 = (f32[160,128]{1,0:T(8,128)S(1)}, f32[160,128]{1,0:T(8,128)S(1)}, u32[]{:S(2)}, u32[]{:S(2)}) collective-permute-start(f32[160,128]{1,0:T(8,128)S(1)} %shard_map.53), channel_id=1, source_target_pairs={{0,16},{2,18},{4,20},{6,22},{8,24},{10,26},{12,28},{14,30},{16,0},... | collective-permute-start | bytes 245768 | tf_op jit(solution)/shard_map/ppermute | solution.py:265
  68.1 7.1 %collective-permute-start.19 = (f32[160,128]{1,0:T(8,128)S(1)}, f32[160,128]{1,0:T(8,128)S(1)}, u32[]{:S(2)}, u32[]{:S(2)}) collective-permute-start(f32[160,128]{1,0:T(8,128)S(1)} %shard_map.53), channel_id=1, source_target_pairs={{0,24},{2,26},{4,28},{6,30},{8,16},{10,18},{12,20},{14,22},{16,8},... | collective-permute-start | bytes 245768 | tf_op jit(solution)/shard_map/ppermute | solution.py:265
  75.2 5.4 %collective-permute-start.20 = (f32[160,128]{1,0:T(8,128)S(1)}, f32[160,128]{1,0:T(8,128)S(1)}, u32[]{:S(2)}, u32[]{:S(2)}) collective-permute-start(f32[160,128]{1,0:T(8,128)S(1)} %get-tuple-element.62), channel_id=1, source_target_pairs={{0,6},{2,4},{4,2},{6,0},{8,14},{10,12},{12,10},{14,8},{16,22},{18,... | collective-permute-start | bytes 245768 | tf_op jit(solution)/shard_map/ppermute | solution.py:265
  77.0 4.5 %collective-permute-start.21 = (f32[160,128]{1,0:T(8,128)S(1)}, f32[160,128]{1,0:T(8,128)S(1)}, u32[]{:S(2)}, u32[]{:S(2)}) collective-permute-start(f32[160,128]{1,0:T(8,128)S(1)} %get-tuple-element.62), channel_id=1, source_target_pairs={{0,4},{2,6},{4,0},{6,2},{8,12},{10,14},{12,8},{14,10},{16,20},{18,... | collective-permute-start | bytes 245768 | tf_op jit(solution)/shard_map/ppermute | solution.py:265
  78.1 4.4 %collective-permute-start.22 = (f32[160,128]{1,0:T(8,128)S(1)}, f32[160,128]{1,0:T(8,128)S(1)}, u32[]{:S(2)}, u32[]{:S(2)}) collective-permute-start(f32[160,128]{1,0:T(8,128)S(1)} %get-tuple-element.62), channel_id=1, source_target_pairs={{0,2},{2,0},{4,6},{6,4},{8,10},{10,8},{12,14},{14,12},{16,18},{18,... | collective-permute-start | bytes 245768 | tf_op jit(solution)/shard_map/ppermute | solution.py:265
  82.5 1.7 %collective-permute-start.23 = (f32[640,128]{1,0:T(8,128)S(1)}, f32[640,128]{1,0:T(8,128)S(1)}, u32[]{:S(2)}, u32[]{:S(2)}) collective-permute-start(f32[640,128]{1,0:T(8,128)S(1)} %bitcast.22), channel_id=1, source_target_pairs={{0,1},{1,0},{2,3},{3,2},{4,5},{5,4},{6,7},{7,6},{8,9},{9,8},{10,11... | collective-permute-start | bytes 983048 | tf_op jit(solution)/shard_map/ppermute | solution.py:265
  (7 other events, 42.0 us)

commit v8 on v7

--- a/solution.py
+++ b/solution.py
@@ -311,7 +311,7 @@
     for stage, after in zip(stages[:-1], stages[1:]):
         axis, stride, _ = stage
         terms = [parts[0]] + [
-            swap(parts[d], axis, d * stride) for d in reversed(range(1, len(parts)))
+            swap(parts[d], axis, d * stride) for d in range(1, len(parts))
         ]
         rows, radix = terms[0].shape[0], after[2]
         if after == stages[-1]:

time: 101 us -> 100 us (0.990)
  transfers between devices with their start and end apart: 24 -> 24, of which waited for: 19 -> 20; matrix products, arithmetic and copies ran while one was open for 0% -> 0% of each run, Pallas kernels for 3% -> 3%
where the time goes in v8:
time: 100 us
  waiting for transfers between devices  38.2 us (38%)
  starting transfers between devices  37 us (37%)
  Pallas kernels  22.3 us (22%)
  local copies, waits for them, and re-layouts  2.22 us (2%)
    ppermute x13, waiting for transfers between devices, to_next(): lax.ppermute(block, axis, [(i, (i + distance) % count) for i in range(cou...  25.9 us
    ppermute x13, starting transfers between devices, to_next(): lax.ppermute(block, axis, [(i, (i + distance) % count) for i in range(cou...  25.4 us
    pallas_call x18, Pallas kernels, call(): pl.pallas_call(body, out_shape=outs, in_specs=[pl.BlockSpec(memory_space=...  22.3 us
    ppermute x11, waiting for transfers between devices, swap(): return lax.ppermute(block, axis, [(i, i ^ distance) for i in range(count)])  12.4 us
    ppermute x11, starting transfers between devices, swap(): return lax.ppermute(block, axis, [(i, i ^ distance) for i in range(count)])  11.6 us
  transfers between devices with their start and end apart: 24, of which 20 were waited for; matrix products, arithmetic and copies ran while one was open for 0% of the time, Pallas kernels for 3%

profile of v8, /device:TPU:0, one launch (start us, length us, event | category | flops | bytes accessed | tf_op | source)
XLA Modules:
  0.0 100.3 jit_solution(11077300510215077077)
XLA Ops:
  0.9 7.0 %collective-permute-start = (f32[1,7,7,512]{3,2,1,0:T(8,128)S(1)}, f32[1,7,7,512]{3,2,1,0:T(8,128)S(1)}, u32[]{:S(2)}, u32[]{:S(2)}) collective-permute-start(f32[1,7,7,512]{3,2,1,0:T(8,128)S(1)} %slice.9), channel_id=1, source_target_pairs={{0,30},{2,0},{4,2},{6,4},{8,6},{10,8},{12,10},{14,12},{16,14},{18,... | collective-permute-start | bytes 301064 | tf_op jit(solution)/shard_map/ppermute | solution.py:550
  7.9 2.4 %collective-permute-done.x_next = f32[1,7,7,512]{3,2,1,0:T(8,128)S(1)} collective-permute-done((f32[1,7,7,512]{3,2,1,0:T(8,128)S(1)}, f32[1,7,7,512]{3,2,1,0:T(8,128)S(1)}, u32[]{:S(2)}, u32[]{:S(2)}) %collective-permute-start) | collective-permute-done | bytes 100384 | tf_op jit(solution)/shard_map/ppermute | solution.py:550
  14.1 6.1 %collective-permute-start.4 = (f32[56,512]{1,0:T(8,128)S(1)}, f32[56,512]{1,0:T(8,128)S(1)}, u32[]{:S(2)}, u32[]{:S(2)}) collective-permute-start(f32[56,512]{1,0:T(8,128)S(1)} %shard_map.39.refs_0_), channel_id=1, source_target_pairs={{0,30},{2,0},{4,2},{6,4},{8,6},{10,8},{12,10},{14,12},{16,14},{18,... | collective-permute-start | bytes 344072 | tf_op jit(solution)/shard_map/ppermute | solution.py:550
  20.3 3.6 %collective-permute-done.3.refs_2_ = f32[56,512]{1,0:T(8,128)S(1)} collective-permute-done((f32[56,512]{1,0:T(8,128)S(1)}, f32[56,512]{1,0:T(8,128)S(1)}, u32[]{:S(2)}, u32[]{:S(2)}) %collective-permute-start.3) | collective-permute-done | bytes 114720 | tf_op jit(solution)/shard_map/ppermute | solution.py:550
  24.5 1.5 %collective-permute-done.5.y_faces.refs_1_ = f32[2,8,8,512]{3,2,1,0:T(8,128)S(1)} collective-permute-done((f32[2,8,8,512]{3,2,1,0:T(8,128)S(1)}, f32[2,8,8,512]{3,2,1,0:T(8,128)S(1)}, u32[]{:S(2)}, u32[]{:S(2)}) %collective-permute-start.5) | collective-permute-done | bytes 262176 | tf_op jit(solution)/shard_map/ppermute | solution.py:550
  26.2 5.6 %collective-permute-start.7 = (f32[56,512]{1,0:T(8,128)S(1)}, f32[56,512]{1,0:T(8,128)S(1)}, u32[]{:S(2)}, u32[]{:S(2)}) collective-permute-start(f32[56,512]{1,0:T(8,128)S(1)} %shard_map.42.refs_0_), channel_id=1, source_target_pairs={{0,30},{2,0},{4,2},{6,4},{8,6},{10,8},{12,10},{14,12},{16,14},{18,... | collective-permute-start | bytes 344072 | tf_op jit(solution)/shard_map/ppermute | solution.py:550
  31.8 3.2 %collective-permute-done.6.refs_2_ = f32[56,512]{1,0:T(8,128)S(1)} collective-permute-done((f32[56,512]{1,0:T(8,128)S(1)}, f32[56,512]{1,0:T(8,128)S(1)}, u32[]{:S(2)}, u32[]{:S(2)}) %collective-permute-start.6) | collective-permute-done | bytes 114720 | tf_op jit(solution)/shard_map/ppermute | solution.py:550
  35.7 1.5 %collective-permute-done.8.y_faces.refs_1_ = f32[2,8,8,512]{3,2,1,0:T(8,128)S(1)} collective-permute-done((f32[2,8,8,512]{3,2,1,0:T(8,128)S(1)}, f32[2,8,8,512]{3,2,1,0:T(8,128)S(1)}, u32[]{:S(2)}, u32[]{:S(2)}) %collective-permute-start.8) | collective-permute-done | bytes 262176 | tf_op jit(solution)/shard_map/ppermute | solution.py:550
  37.4 5.6 %collective-permute-start.10 = (f32[56,512]{1,0:T(8,128)S(1)}, f32[56,512]{1,0:T(8,128)S(1)}, u32[]{:S(2)}, u32[]{:S(2)}) collective-permute-start(f32[56,512]{1,0:T(8,128)S(1)} %shard_map.45.refs_0_), channel_id=1, source_target_pairs={{0,30},{2,0},{4,2},{6,4},{8,6},{10,8},{12,10},{14,12},{16,14},{18,... | collective-permute-start | bytes 344072 | tf_op jit(solution)/shard_map/ppermute | solution.py:550
  43.0 3.2 %collective-permute-done.9.refs_2_ = f32[56,512]{1,0:T(8,128)S(1)} collective-permute-done((f32[56,512]{1,0:T(8,128)S(1)}, f32[56,512]{1,0:T(8,128)S(1)}, u32[]{:S(2)}, u32[]{:S(2)}) %collective-permute-start.9) | collective-permute-done | bytes 114720 | tf_op jit(solution)/shard_map/ppermute | solution.py:550
  46.9 1.3 %collective-permute-done.11.y_faces.y_face = f32[1,8,8,512]{3,2,1,0:T(8,128)S(1)} collective-permute-done((f32[1,8,8,512]{3,2,1,0:T(8,128)S(1)}, f32[1,8,8,512]{3,2,1,0:T(8,128)S(1)}, u32[]{:S(2)}, u32[]{:S(2)}) %collective-permute-start.11) | collective-permute-done | bytes 131104 | tf_op jit(solution)/shard_map/ppermute | solution.py:550
  48.4 1.2 %shard_map.49 = (f32[336,512]{1,0:T(8,128)}, f32[640,128]{1,0:T(8,128)S(1)}, f32[640,128]{1,0:T(8,128)S(1)}) custom-call(s32[1]{0:T(128)} %bitcast.1.mine, f32[8,8,8,512]{3,2,1,0:T(8,128)S(1)} %get-tuple-element.48.image, f32[1,8,8,512]{3,2,1,0:T(8,128)S(1)} %collective-permute-done.11.y_faces.y_face, f32[8,8,8,512]{3,2,1,0:T(8,128)S(1)} %get-tuple-element.51.current, ...), custom_call_target="tpu_custom_call" | custom-call | flops 805306368 | bytes 1048576 | tf_op jit(solution)/shard_map/pallas_call | solution.py:40
  49.6 7.6 %collective-permute-done.12.x_low = f32[56,512]{1,0:T(8,128)S(1)} collective-permute-done((f32[56,512]{1,0:T(8,128)S(1)}, f32[56,512]{1,0:T(8,128)S(1)}, u32[]{:S(2)}, u32[]{:S(2)}) %collective-permute-start.12) | collective-permute-done | bytes 114720 | tf_op jit(solution)/shard_map/ppermute | solution.py:550
  60.4 3.4 %collective-permute-start.16 = (f32[160,128]{1,0:T(8,128)S(1)}, f32[160,128]{1,0:T(8,128)S(1)}, u32[]{:S(2)}, u32[]{:S(2)}) collective-permute-start(f32[160,128]{1,0:T(8,128)S(1)} %get-tuple-element.59), channel_id=1, source_target_pairs={{0,6},{2,4},{4,2},{6,0},{8,14},{10,12},{12,10},{14,8},{16,22},{18,... | collective-permute-start | bytes 245768 | tf_op jit(solution)/shard_map/ppermute | solution.py:265
  63.8 1.6 %collective-permute-done.14.refs_1_ = f32[160,128]{1,0:T(8,128)S(1)} collective-permute-done((f32[160,128]{1,0:T(8,128)S(1)}, f32[160,128]{1,0:T(8,128)S(1)}, u32[]{:S(2)}, u32[]{:S(2)}) %collective-permute-start.14) | collective-permute-done | bytes 81952 | tf_op jit(solution)/shard_map/ppermute | solution.py:265
  65.4 1.3 %collective-permute-done.15.refs_2_ = f32[160,128]{1,0:T(8,128)S(1)} collective-permute-done((f32[160,128]{1,0:T(8,128)S(1)}, f32[160,128]{1,0:T(8,128)S(1)}, u32[]{:S(2)}, u32[]{:S(2)}) %collective-permute-start.15) | collective-permute-done | bytes 81952 | tf_op jit(solution)/shard_map/ppermute | solution.py:265
  66.7 2.4 %collective-permute-start.18 = (f32[160,128]{1,0:T(8,128)S(1)}, f32[160,128]{1,0:T(8,128)S(1)}, u32[]{:S(2)}, u32[]{:S(2)}) collective-permute-start(f32[160,128]{1,0:T(8,128)S(1)} %shard_map.53), channel_id=1, source_target_pairs={{0,16},{2,18},{4,20},{6,22},{8,24},{10,26},{12,28},{14,30},{16,0},... | collective-permute-start | bytes 245768 | tf_op jit(solution)/shard_map/ppermute | solution.py:265
  69.1 2.0 %collective-permute-start.19 = (f32[160,128]{1,0:T(8,128)S(1)}, f32[160,128]{1,0:T(8,128)S(1)}, u32[]{:S(2)}, u32[]{:S(2)}) collective-permute-start(f32[160,128]{1,0:T(8,128)S(1)} %shard_map.53), channel_id=1, source_target_pairs={{0,24},{2,26},{4,28},{6,30},{8,16},{10,18},{12,20},{14,22},{16,8},... | collective-permute-start | bytes 245768 | tf_op jit(solution)/shard_map/ppermute | solution.py:265
  71.2 2.8 %collective-permute-done.18 = f32[160,128]{1,0:T(8,128)S(1)} collective-permute-done((f32[160,128]{1,0:T(8,128)S(1)}, f32[160,128]{1,0:T(8,128)S(1)}, u32[]{:S(2)}, u32[]{:S(2)}) %collective-permute-start.18) | collective-permute-done | bytes 81952 | tf_op jit(solution)/shard_map/ppermute | solution.py:265
  74.0 1.5 %collective-permute-done.19 = f32[160,128]{1,0:T(8,128)S(1)} collective-permute-done((f32[160,128]{1,0:T(8,128)S(1)}, f32[160,128]{1,0:T(8,128)S(1)}, u32[]{:S(2)}, u32[]{:S(2)}) %collective-permute-start.19) | collective-permute-done | bytes 81952 | tf_op jit(solution)/shard_map/ppermute | solution.py:265
  75.5 2.0 %collective-permute-start.20 = (f32[160,128]{1,0:T(8,128)S(1)}, f32[160,128]{1,0:T(8,128)S(1)}, u32[]{:S(2)}, u32[]{:S(2)}) collective-permute-start(f32[160,128]{1,0:T(8,128)S(1)} %get-tuple-element.62), channel_id=1, source_target_pairs={{0,6},{2,4},{4,2},{6,0},{8,14},{10,12},{12,10},{14,8},{16,22},{18,... | collective-permute-start | bytes 245768 | tf_op jit(solution)/shard_map/ppermute | solution.py:265
  79.1 1.9 %collective-permute-done.20 = f32[160,128]{1,0:T(8,128)S(1)} collective-permute-done((f32[160,128]{1,0:T(8,128)S(1)}, f32[160,128]{1,0:T(8,128)S(1)}, u32[]{:S(2)}, u32[]{:S(2)}) %collective-permute-start.20) | collective-permute-done | bytes 81952 | tf_op jit(solution)/shard_map/ppermute | solution.py:265
  82.6 1.5 %collective-permute-done.23 = f32[640,128]{1,0:T(8,128)S(1)} collective-permute-done((f32[640,128]{1,0:T(8,128)S(1)}, f32[640,128]{1,0:T(8,128)S(1)}, u32[]{:S(2)}, u32[]{:S(2)}) %collective-permute-start.23) | collective-permute-done | bytes 327712 | tf_op jit(solution)/shard_map/ppermute | solution.py:265
  84.1 16.0 %shard_map.54 = f32[49,7,512]{2,1,0:T(8,128)} custom-call(f32[1280,128]{1,0:T(8,128)S(1)} %bitcast.20, f32[56,512]{1,0:T(8,128)S(1)} %get-tuple-element.53.own.first, f32[336,512]{1,0:T(8,128)S(1)} %copy-done.1), custom_call_target="tpu_custom_call" | custom-call | flops 134217728 | bytes 1048576 | tf_op jit(solution)/shard_map/pallas_call | solution.py:40
  (68 shorter events, 13.5 us)
Async XLA Ops:
  0.9 9.4 %collective-permute-start = (f32[1,7,7,512]{3,2,1,0:T(8,128)S(1)}, f32[1,7,7,512]{3,2,1,0:T(8,128)S(1)}, u32[]{:S(2)}, u32[]{:S(2)}) collective-permute-start(f32[1,7,7,512]{3,2,1,0:T(8,128)S(1)} %slice.9), channel_id=1, source_target_pairs={{0,30},{2,0},{4,2},{6,4},{8,6},{10,8},{12,10},{14,12},{16,14},{18,... | collective-permute-start | bytes 301064 | tf_op jit(solution)/shard_map/ppermute | solution.py:550
  10.4 1.4 %collective-permute-start.1 = (f32[8,1,7,512]{3,2,1,0:T(8,128)S(1)}, f32[8,1,7,512]{3,2,1,0:T(8,128)S(1)}, u32[]{:S(2)}, u32[]{:S(2)}) collective-permute-start(f32[8,1,7,512]{3,2,1,0:T(8,128)S(1)} %pad_maximum_fusion), channel_id=1, source_target_pairs={{0,1},{1,0},{2,3},{3,2},{4,5},{5,4},{6,7},{7,6},{8,9},{9,8},{10,11... | collective-permute-start | bytes 344072 | tf_op jit(solution)/shard_map/ppermute | solution.py:550
  12.3 1.7 %collective-permute-start.2 = (f32[2,8,8,512]{3,2,1,0:T(8,128)S(1)}, f32[2,8,8,512]{3,2,1,0:T(8,128)S(1)}, u32[]{:S(2)}, u32[]{:S(2)}) collective-permute-start(f32[2,8,8,512]{3,2,1,0:T(8,128)S(1)} %get-tuple-element.34), channel_id=1, source_target_pairs={{0,1},{1,0},{2,3},{3,2},{4,5},{5,4},{6,7},{7,6},{8,9},{9,8},{10,11... | collective-permute-start | bytes 786440 | tf_op jit(solution)/shard_map/ppermute | solution.py:550
  14.1 9.8 %collective-permute-start.3 = (f32[56,512]{1,0:T(8,128)S(1)}, f32[56,512]{1,0:T(8,128)S(1)}, u32[]{:S(2)}, u32[]{:S(2)}) collective-permute-start(f32[56,512]{1,0:T(8,128)S(1)} %shard_map.40), channel_id=1, source_target_pairs={{0,2},{2,4},{4,6},{6,8},{8,10},{10,12},{12,14},{14,16},{16,18},{18... | collective-permute-start | bytes 344072 | tf_op jit(solution)/shard_map/ppermute | solution.py:550
  14.1 9.8 %collective-permute-start.4 = (f32[56,512]{1,0:T(8,128)S(1)}, f32[56,512]{1,0:T(8,128)S(1)}, u32[]{:S(2)}, u32[]{:S(2)}) collective-permute-start(f32[56,512]{1,0:T(8,128)S(1)} %shard_map.39.refs_0_), channel_id=1, source_target_pairs={{0,30},{2,0},{4,2},{6,4},{8,6},{10,8},{12,10},{14,12},{16,14},{18,... | collective-permute-start | bytes 344072 | tf_op jit(solution)/shard_map/ppermute | solution.py:550
  24.5 1.6 %collective-permute-start.5 = (f32[2,8,8,512]{3,2,1,0:T(8,128)S(1)}, f32[2,8,8,512]{3,2,1,0:T(8,128)S(1)}, u32[]{:S(2)}, u32[]{:S(2)}) collective-permute-start(f32[2,8,8,512]{3,2,1,0:T(8,128)S(1)} %get-tuple-element.39), channel_id=1, source_target_pairs={{0,1},{1,0},{2,3},{3,2},{4,5},{5,4},{6,7},{7,6},{8,9},{9,8},{10,11... | collective-permute-start | bytes 786440 | tf_op jit(solution)/shard_map/ppermute | solution.py:550
  26.1 8.9 %collective-permute-start.6 = (f32[56,512]{1,0:T(8,128)S(1)}, f32[56,512]{1,0:T(8,128)S(1)}, u32[]{:S(2)}, u32[]{:S(2)}) collective-permute-start(f32[56,512]{1,0:T(8,128)S(1)} %shard_map.43), channel_id=1, source_target_pairs={{0,2},{2,4},{4,6},{6,8},{8,10},{10,12},{12,14},{14,16},{16,18},{18... | collective-permute-start | bytes 344072 | tf_op jit(solution)/shard_map/ppermute | solution.py:550
  26.2 8.8 %collective-permute-start.7 = (f32[56,512]{1,0:T(8,128)S(1)}, f32[56,512]{1,0:T(8,128)S(1)}, u32[]{:S(2)}, u32[]{:S(2)}) collective-permute-start(f32[56,512]{1,0:T(8,128)S(1)} %shard_map.42.refs_0_), channel_id=1, source_target_pairs={{0,30},{2,0},{4,2},{6,4},{8,6},{10,8},{12,10},{14,12},{16,14},{18,... | collective-permute-start | bytes 344072 | tf_op jit(solution)/shard_map/ppermute | solution.py:550
  35.6 1.6 %collective-permute-start.8 = (f32[2,8,8,512]{3,2,1,0:T(8,128)S(1)}, f32[2,8,8,512]{3,2,1,0:T(8,128)S(1)}, u32[]{:S(2)}, u32[]{:S(2)}) collective-permute-start(f32[2,8,8,512]{3,2,1,0:T(8,128)S(1)} %get-tuple-element.44), channel_id=1, source_target_pairs={{0,1},{1,0},{2,3},{3,2},{4,5},{5,4},{6,7},{7,6},{8,9},{9,8},{10,11... | collective-permute-start | bytes 786440 | tf_op jit(solution)/shard_map/ppermute | solution.py:550
  37.3 8.9 %collective-permute-start.9 = (f32[56,512]{1,0:T(8,128)S(1)}, f32[56,512]{1,0:T(8,128)S(1)}, u32[]{:S(2)}, u32[]{:S(2)}) collective-permute-start(f32[56,512]{1,0:T(8,128)S(1)} %shard_map.46), channel_id=1, source_target_pairs={{0,2},{2,4},{4,6},{6,8},{8,10},{10,12},{12,14},{14,16},{16,18},{18... | collective-permute-start | bytes 344072 | tf_op jit(solution)/shard_map/ppermute | solution.py:550
  37.4 8.8 %collective-permute-start.10 = (f32[56,512]{1,0:T(8,128)S(1)}, f32[56,512]{1,0:T(8,128)S(1)}, u32[]{:S(2)}, u32[]{:S(2)}) collective-permute-start(f32[56,512]{1,0:T(8,128)S(1)} %shard_map.45.refs_0_), channel_id=1, source_target_pairs={{0,30},{2,0},{4,2},{6,4},{8,6},{10,8},{12,10},{14,12},{16,14},{18,... | collective-permute-start | bytes 344072 | tf_op jit(solution)/shard_map/ppermute | solution.py:550
  46.9 1.4 %collective-permute-start.11 = (f32[1,8,8,512]{3,2,1,0:T(8,128)S(1)}, f32[1,8,8,512]{3,2,1,0:T(8,128)S(1)}, u32[]{:S(2)}, u32[]{:S(2)}) collective-permute-start(f32[1,8,8,512]{3,2,1,0:T(8,128)S(1)} %get-tuple-element.49), channel_id=1, source_target_pairs={{0,1},{1,0},{2,3},{3,2},{4,5},{5,4},{6,7},{7,6},{8,9},{9,8},{10,11... | collective-permute-start | bytes 393224 | tf_op jit(solution)/shard_map/ppermute | solution.py:550
  48.3 8.9 %collective-permute-start.12 = (f32[56,512]{1,0:T(8,128)S(1)}, f32[56,512]{1,0:T(8,128)S(1)}, u32[]{:S(2)}, u32[]{:S(2)}) collective-permute-start(f32[56,512]{1,0:T(8,128)S(1)} %shard_map.48), channel_id=1, source_target_pairs={{0,2},{2,4},{4,6},{6,8},{8,10},{10,12},{12,14},{14,16},{16,18},{18... | collective-permute-start | bytes 344072 | tf_op jit(solution)/shard_map/ppermute | solution.py:550
  58.3 1.8 %collective-permute-start.13 = (f32[640,128]{1,0:T(8,128)}, f32[640,128]{1,0:T(8,128)S(1)}, u32[]{:S(2)}, u32[]{:S(2)}) collective-permute-start(f32[640,128]{1,0:T(8,128)} %get-tuple-element.55), channel_id=1, source_target_pairs={{0,1},{1,0},{2,3},{3,2},{4,5},{5,4},{6,7},{7,6},{8,9},{9,8},{10,11... | collective-permute-start | bytes 983048 | tf_op jit(solution)/shard_map/ppermute | solution.py:265
  60.2 5.1 %collective-permute-start.14 = (f32[160,128]{1,0:T(8,128)S(1)}, f32[160,128]{1,0:T(8,128)S(1)}, u32[]{:S(2)}, u32[]{:S(2)}) collective-permute-start(f32[160,128]{1,0:T(8,128)S(1)} %get-tuple-element.57), channel_id=1, source_target_pairs={{0,2},{2,0},{4,6},{6,4},{8,10},{10,8},{12,14},{14,12},{16,18},{18,... | collective-permute-start | bytes 245768 | tf_op jit(solution)/shard_map/ppermute | solution.py:265
  60.3 6.3 %collective-permute-start.15 = (f32[160,128]{1,0:T(8,128)S(1)}, f32[160,128]{1,0:T(8,128)S(1)}, u32[]{:S(2)}, u32[]{:S(2)}) collective-permute-start(f32[160,128]{1,0:T(8,128)S(1)} %get-tuple-element.58), channel_id=1, source_target_pairs={{0,4},{2,6},{4,0},{6,2},{8,12},{10,14},{12,8},{14,10},{16,20},{18,... | collective-permute-start | bytes 245768 | tf_op jit(solution)/shard_map/ppermute | solution.py:265
  60.4 6.3 %collective-permute-start.16 = (f32[160,128]{1,0:T(8,128)S(1)}, f32[160,128]{1,0:T(8,128)S(1)}, u32[]{:S(2)}, u32[]{:S(2)}) collective-permute-start(f32[160,128]{1,0:T(8,128)S(1)} %get-tuple-element.59), channel_id=1, source_target_pairs={{0,6},{2,4},{4,2},{6,0},{8,14},{10,12},{12,10},{14,8},{16,22},{18,... | collective-permute-start | bytes 245768 | tf_op jit(solution)/shard_map/ppermute | solution.py:265
  66.7 4.5 %collective-permute-start.17 = (f32[160,128]{1,0:T(8,128)S(1)}, f32[160,128]{1,0:T(8,128)S(1)}, u32[]{:S(2)}, u32[]{:S(2)}) collective-permute-start(f32[160,128]{1,0:T(8,128)S(1)} %shard_map.53), channel_id=1, source_target_pairs={{0,8},{2,10},{4,12},{6,14},{8,0},{10,2},{12,4},{14,6},{16,24},{18,... | collective-permute-start | bytes 245768 | tf_op jit(solution)/shard_map/ppermute | solution.py:265
  66.7 7.2 %collective-permute-start.18 = (f32[160,128]{1,0:T(8,128)S(1)}, f32[160,128]{1,0:T(8,128)S(1)}, u32[]{:S(2)}, u32[]{:S(2)}) collective-permute-start(f32[160,128]{1,0:T(8,128)S(1)} %shard_map.53), channel_id=1, source_target_pairs={{0,16},{2,18},{4,20},{6,22},{8,24},{10,26},{12,28},{14,30},{16,0},... | collective-permute-start | bytes 245768 | tf_op jit(solution)/shard_map/ppermute | solution.py:265
  69.1 6.3 %collective-permute-start.19 = (f32[160,128]{1,0:T(8,128)S(1)}, f32[160,128]{1,0:T(8,128)S(1)}, u32[]{:S(2)}, u32[]{:S(2)}) collective-permute-start(f32[160,128]{1,0:T(8,128)S(1)} %shard_map.53), channel_id=1, source_target_pairs={{0,24},{2,26},{4,28},{6,30},{8,16},{10,18},{12,20},{14,22},{16,8},... | collective-permute-start | bytes 245768 | tf_op jit(solution)/shard_map/ppermute | solution.py:265
  75.5 5.4 %collective-permute-start.20 = (f32[160,128]{1,0:T(8,128)S(1)}, f32[160,128]{1,0:T(8,128)S(1)}, u32[]{:S(2)}, u32[]{:S(2)}) collective-permute-start(f32[160,128]{1,0:T(8,128)S(1)} %get-tuple-element.62), channel_id=1, source_target_pairs={{0,6},{2,4},{4,2},{6,0},{8,14},{10,12},{12,10},{14,8},{16,22},{18,... | collective-permute-start | bytes 245768 | tf_op jit(solution)/shard_map/ppermute | solution.py:265
  77.5 4.4 %collective-permute-start.21 = (f32[160,128]{1,0:T(8,128)S(1)}, f32[160,128]{1,0:T(8,128)S(1)}, u32[]{:S(2)}, u32[]{:S(2)}) collective-permute-start(f32[160,128]{1,0:T(8,128)S(1)} %get-tuple-element.62), channel_id=1, source_target_pairs={{0,4},{2,6},{4,0},{6,2},{8,12},{10,14},{12,8},{14,10},{16,20},{18,... | collective-permute-start | bytes 245768 | tf_op jit(solution)/shard_map/ppermute | solution.py:265
  78.0 4.4 %collective-permute-start.22 = (f32[160,128]{1,0:T(8,128)S(1)}, f32[160,128]{1,0:T(8,128)S(1)}, u32[]{:S(2)}, u32[]{:S(2)}) collective-permute-start(f32[160,128]{1,0:T(8,128)S(1)} %get-tuple-element.62), channel_id=1, source_target_pairs={{0,2},{2,0},{4,6},{6,4},{8,10},{10,8},{12,14},{14,12},{16,18},{18,... | collective-permute-start | bytes 245768 | tf_op jit(solution)/shard_map/ppermute | solution.py:265
  82.4 1.7 %collective-permute-start.23 = (f32[640,128]{1,0:T(8,128)S(1)}, f32[640,128]{1,0:T(8,128)S(1)}, u32[]{:S(2)}, u32[]{:S(2)}) collective-permute-start(f32[640,128]{1,0:T(8,128)S(1)} %bitcast.22), channel_id=1, source_target_pairs={{0,1},{1,0},{2,3},{3,2},{4,5},{5,4},{6,7},{7,6},{8,9},{9,8},{10,11... | collective-permute-start | bytes 983048 | tf_op jit(solution)/shard_map/ppermute | solution.py:265
  (7 other events, 42.0 us)
